TPU v7x, 256 devices: a whole 4x4x8 slice. The times are simulated.
256 devices in a mesh: row: 32 (over z, x_hi, core), col: 8 (over x_lo, y).
Axes of the slice: x: 4 (x_hi: 2, x_lo: 2; x = x_hi * 2 + x_lo), y: 4, z: 8, core: 2. Of those that a mesh axis runs over, the one named last changes fastest.
Arguments:
- tokens: bfloat16 [512, 16384], P('row', 'col'), may hold values from -6 to 6
- gate_up: bfloat16 [16384, 2, 28672], P('col', None, 'row'), may hold values from -0.046875 to 0.046875
- down_weight: bfloat16 [28672, 16384], P('row', 'col'), may hold values from -0.03125 to 0.03125
- out_grad: bfloat16 [512, 16384], P('row', 'col'), may hold values from -6 to 6
Outputs:
- block_out: bfloat16 [512, 16384], P('row', 'col')
- grad_tokens: bfloat16 [512, 16384], P('row', 'col')
All inputs are finite; a program needn't handle non-finite values.
Results may differ from a plain program's by a relative error of at most 0.0049.
Values may be sent and summed in bfloat16 or wider, within the bound.
No kernel may reach another device: no remote copies, remote signals or barrier semaphores. Data moves between devices by JAX's collectives and lax.ppermute only.
A program may use at most 128 MiB of HBM per device.

v0:
```python
import jax
import jax.numpy as jnp
from jax import lax
from jax.experimental import pallas as pl
from jax.experimental.pallas import tpu as pltpu
from jax.sharding import Mesh, PartitionSpec as P

BF = jnp.bfloat16
F16 = jnp.float16
F32 = jnp.float32
ROW, COL = ("z", "xh", "core"), ("xl", "y")
LAST = (((1,), (1,)), ((), ()))
SWAP = [(0, 1), (1, 0)]
NZ = 8
SCALE = 64.0


def product(xs, w, turned, types, width):
    depth = xs[0].shape[1]
    n = w.shape[0] if turned else w.shape[1]
    dims = (((1,), (1 if turned else 0,)), ((), ()))

    def body(*refs):
        w_ref = refs[len(xs)]
        for x_ref, o_ref in zip(refs, refs[len(xs) + 1 :]):
            o_ref[...] = lax.dot_general(
                x_ref[...], w_ref[...], dims, preferred_element_type=F32
            ).astype(o_ref.dtype)

    if turned:
        w_spec = pl.BlockSpec((width, depth), lambda i: (i, 0))
    else:
        w_spec = pl.BlockSpec((depth, width), lambda i: (0, i))
    rows = sum(x.shape[0] for x in xs)
    return pl.pallas_call(
        body,
        grid=(n // width,),
        in_specs=[pl.BlockSpec(x.shape, lambda i: (0, 0)) for x in xs] + [w_spec],
        out_specs=[pl.BlockSpec((x.shape[0], width), lambda i: (0, i)) for x in xs],
        out_shape=[jax.ShapeDtypeStruct((x.shape[0], n), t) for x, t in zip(xs, types)],
        compiler_params=pltpu.CompilerParams(vmem_limit_bytes=40 << 20),
        cost_estimate=pl.CostEstimate(
            flops=2 * rows * depth * n,
            bytes_accessed=2 * (w.size + rows * depth + rows * n),
            transcendentals=0,
        ),
    )(*xs, w)


def swap(x, axis):
    return lax.ppermute(x, axis, SWAP)


def shift(x, by):
    return lax.ppermute(x, "z", [(i, (i - by) % NZ) for i in range(NZ)])


def gather_z(pair):
    half = pair.shape[0] // 2
    got = {0: pair}
    for step in (1, 2, 3):
        got[step] = shift(got[step - 1], 1)
        got[-step] = shift(got[1 - step], -1)
    got[4] = jnp.concatenate([shift(got[3][:half], 1), shift(got[-3][half:], -1)])
    return jnp.concatenate([got[r] if r <= 4 else got[r - NZ] for r in range(NZ)])


def scatter_rows(mine, held=None):
    block = mine.reshape(NZ, mine.shape[0] // NZ, -1)
    rows = block.shape[1] // 2
    total = block[0]
    seconds = []
    for way in (1, -1):
        far = block[4][:rows] if way == 1 else block[4][rows:]
        near = jnp.concatenate([block[way % NZ], block[3 * way % NZ]]).astype(BF)
        near = shift(near, -way).astype(F32)
        far = shift(far.astype(BF), -2 * way).astype(F32)
        total = total + near[: 2 * rows]
        zero = jnp.zeros_like(far)
        relayed = jnp.concatenate([far, zero] if way == 1 else [zero, far])
        second = block[2 * way % NZ] + near[2 * rows :] + relayed
        seconds.append(shift(second.astype(BF), -2 * way))
    seconds, held = lax.optimization_barrier((seconds, held))
    total = total + seconds[0].astype(F32) + seconds[1].astype(F32)
    return (total[:rows] + swap(total[rows:].astype(BF), "xh").astype(F32)).astype(BF), held


def exchange(x):
    return lax.all_to_all(x, COL, 0, 0, tiled=True)


def copies(x):
    return jnp.broadcast_to(x[None], (8,) + x.shape)


def per_device(tokens, gate_up, down_weight, out_grad):
    width = gate_up.shape[2]
    n = tokens.shape[0]
    weights = gate_up.reshape(gate_up.shape[0], 2 * width)

    other = swap(jnp.concatenate([tokens, out_grad]), "xh")
    tok = gather_z(jnp.concatenate([tokens, other[:n]]))
    grad = gather_z(jnp.concatenate([out_grad, other[n:]]))
    half = tok.shape[0]
    chunk = half // 4

    tok = jnp.concatenate([tok, swap(tok, "core")])
    parts = (jnp.dot(tok, weights, preferred_element_type=F32) * SCALE).astype(F16)
    both = exchange(parts.reshape(8, chunk, -1))
    part = jnp.concatenate(
        product([grad, swap(grad, "core")], down_weight, True, (BF, BF), 128)
    ).reshape(8, chunk, width)

    both = both.astype(F32).sum(0) * (1.0 / SCALE)
    gate, up = both[:, :width], both[:, width:]
    squash = jax.nn.sigmoid(gate)
    hidden = (gate * squash * up).astype(BF)
    here = exchange(jnp.concatenate([copies(hidden), part], axis=1))
    hid_grad = here[:, chunk:].astype(F32).sum(0)

    gate_grad = (hid_grad * up * squash * (1.0 + gate * (1.0 - squash))).astype(BF)
    up_grad = (hid_grad * gate * squash).astype(BF)
    send = copies(jnp.concatenate([gate_grad, up_grad], axis=1))
    hidden = [here[i : i + 4, :chunk].reshape(half, width) for i in (0, 4)]
    send, hidden = lax.optimization_barrier((send, hidden))
    grads = exchange(send).reshape(2 * half, 2 * width)

    kept, sent = product(hidden, down_weight, False, (F32, BF), 512)
    block_out, grads = scatter_rows(kept + swap(sent, "core").astype(F32), grads)
    out, sent = product([grads[:half], grads[half:]], weights, True, (F32, BF), 256)
    out = out + swap(sent, "core").astype(F32)
    grad_tokens, _ = scatter_rows(out)
    return block_out, grad_tokens


def solution(mesh):
    fine = Mesh(mesh.devices.reshape(8, 2, 2, 2, 4), ("z", "xh", "core", "xl", "y"))
    return jax.shard_map(
        per_device,
        mesh=fine,
        in_specs=(P(ROW, COL), P(COL, None, ROW), P(ROW, COL), P(ROW, COL)),
        out_specs=(P(ROW, COL), P(ROW, COL)),
        check_vma=False,
    )
```

profile of v0, /device:TPU:6, one launch (start us, length us, event | category | flops | bytes accessed | tf_op | source)
XLA Modules:
  0.0 197.3 jit_solution(5431054053601378204)
XLA Ops:
  4.7 3.6 %collective-permute-done = bf16[32,2048]{1,0:T(8,128)(2,1)S(1)} collective-permute-done((bf16[32,2048]{1,0:T(8,128)(2,1)S(1)}, bf16[32,2048]{1,0:T(8,128)(2,1)S(1)}, u32[]{:S(2)}, u32[]{:S(2)}) %collective-permute-start) | collective-permute-done | bytes 131104 | tf_op jit(solution)/shard_map/ppermute | solution.py:51
  11.3 4.0 %collective-permute-start.1 = (bf16[32,2048]{1,0:T(8,128)(2,1)S(1)}, bf16[32,2048]{1,0:T(8,128)(2,1)S(1)}, u32[]{:S(2)}, u32[]{:S(2)}) collective-permute-start(bf16[32,2048]{1,0:T(8,128)(2,1)S(1)} %get-tuple-element.79), channel_id=1, source_target_pairs={{0,224},{32,0},{64,32},{96,64},{128,96},{160,128},{192,160},{224,1... | collective-permute-start | bytes 393224 | tf_op jit(solution)/shard_map/ppermute | solution.py:55
  15.3 3.2 %collective-permute-start.10 = (bf16[32,2048]{1,0:T(8,128)(2,1)S(1)}, bf16[32,2048]{1,0:T(8,128)(2,1)S(1)}, u32[]{:S(2)}, u32[]{:S(2)}) collective-permute-start(bf16[32,2048]{1,0:T(8,128)(2,1)S(1)} %get-tuple-element.80), channel_id=1, source_target_pairs={{0,224},{32,0},{64,32},{96,64},{128,96},{160,128},{192,160},{224,1... | collective-permute-start | bytes 393224 | tf_op jit(solution)/shard_map/ppermute | solution.py:55
  18.5 4.6 %copy.6 = bf16[256,8,2,896]{3,1,2,0:T(8,128)(2,1)S(1)} copy(bf16[256,8,2,896]{3,2,1,0:T(2,128)(2,1)} %bitcast.13) | data formatting | bytes 14680064
  23.2 3.2 %collective-permute-start.2 = (bf16[32,2048]{1,0:T(8,128)(2,1)S(1)}, bf16[32,2048]{1,0:T(8,128)(2,1)S(1)}, u32[]{:S(2)}, u32[]{:S(2)}) collective-permute-start(bf16[32,2048]{1,0:T(8,128)(2,1)S(1)} %collective-permute-done.1), channel_id=1, source_target_pairs={{0,224},{32,0},{64,32},{96,64},{128,96},{160,128},{192,160},{224,1... | collective-permute-start | bytes 393224 | tf_op jit(solution)/shard_map/ppermute | solution.py:55
  26.5 3.2 %collective-permute-start.11 = (bf16[32,2048]{1,0:T(8,128)(2,1)S(1)}, bf16[32,2048]{1,0:T(8,128)(2,1)S(1)}, u32[]{:S(2)}, u32[]{:S(2)}) collective-permute-start(bf16[32,2048]{1,0:T(8,128)(2,1)S(1)} %collective-permute-done.10), channel_id=1, source_target_pairs={{0,224},{32,0},{64,32},{96,64},{128,96},{160,128},{192,160},{224,1... | collective-permute-start | bytes 393224 | tf_op jit(solution)/shard_map/ppermute | solution.py:55
  30.6 3.2 %collective-permute-start.3 = (bf16[32,2048]{1,0:T(8,128)(2,1)S(1)}, bf16[32,2048]{1,0:T(8,128)(2,1)S(1)}, u32[]{:S(2)}, u32[]{:S(2)}) collective-permute-start(bf16[32,2048]{1,0:T(8,128)(2,1)S(1)} %collective-permute-done.2), channel_id=1, source_target_pairs={{0,224},{32,0},{64,32},{96,64},{128,96},{160,128},{192,160},{224,1... | collective-permute-start | bytes 393224 | tf_op jit(solution)/shard_map/ppermute | solution.py:55
  33.9 3.2 %collective-permute-start.12 = (bf16[32,2048]{1,0:T(8,128)(2,1)S(1)}, bf16[32,2048]{1,0:T(8,128)(2,1)S(1)}, u32[]{:S(2)}, u32[]{:S(2)}) collective-permute-start(bf16[32,2048]{1,0:T(8,128)(2,1)S(1)} %collective-permute-done.11), channel_id=1, source_target_pairs={{0,224},{32,0},{64,32},{96,64},{128,96},{160,128},{192,160},{224,1... | collective-permute-start | bytes 393224 | tf_op jit(solution)/shard_map/ppermute | solution.py:55
  37.5 3.3 %collective-permute-start.4 = (bf16[16,2048]{1,0:T(8,128)(2,1)S(1)}, bf16[16,2048]{1,0:T(8,128)(2,1)S(1)}, u32[]{:S(2)}, u32[]{:S(2)}) collective-permute-start(bf16[16,2048]{1,0:T(8,128)(2,1)S(1)} %slice.213), channel_id=1, source_target_pairs={{0,224},{32,0},{64,32},{96,64},{128,96},{160,128},{192,160},{224,1... | collective-permute-start | bytes 196616 | tf_op jit(solution)/shard_map/ppermute | solution.py:55
  43.3 3.4 %collective-permute-start.13 = (bf16[16,2048]{1,0:T(8,128)(2,1)S(1)}, bf16[16,2048]{1,0:T(8,128)(2,1)S(1)}, u32[]{:S(2)}, u32[]{:S(2)}) collective-permute-start(bf16[16,2048]{1,0:T(8,128)(2,1)S(1)} %slice.218), channel_id=1, source_target_pairs={{0,224},{32,0},{64,32},{96,64},{128,96},{160,128},{192,160},{224,1... | collective-permute-start | bytes 196616 | tf_op jit(solution)/shard_map/ppermute | solution.py:55
  49.5 5.1 %multiply_convert_fusion = f16[512,1792]{1,0:T(8,128)(2,1)} fusion(bf16[512,2048]{1,0:T(8,128)(2,1)S(1)} %constant_dynamic-update-slice_fusion.10, bf16[2048,1792]{1,0:T(8,128)(2,1)S(1)} %bitcast.9), kind=kOutput, calls=%fused_computation.1 | convolution fusion | flops 3759931392 | bytes 11272192 | tf_op jit(solution)/shard_map/dot_general | solution.py:108
  57.5 5.9 %all-to-all-start = ((f16[8,64,1792]{2,1,0:T(8,128)(2,1)}), f16[8,64,1792]{2,1,0:T(8,128)(2,1)S(1)}, u32[]{:S(2)}, u32[]{:S(2)}) async-start(f16[8,64,1792]{2,1,0:T(8,128)(2,1)} %bitcast.15), calls=%async_computation | async-start | bytes 3670016 | tf_op jit(solution)/shard_map/all_to_all | solution.py:89
  68.2 5.2 %shard_map.59 = (bf16[256,896]{1,0:T(8,128)(2,1)S(1)}, bf16[256,896]{1,0:T(8,128)(2,1)S(1)}) custom-call(bf16[256,2048]{1,0:T(8,128)(2,1)S(1)} %constant_dynamic-update-slice_fusion.21.refs_0_, bf16[256,2048]{1,0:T(8,128)(2,1)S(1)} %collective-permute-done.18.refs_1_, bf16[896,2048]{1,0:T(8,128)(2,1)S(1)} %copy-done.2), custom_call_target="tpu_custom_call" | custom-call | flops 1879048192 | bytes 6684672 | tf_op jit(solution)/shard_map/pallas_call | solution.py:35
  73.5 12.7 %all-to-all-done = f16[8,64,1792]{2,1,0:T(8,128)(2,1)S(1)} async-done(((f16[8,64,1792]{2,1,0:T(8,128)(2,1)}), f16[8,64,1792]{2,1,0:T(8,128)(2,1)S(1)}, u32[]{:S(2)}, u32[]{:S(2)}) %all-to-all-start) | async-done | bytes 1835040 | tf_op jit(solution)/shard_map/all_to_all | solution.py:89
  86.8 27.1 %all_to_all.15 = bf16[8,128,896]{2,1,0:T(8,128)(2,1)S(1)} all-to-all(bf16[8,128,896]{2,1,0:T(8,128)(2,1)S(1)} %pad_maximum_fusion), channel_id=1, replica_groups=mesh['z'=8,'xh'=2,'core'=2,'xl'=2,'y'=4] {'xl','y'}, dimensions={0} | all-to-all | bytes 3670016 | tf_op jit(solution)/shard_map/all_to_all | solution.py:89
  116.9 3.3 %shard_map.60 = (f32[256,2048]{1,0:T(8,128)S(1)}, bf16[256,2048]{1,0:T(8,128)(2,1)S(1)}) custom-call(bf16[256,896]{1,0:T(8,128)(2,1)S(1)} %bitcast.12, bf16[256,896]{1,0:T(8,128)(2,1)S(1)} %bitcast.11, bf16[896,2048]{1,0:T(8,128)(2,1)S(1)} %copy-done.3), custom_call_target="tpu_custom_call" | custom-call | flops 1879048192 | bytes 6684672 | tf_op jit(solution)/shard_map/pallas_call | solution.py:35
  120.3 5.7 %all-to-all-start.2 = ((bf16[8,64,1792]{2,1,0:T(8,128)(2,1)}), bf16[8,64,1792]{2,1,0:T(8,128)(2,1)}, u32[]{:S(2)}, u32[]{:S(2)}) async-start(bf16[8,64,1792]{2,1,0:T(8,128)(2,1)} %broadcast_in_dim.5), calls=%async_computation.2 | async-start | bytes 3670016 | tf_op jit(solution)/shard_map/all_to_all | solution.py:89
  133.7 4.8 %collective-permute-done.21 = bf16[64,2048]{1,0:T(8,128)(2,1)S(1)} collective-permute-done((bf16[64,2048]{1,0:T(8,128)(2,1)S(1)}, bf16[64,2048]{1,0:T(8,128)(2,1)S(1)}, u32[]{:S(2)}, u32[]{:S(2)}) %collective-permute-start.21) | collective-permute-done | bytes 262176 | tf_op jit(solution)/shard_map/ppermute | solution.py:55
  138.6 3.6 %collective-permute-done.20 = bf16[64,2048]{1,0:T(8,128)(2,1)S(1)} collective-permute-done((bf16[64,2048]{1,0:T(8,128)(2,1)S(1)}, bf16[64,2048]{1,0:T(8,128)(2,1)S(1)}, u32[]{:S(2)}, u32[]{:S(2)}) %collective-permute-start.20) | collective-permute-done | bytes 262176 | tf_op jit(solution)/shard_map/ppermute | solution.py:55
  145.5 5.5 %collective-permute-done.25 = bf16[32,2048]{1,0:T(8,128)(2,1)S(1)} collective-permute-done((bf16[32,2048]{1,0:T(8,128)(2,1)S(1)}, bf16[32,2048]{1,0:T(8,128)(2,1)S(1)}, u32[]{:S(2)}, u32[]{:S(2)}) %collective-permute-start.25) | collective-permute-done | bytes 131104 | tf_op jit(solution)/shard_map/ppermute | solution.py:55
  158.5 5.6 %shard_map.61 = (f32[256,2048]{1,0:T(8,128)S(1)}, bf16[256,2048]{1,0:T(8,128)(2,1)S(1)}) custom-call(bf16[256,1792]{1,0:T(8,128)(2,1)S(1)} %get-tuple-element.39.refs_0_, bf16[256,1792]{1,0:T(8,128)(2,1)S(1)} %get-tuple-element.38.refs_1_, bf16[2048,1792]{1,0:T(8,128)(2,1)S(1)} %bitcast.10), custom_call_target="tpu_custom_call" | custom-call | flops 3758096384 | bytes 11272192 | tf_op jit(solution)/shard_map/pallas_call | solution.py:35
  172.5 4.5 %collective-permute-done.29 = bf16[64,2048]{1,0:T(8,128)(2,1)S(1)} collective-permute-done((bf16[64,2048]{1,0:T(8,128)(2,1)S(1)}, bf16[64,2048]{1,0:T(8,128)(2,1)S(1)}, u32[]{:S(2)}, u32[]{:S(2)}) %collective-permute-start.29) | collective-permute-done | bytes 262176 | tf_op jit(solution)/shard_map/ppermute | solution.py:55
  177.1 3.2 %collective-permute-done.28 = bf16[64,2048]{1,0:T(8,128)(2,1)S(1)} collective-permute-done((bf16[64,2048]{1,0:T(8,128)(2,1)S(1)}, bf16[64,2048]{1,0:T(8,128)(2,1)S(1)}, u32[]{:S(2)}, u32[]{:S(2)}) %collective-permute-start.28) | collective-permute-done | bytes 262176 | tf_op jit(solution)/shard_map/ppermute | solution.py:55
  192.9 3.7 %collective-permute-done.34 = bf16[16,2048]{1,0:T(8,128)(2,1)S(1)} collective-permute-done((bf16[16,2048]{1,0:T(8,128)(2,1)S(1)}, bf16[16,2048]{1,0:T(8,128)(2,1)S(1)}, u32[]{:S(2)}, u32[]{:S(2)}) %collective-permute-start.34) | collective-permute-done | bytes 65568 | tf_op jit(solution)/shard_map/ppermute | solution.py:51
  (126 shorter events, 65.2 us)
Async XLA Ops:
  9.3 13.9 %collective-permute-start.5 = (bf16[32,2048]{1,0:T(8,128)(2,1)S(1)}, bf16[32,2048]{1,0:T(8,128)(2,1)S(1)}, u32[]{:S(2)}, u32[]{:S(2)}) collective-permute-start(bf16[32,2048]{1,0:T(8,128)(2,1)S(1)} %get-tuple-element.79), channel_id=1, source_target_pairs={{0,32},{32,64},{64,96},{96,128},{128,160},{160,192},{192,224},{224... | collective-permute-start | bytes 393224 | tf_op jit(solution)/shard_map/ppermute | solution.py:55
  11.3 12.0 %collective-permute-start.1 = (bf16[32,2048]{1,0:T(8,128)(2,1)S(1)}, bf16[32,2048]{1,0:T(8,128)(2,1)S(1)}, u32[]{:S(2)}, u32[]{:S(2)}) collective-permute-start(bf16[32,2048]{1,0:T(8,128)(2,1)S(1)} %get-tuple-element.79), channel_id=1, source_target_pairs={{0,224},{32,0},{64,32},{96,64},{128,96},{160,128},{192,160},{224,1... | collective-permute-start | bytes 393224 | tf_op jit(solution)/shard_map/ppermute | solution.py:55
  15.3 11.2 %collective-permute-start.14 = (bf16[32,2048]{1,0:T(8,128)(2,1)S(1)}, bf16[32,2048]{1,0:T(8,128)(2,1)S(1)}, u32[]{:S(2)}, u32[]{:S(2)}) collective-permute-start(bf16[32,2048]{1,0:T(8,128)(2,1)S(1)} %get-tuple-element.80), channel_id=1, source_target_pairs={{0,32},{32,64},{64,96},{96,128},{128,160},{160,192},{192,224},{224... | collective-permute-start | bytes 393224 | tf_op jit(solution)/shard_map/ppermute | solution.py:55
  15.3 11.2 %collective-permute-start.10 = (bf16[32,2048]{1,0:T(8,128)(2,1)S(1)}, bf16[32,2048]{1,0:T(8,128)(2,1)S(1)}, u32[]{:S(2)}, u32[]{:S(2)}) collective-permute-start(bf16[32,2048]{1,0:T(8,128)(2,1)S(1)} %get-tuple-element.80), channel_id=1, source_target_pairs={{0,224},{32,0},{64,32},{96,64},{128,96},{160,128},{192,160},{224,1... | collective-permute-start | bytes 393224 | tf_op jit(solution)/shard_map/ppermute | solution.py:55
  23.1 7.5 %collective-permute-start.6 = (bf16[32,2048]{1,0:T(8,128)(2,1)S(1)}, bf16[32,2048]{1,0:T(8,128)(2,1)S(1)}, u32[]{:S(2)}, u32[]{:S(2)}) collective-permute-start(bf16[32,2048]{1,0:T(8,128)(2,1)S(1)} %collective-permute-done.5), channel_id=1, source_target_pairs={{0,32},{32,64},{64,96},{96,128},{128,160},{160,192},{192,224},{224... | collective-permute-start | bytes 393224 | tf_op jit(solution)/shard_map/ppermute | solution.py:55
  26.5 7.4 %collective-permute-start.15 = (bf16[32,2048]{1,0:T(8,128)(2,1)S(1)}, bf16[32,2048]{1,0:T(8,128)(2,1)S(1)}, u32[]{:S(2)}, u32[]{:S(2)}) collective-permute-start(bf16[32,2048]{1,0:T(8,128)(2,1)S(1)} %collective-permute-done.14), channel_id=1, source_target_pairs={{0,32},{32,64},{64,96},{96,128},{128,160},{160,192},{192,224},{224... | collective-permute-start | bytes 393224 | tf_op jit(solution)/shard_map/ppermute | solution.py:55
  26.5 7.4 %collective-permute-start.11 = (bf16[32,2048]{1,0:T(8,128)(2,1)S(1)}, bf16[32,2048]{1,0:T(8,128)(2,1)S(1)}, u32[]{:S(2)}, u32[]{:S(2)}) collective-permute-start(bf16[32,2048]{1,0:T(8,128)(2,1)S(1)} %collective-permute-done.10), channel_id=1, source_target_pairs={{0,224},{32,0},{64,32},{96,64},{128,96},{160,128},{192,160},{224,1... | collective-permute-start | bytes 393224 | tf_op jit(solution)/shard_map/ppermute | solution.py:55
  33.9 9.2 %collective-permute-start.16 = (bf16[32,2048]{1,0:T(8,128)(2,1)S(1)}, bf16[32,2048]{1,0:T(8,128)(2,1)S(1)}, u32[]{:S(2)}, u32[]{:S(2)}) collective-permute-start(bf16[32,2048]{1,0:T(8,128)(2,1)S(1)} %collective-permute-done.15), channel_id=1, source_target_pairs={{0,32},{32,64},{64,96},{96,128},{128,160},{160,192},{192,224},{224... | collective-permute-start | bytes 393224 | tf_op jit(solution)/shard_map/ppermute | solution.py:55
  33.9 9.4 %collective-permute-start.12 = (bf16[32,2048]{1,0:T(8,128)(2,1)S(1)}, bf16[32,2048]{1,0:T(8,128)(2,1)S(1)}, u32[]{:S(2)}, u32[]{:S(2)}) collective-permute-start(bf16[32,2048]{1,0:T(8,128)(2,1)S(1)} %collective-permute-done.11), channel_id=1, source_target_pairs={{0,224},{32,0},{64,32},{96,64},{128,96},{160,128},{192,160},{224,1... | collective-permute-start | bytes 393224 | tf_op jit(solution)/shard_map/ppermute | solution.py:55
  57.5 28.7 %all-to-all-start = ((f16[8,64,1792]{2,1,0:T(8,128)(2,1)}), f16[8,64,1792]{2,1,0:T(8,128)(2,1)S(1)}, u32[]{:S(2)}, u32[]{:S(2)}) async-start(f16[8,64,1792]{2,1,0:T(8,128)(2,1)} %bitcast.15), calls=%async_computation | async-start | bytes 3670016 | tf_op jit(solution)/shard_map/all_to_all | solution.py:89
  120.3 33.5 %all-to-all-start.2 = ((bf16[8,64,1792]{2,1,0:T(8,128)(2,1)}), bf16[8,64,1792]{2,1,0:T(8,128)(2,1)}, u32[]{:S(2)}, u32[]{:S(2)}) async-start(bf16[8,64,1792]{2,1,0:T(8,128)(2,1)} %broadcast_in_dim.5), calls=%async_computation.2 | async-start | bytes 3670016 | tf_op jit(solution)/shard_map/all_to_all | solution.py:89
  127.6 10.9 %collective-permute-start.21 = (bf16[64,2048]{1,0:T(8,128)(2,1)S(1)}, bf16[64,2048]{1,0:T(8,128)(2,1)S(1)}, u32[]{:S(2)}, u32[]{:S(2)}) collective-permute-start(bf16[64,2048]{1,0:T(8,128)(2,1)S(1)} %pad_maximum_fusion.3), channel_id=1, source_target_pairs={{0,224},{32,0},{64,32},{96,64},{128,96},{160,128},{192,160},{224,1... | collective-permute-start | bytes 786440 | tf_op jit(solution)/shard_map/ppermute | solution.py:55
  130.6 11.5 %collective-permute-start.20 = (bf16[64,2048]{1,0:T(8,128)(2,1)S(1)}, bf16[64,2048]{1,0:T(8,128)(2,1)S(1)}, u32[]{:S(2)}, u32[]{:S(2)}) collective-permute-start(bf16[64,2048]{1,0:T(8,128)(2,1)S(1)} %pad_maximum_fusion.2), channel_id=1, source_target_pairs={{0,32},{32,64},{64,96},{96,128},{128,160},{160,192},{192,224},{224... | collective-permute-start | bytes 786440 | tf_op jit(solution)/shard_map/ppermute | solution.py:55
  130.7 11.5 %collective-permute-start.24 = (bf16[16,2048]{1,0:T(8,128)(2,1)S(1)}, bf16[16,2048]{1,0:T(8,128)(2,1)S(1)}, u32[]{:S(2)}, u32[]{:S(2)}) collective-permute-start(bf16[16,2048]{1,0:T(8,128)(2,1)S(1)} %get-tuple-element.48), channel_id=1, source_target_pairs={{0,192},{32,224},{64,0},{96,32},{128,64},{160,96},{192,128},{224,1... | collective-permute-start | bytes 196616 | tf_op jit(solution)/shard_map/ppermute | solution.py:55
  132.3 9.9 %collective-permute-start.22 = (bf16[16,2048]{1,0:T(8,128)(2,1)S(1)}, bf16[16,2048]{1,0:T(8,128)(2,1)S(1)}, u32[]{:S(2)}, u32[]{:S(2)}) collective-permute-start(bf16[16,2048]{1,0:T(8,128)(2,1)S(1)} %get-tuple-element.49), channel_id=1, source_target_pairs={{0,64},{32,96},{64,128},{96,160},{128,192},{160,224},{192,0},{224,... | collective-permute-start | bytes 196616 | tf_op jit(solution)/shard_map/ppermute | solution.py:55
  142.3 8.7 %collective-permute-start.25 = (bf16[32,2048]{1,0:T(8,128)(2,1)S(1)}, bf16[32,2048]{1,0:T(8,128)(2,1)S(1)}, u32[]{:S(2)}, u32[]{:S(2)}) collective-permute-start(bf16[32,2048]{1,0:T(8,128)(2,1)S(1)} %get-tuple-element.36), channel_id=1, source_target_pairs={{0,192},{32,224},{64,0},{96,32},{128,64},{160,96},{192,128},{224,1... | collective-permute-start | bytes 393224 | tf_op jit(solution)/shard_map/ppermute | solution.py:55
  144.3 9.5 %collective-permute-start.23 = (bf16[32,2048]{1,0:T(8,128)(2,1)S(1)}, bf16[32,2048]{1,0:T(8,128)(2,1)S(1)}, u32[]{:S(2)}, u32[]{:S(2)}) collective-permute-start(bf16[32,2048]{1,0:T(8,128)(2,1)S(1)} %get-tuple-element.37), channel_id=1, source_target_pairs={{0,64},{32,96},{64,128},{96,160},{128,192},{160,224},{192,0},{224,... | collective-permute-start | bytes 393224 | tf_op jit(solution)/shard_map/ppermute | solution.py:55
  167.3 9.8 %collective-permute-start.29 = (bf16[64,2048]{1,0:T(8,128)(2,1)S(1)}, bf16[64,2048]{1,0:T(8,128)(2,1)S(1)}, u32[]{:S(2)}, u32[]{:S(2)}) collective-permute-start(bf16[64,2048]{1,0:T(8,128)(2,1)S(1)} %pad_maximum_fusion.5), channel_id=1, source_target_pairs={{0,224},{32,0},{64,32},{96,64},{128,96},{160,128},{192,160},{224,1... | collective-permute-start | bytes 786440 | tf_op jit(solution)/shard_map/ppermute | solution.py:55
  168.8 11.5 %collective-permute-start.28 = (bf16[64,2048]{1,0:T(8,128)(2,1)S(1)}, bf16[64,2048]{1,0:T(8,128)(2,1)S(1)}, u32[]{:S(2)}, u32[]{:S(2)}) collective-permute-start(bf16[64,2048]{1,0:T(8,128)(2,1)S(1)} %pad_maximum_fusion.4), channel_id=1, source_target_pairs={{0,32},{32,64},{64,96},{96,128},{128,160},{160,192},{192,224},{224... | collective-permute-start | bytes 786440 | tf_op jit(solution)/shard_map/ppermute | solution.py:55
  169.5 10.8 %collective-permute-start.32 = (bf16[16,2048]{1,0:T(8,128)(2,1)S(1)}, bf16[16,2048]{1,0:T(8,128)(2,1)S(1)}, u32[]{:S(2)}, u32[]{:S(2)}) collective-permute-start(bf16[16,2048]{1,0:T(8,128)(2,1)S(1)} %get-tuple-element.42), channel_id=1, source_target_pairs={{0,192},{32,224},{64,0},{96,32},{128,64},{160,96},{192,128},{224,1... | collective-permute-start | bytes 196616 | tf_op jit(solution)/shard_map/ppermute | solution.py:55
  170.6 9.7 %collective-permute-start.30 = (bf16[16,2048]{1,0:T(8,128)(2,1)S(1)}, bf16[16,2048]{1,0:T(8,128)(2,1)S(1)}, u32[]{:S(2)}, u32[]{:S(2)}) collective-permute-start(bf16[16,2048]{1,0:T(8,128)(2,1)S(1)} %get-tuple-element.43), channel_id=1, source_target_pairs={{0,64},{32,96},{64,128},{96,160},{128,192},{160,224},{192,0},{224,... | collective-permute-start | bytes 196616 | tf_op jit(solution)/shard_map/ppermute | solution.py:55
  180.4 7.6 %collective-permute-start.33 = (bf16[32,2048]{1,0:T(8,128)(2,1)S(1)}, bf16[32,2048]{1,0:T(8,128)(2,1)S(1)}, u32[]{:S(2)}, u32[]{:S(2)}) collective-permute-start(bf16[32,2048]{1,0:T(8,128)(2,1)S(1)} %get-tuple-element.34), channel_id=1, source_target_pairs={{0,192},{32,224},{64,0},{96,32},{128,64},{160,96},{192,128},{224,1... | collective-permute-start | bytes 393224 | tf_op jit(solution)/shard_map/ppermute | solution.py:55
  182.2 8.5 %collective-permute-start.31 = (bf16[32,2048]{1,0:T(8,128)(2,1)S(1)}, bf16[32,2048]{1,0:T(8,128)(2,1)S(1)}, u32[]{:S(2)}, u32[]{:S(2)}) collective-permute-start(bf16[32,2048]{1,0:T(8,128)(2,1)S(1)} %get-tuple-element.35), channel_id=1, source_target_pairs={{0,64},{32,96},{64,128},{96,160},{128,192},{160,224},{192,0},{224,... | collective-permute-start | bytes 393224 | tf_op jit(solution)/shard_map/ppermute | solution.py:55
  184.4 7.9 %collective-permute-start.26 = (bf16[16,2048]{1,0:T(8,128)(2,1)S(1)}, bf16[16,2048]{1,0:T(8,128)(2,1)S(1)}, u32[]{:S(2)}, u32[]{:S(2)}) collective-permute-start(bf16[16,2048]{1,0:T(8,128)(2,1)S(1)} %slice.313), channel_id=1, source_target_pairs={{0,16},{16,0},{1,17},{17,1},{2,18},{18,2},{3,19},{19,3},{4,20},{20... | collective-permute-start | bytes 196616 | tf_op jit(solution)/shard_map/ppermute | solution.py:51
  (18 other events, 99.1 us)
where the time goes:
time: 198 us; the launch traced here: 197 us
  starting transfers between devices  63.2 us (32%)
  waiting for transfers between devices  60.2 us (30%)
  blocking collectives  27.1 us (14%)
  local copies, waits for them, and re-layouts  19.1 us (10%)
  Pallas kernels  14.1 us (7%)
  other arithmetic  7.38 us (4%)
  matrix products  5.08 us (3%)
    ppermute x28, starting transfers between devices, shift(): return lax.ppermute(x, 'z', [(i, (i - by) % NZ) for i in range(NZ)])  46.8 us
    ppermute x28, waiting for transfers between devices, shift(): return lax.ppermute(x, 'z', [(i, (i - by) % NZ) for i in range(NZ)])  34.8 us
    all_to_all x1, blocking collectives, exchange(): return lax.all_to_all(x, COL, 0, 0, tiled=True)  27.1 us
    unnamed x28, local copies, waits for them, and re-layouts  15.7 us
    pallas_call x3, Pallas kernels, product(): pl.pallas_call(body, grid=(n // width,), in_specs=[pl.BlockSpec(x.shape,...  14.1 us
    ppermute x7, waiting for transfers between devices, swap(): return lax.ppermute(x, axis, SWAP)  12.7 us
    all_to_all x2, waiting for transfers between devices, exchange(): return lax.all_to_all(x, COL, 0, 0, tiled=True)  12.7 us
    all_to_all x2, starting transfers between devices, exchange(): return lax.all_to_all(x, COL, 0, 0, tiled=True)  11.6 us
  transfers between devices with their start and end apart: 37, of which 19 were waited for; matrix products, arithmetic and copies ran while one was open for 5% of the time, Pallas kernels for 3%

commit v1 on v0

--- a/solution.py
+++ b/solution.py
@@ -55,14 +55,17 @@
     return lax.ppermute(x, "z", [(i, (i - by) % NZ) for i in range(NZ)])
 
 
-def gather_z(pair):
-    half = pair.shape[0] // 2
-    got = {0: pair}
+def gather_z(block):
+    half = block.shape[0] // 2
+    got = {0: block}
     for step in (1, 2, 3):
         got[step] = shift(got[step - 1], 1)
         got[-step] = shift(got[1 - step], -1)
-    got[4] = jnp.concatenate([shift(got[3][:half], 1), shift(got[-3][half:], -1)])
-    return jnp.concatenate([got[r] if r <= 4 else got[r - NZ] for r in range(NZ)])
+    first = [got[r][:half] for r in range(4)] + [shift(got[3][:half], 1)]
+    second = [got[r][half:] for r in range(4)] + [shift(got[-3][half:], -1)]
+    first += [got[r][:half] for r in (-3, -2, -1)]
+    second += [got[r][half:] for r in (-3, -2, -1)]
+    return jnp.concatenate(first), jnp.concatenate(second)
 
 
 def scatter_rows(mine, held=None):
@@ -78,10 +81,10 @@
         total = total + near[: 2 * rows]
         zero = jnp.zeros_like(far)
         relayed = jnp.concatenate([far, zero] if way == 1 else [zero, far])
-        second = block[2 * way % NZ] + near[2 * rows :] + relayed
-        seconds.append(shift(second.astype(BF), -2 * way))
+        seconds.append((block[2 * way % NZ] + near[2 * rows :] + relayed).astype(BF))
     seconds, held = lax.optimization_barrier((seconds, held))
-    total = total + seconds[0].astype(F32) + seconds[1].astype(F32)
+    for way, second in zip((1, -1), seconds):
+        total = total + shift(second, -2 * way).astype(F32)
     return (total[:rows] + swap(total[rows:].astype(BF), "xh").astype(F32)).astype(BF), held
 
 
@@ -99,8 +102,7 @@
     weights = gate_up.reshape(gate_up.shape[0], 2 * width)
 
     other = swap(jnp.concatenate([tokens, out_grad]), "xh")
-    tok = gather_z(jnp.concatenate([tokens, other[:n]]))
-    grad = gather_z(jnp.concatenate([out_grad, other[n:]]))
+    tok, grad = gather_z(jnp.concatenate([tokens, other[:n], out_grad, other[n:]]))
     half = tok.shape[0]
     chunk = half // 4
 
@@ -108,7 +110,7 @@
     parts = (jnp.dot(tok, weights, preferred_element_type=F32) * SCALE).astype(F16)
     both = exchange(parts.reshape(8, chunk, -1))
     part = jnp.concatenate(
-        product([grad, swap(grad, "core")], down_weight, True, (BF, BF), 128)
+        product([grad, swap(grad, "core")], down_weight, True, (BF, BF), width)
     ).reshape(8, chunk, width)
 
     both = both.astype(F32).sum(0) * (1.0 / SCALE)
@@ -127,8 +129,8 @@
 
     kept, sent = product(hidden, down_weight, False, (F32, BF), 512)
     block_out, grads = scatter_rows(kept + swap(sent, "core").astype(F32), grads)
-    out, sent = product([grads[:half], grads[half:]], weights, True, (F32, BF), 256)
-    out = out + swap(sent, "core").astype(F32)
+    out = lax.dot_general(grads, weights, LAST, preferred_element_type=F32)
+    out = out[:half] + swap(out[half:].astype(BF), "core").astype(F32)
     grad_tokens, _ = scatter_rows(out)
     return block_out, grad_tokens
 

time: 198 us -> 194 us (0.980)
  waiting for transfers between devices: 60.2 us -> 77.3 us
  starting transfers between devices: 63.2 us -> 51.9 us
  Pallas kernels: 14.1 us -> 5.68 us
  local copies, waits for them, and re-layouts: 19.1 us -> 10.9 us
  matrix products: 5.08 us -> 12 us
    ppermute x28 -> x20, starting transfers between devices: 46.8 us -> 35.6 us  [shift(): return lax.ppermute(x, 'z', [(i, (i - by) % NZ) for i in range(NZ)])]
    all_to_all x2, waiting for transfers between devices: 12.7 us -> 23.1 us  [exchange(): return lax.all_to_all(x, COL, 0, 0, tiled=True)]
    pallas_call x3 -> x2, Pallas kernels: 14.1 us -> 5.68 us  [product(): pl.pallas_call(body, grid=(n // width,), in_specs=[pl.BlockSpec(x.shape,...]
    unnamed x28 -> x18, local copies, waits for them, and re-layouts: 15.7 us -> 8.85 us
    dot_general x0 -> x1, matrix products: none -> 6.82 us  [per_device(): out = lax.dot_general(grads, weights, LAST, preferred_element_type=F32)]
    ppermute x28 -> x20, waiting for transfers between devices: 34.8 us -> 40.7 us  [shift(): return lax.ppermute(x, 'z', [(i, (i - by) % NZ) for i in range(NZ)])]
  transfers between devices with their start and end apart: 37 -> 29, of which waited for: 19 -> 16; matrix products, arithmetic and copies ran while one was open for 5% -> 5% of each run, Pallas kernels for 3% -> 1%
where the time goes in v1:
time: 194 us; the launch traced here: 193 us
  waiting for transfers between devices  77.3 us (40%)
  starting transfers between devices  51.9 us (27%)
  blocking collectives  27.1 us (14%)
  matrix products  12 us (6%)
  local copies, waits for them, and re-layouts  10.9 us (6%)
  other arithmetic  7.38 us (4%)
  Pallas kernels  5.68 us (3%)
    ppermute x20, waiting for transfers between devices, shift(): return lax.ppermute(x, 'z', [(i, (i - by) % NZ) for i in range(NZ)])  40.7 us
    ppermute x20, starting transfers between devices, shift(): return lax.ppermute(x, 'z', [(i, (i - by) % NZ) for i in range(NZ)])  35.6 us
    all_to_all x1, blocking collectives, exchange(): return lax.all_to_all(x, COL, 0, 0, tiled=True)  27.1 us
    all_to_all x2, waiting for transfers between devices, exchange(): return lax.all_to_all(x, COL, 0, 0, tiled=True)  23.1 us
    ppermute x7, waiting for transfers between devices, swap(): return lax.ppermute(x, axis, SWAP)  13.5 us
    all_to_all x2, starting transfers between devices, exchange(): return lax.all_to_all(x, COL, 0, 0, tiled=True)  11.6 us
    unnamed x18, local copies, waits for them, and re-layouts  8.85 us
    dot_general x1, matrix products, per_device(): out = lax.dot_general(grads, weights, LAST, preferred_element_type=F32)  6.82 us
  transfers between devices with their start and end apart: 29, of which 16 were waited for; matrix products, arithmetic and copies ran while one was open for 5% of the time, Pallas kernels for 1%

profile of v1, /device:TPU:6, one launch (start us, length us, event | category | flops | bytes accessed | tf_op | source)
XLA Modules:
  0.0 193.4 jit_solution(7568451075090857050)
XLA Ops:
  3.9 4.4 %collective-permute-done = bf16[32,2048]{1,0:T(8,128)(2,1)S(1)} collective-permute-done((bf16[32,2048]{1,0:T(8,128)(2,1)S(1)}, bf16[32,2048]{1,0:T(8,128)(2,1)S(1)}, u32[]{:S(2)}, u32[]{:S(2)}) %collective-permute-start) | collective-permute-done | bytes 131104 | tf_op jit(solution)/shard_map/ppermute | solution.py:51
  9.3 5.9 %collective-permute-start.1 = (bf16[64,2048]{1,0:T(8,128)(2,1)S(1)}, bf16[64,2048]{1,0:T(8,128)(2,1)S(1)}, u32[]{:S(2)}, u32[]{:S(2)}) collective-permute-start(bf16[64,2048]{1,0:T(8,128)(2,1)S(1)} %pad_maximum_fusion.2), channel_id=1, source_target_pairs={{0,224},{32,0},{64,32},{96,64},{128,96},{160,128},{192,160},{224,1... | collective-permute-start | bytes 786440 | tf_op jit(solution)/shard_map/ppermute | solution.py:55
  15.2 4.7 %collective-permute-done.1 = bf16[64,2048]{1,0:T(8,128)(2,1)S(1)} collective-permute-done((bf16[64,2048]{1,0:T(8,128)(2,1)S(1)}, bf16[64,2048]{1,0:T(8,128)(2,1)S(1)}, u32[]{:S(2)}, u32[]{:S(2)}) %collective-permute-start.1) | collective-permute-done | bytes 262176 | tf_op jit(solution)/shard_map/ppermute | solution.py:55
  19.9 3.7 %collective-permute-start.2 = (bf16[64,2048]{1,0:T(8,128)(2,1)S(1)}, bf16[64,2048]{1,0:T(8,128)(2,1)S(1)}, u32[]{:S(2)}, u32[]{:S(2)}) collective-permute-start(bf16[64,2048]{1,0:T(8,128)(2,1)S(1)} %collective-permute-done.1), channel_id=1, source_target_pairs={{0,224},{32,0},{64,32},{96,64},{128,96},{160,128},{192,160},{224,1... | collective-permute-start | bytes 786440 | tf_op jit(solution)/shard_map/ppermute | solution.py:55
  23.6 3.8 %collective-permute-done.2 = bf16[64,2048]{1,0:T(8,128)(2,1)S(1)} collective-permute-done((bf16[64,2048]{1,0:T(8,128)(2,1)S(1)}, bf16[64,2048]{1,0:T(8,128)(2,1)S(1)}, u32[]{:S(2)}, u32[]{:S(2)}) %collective-permute-start.2) | collective-permute-done | bytes 262176 | tf_op jit(solution)/shard_map/ppermute | solution.py:55
  27.5 3.7 %collective-permute-start.3 = (bf16[64,2048]{1,0:T(8,128)(2,1)S(1)}, bf16[64,2048]{1,0:T(8,128)(2,1)S(1)}, u32[]{:S(2)}, u32[]{:S(2)}) collective-permute-start(bf16[64,2048]{1,0:T(8,128)(2,1)S(1)} %collective-permute-done.2), channel_id=1, source_target_pairs={{0,224},{32,0},{64,32},{96,64},{128,96},{160,128},{192,160},{224,1... | collective-permute-start | bytes 786440 | tf_op jit(solution)/shard_map/ppermute | solution.py:55
  31.2 8.1 %collective-permute-done.7 = bf16[64,2048]{1,0:T(8,128)(2,1)S(1)} collective-permute-done((bf16[64,2048]{1,0:T(8,128)(2,1)S(1)}, bf16[64,2048]{1,0:T(8,128)(2,1)S(1)}, u32[]{:S(2)}, u32[]{:S(2)}) %collective-permute-start.7) | collective-permute-done | bytes 262176 | tf_op jit(solution)/shard_map/ppermute | solution.py:55
  39.5 3.3 %collective-permute-start.4 = (bf16[32,2048]{1,0:T(8,128)(2,1)S(1)}, bf16[32,2048]{1,0:T(8,128)(2,1)S(1)}, u32[]{:S(2)}, u32[]{:S(2)}) collective-permute-start(bf16[32,2048]{1,0:T(8,128)(2,1)S(1)} %get-tuple-element.62), channel_id=1, source_target_pairs={{0,224},{32,0},{64,32},{96,64},{128,96},{160,128},{192,160},{224,1... | collective-permute-start | bytes 393224 | tf_op jit(solution)/shard_map/ppermute | solution.py:55
  45.9 4.6 %copy.6 = bf16[256,8,2,896]{3,1,2,0:T(8,128)(2,1)S(1)} copy(bf16[256,8,2,896]{3,2,1,0:T(2,128)(2,1)} %bitcast.13) | data formatting | bytes 14680064
  50.6 5.1 %multiply_convert_fusion = f16[512,1792]{1,0:T(8,128)(2,1)} fusion(bf16[512,2048]{1,0:T(8,128)(2,1)S(1)} %constant_dynamic-update-slice_fusion.4, bf16[2048,1792]{1,0:T(8,128)(2,1)S(1)} %bitcast.14), kind=kOutput, calls=%fused_computation.1 | convolution fusion | flops 3759931392 | bytes 11272192 | tf_op jit(solution)/shard_map/dot_general | solution.py:110
  55.7 5.9 %all-to-all-start = ((f16[8,64,1792]{2,1,0:T(8,128)(2,1)}), f16[8,64,1792]{2,1,0:T(8,128)(2,1)S(1)}, u32[]{:S(2)}, u32[]{:S(2)}) async-start(f16[8,64,1792]{2,1,0:T(8,128)(2,1)} %bitcast.17), calls=%async_computation | async-start | bytes 3670016 | tf_op jit(solution)/shard_map/all_to_all | solution.py:92
  68.8 16.2 %all-to-all-done = f16[8,64,1792]{2,1,0:T(8,128)(2,1)S(1)} async-done(((f16[8,64,1792]{2,1,0:T(8,128)(2,1)}), f16[8,64,1792]{2,1,0:T(8,128)(2,1)S(1)}, u32[]{:S(2)}, u32[]{:S(2)}) %all-to-all-start) | async-done | bytes 1835040 | tf_op jit(solution)/shard_map/all_to_all | solution.py:92
  85.6 27.1 %all_to_all.15 = bf16[8,128,896]{2,1,0:T(8,128)(2,1)S(1)} all-to-all(bf16[8,128,896]{2,1,0:T(8,128)(2,1)S(1)} %pad_maximum_fusion), channel_id=1, replica_groups=mesh['z'=8,'xh'=2,'core'=2,'xl'=2,'y'=4] {'xl','y'}, dimensions={0} | all-to-all | bytes 3670016 | tf_op jit(solution)/shard_map/all_to_all | solution.py:92
  115.7 3.3 %shard_map.60 = (f32[256,2048]{1,0:T(8,128)S(1)}, bf16[256,2048]{1,0:T(8,128)(2,1)S(1)}) custom-call(bf16[256,896]{1,0:T(8,128)(2,1)S(1)} %bitcast.12, bf16[256,896]{1,0:T(8,128)(2,1)S(1)} %bitcast.11, bf16[896,2048]{1,0:T(8,128)(2,1)S(1)} %copy-done.1), custom_call_target="tpu_custom_call" | custom-call | flops 1879048192 | bytes 6684672 | tf_op jit(solution)/shard_map/pallas_call | solution.py:35
  119.1 5.7 %all-to-all-start.2 = ((bf16[8,64,1792]{2,1,0:T(8,128)(2,1)}), bf16[8,64,1792]{2,1,0:T(8,128)(2,1)}, u32[]{:S(2)}, u32[]{:S(2)}) async-start(bf16[8,64,1792]{2,1,0:T(8,128)(2,1)} %broadcast_in_dim.5), calls=%async_computation.2 | async-start | bytes 3670016 | tf_op jit(solution)/shard_map/all_to_all | solution.py:92
  126.5 3.4 %collective-permute-start.13 = (bf16[64,2048]{1,0:T(8,128)(2,1)S(1)}, bf16[64,2048]{1,0:T(8,128)(2,1)S(1)}, u32[]{:S(2)}, u32[]{:S(2)}) collective-permute-start(bf16[64,2048]{1,0:T(8,128)(2,1)S(1)} %pad_maximum_fusion.4), channel_id=1, source_target_pairs={{0,224},{32,0},{64,32},{96,64},{128,96},{160,128},{192,160},{224,1... | collective-permute-start | bytes 786440 | tf_op jit(solution)/shard_map/ppermute | solution.py:55
  133.0 4.8 %collective-permute-done.13 = bf16[64,2048]{1,0:T(8,128)(2,1)S(1)} collective-permute-done((bf16[64,2048]{1,0:T(8,128)(2,1)S(1)}, bf16[64,2048]{1,0:T(8,128)(2,1)S(1)}, u32[]{:S(2)}, u32[]{:S(2)}) %collective-permute-start.13) | collective-permute-done | bytes 262176 | tf_op jit(solution)/shard_map/ppermute | solution.py:55
  137.9 3.6 %collective-permute-done.12 = bf16[64,2048]{1,0:T(8,128)(2,1)S(1)} collective-permute-done((bf16[64,2048]{1,0:T(8,128)(2,1)S(1)}, bf16[64,2048]{1,0:T(8,128)(2,1)S(1)}, u32[]{:S(2)}, u32[]{:S(2)}) %collective-permute-start.12) | collective-permute-done | bytes 262176 | tf_op jit(solution)/shard_map/ppermute | solution.py:55
  141.6 6.9 %all-to-all-done.2 = bf16[8,64,1792]{2,1,0:T(8,128)(2,1)} async-done(((bf16[8,64,1792]{2,1,0:T(8,128)(2,1)}), bf16[8,64,1792]{2,1,0:T(8,128)(2,1)}, u32[]{:S(2)}, u32[]{:S(2)}) %all-to-all-start.2) | async-done | bytes 1835040 | tf_op jit(solution)/shard_map/all_to_all | solution.py:92
  148.5 6.8 %fusion.21 = f32[512,2048]{1,0:T(8,128)S(1)} fusion(bf16[512,1792]{1,0:T(8,128)(2,1)} %bitcast.4, bf16[2048,1792]{1,0:T(8,128)(2,1)} %bitcast.15), kind=kOutput, calls=%fused_computation.81 | convolution fusion | flops 3758096384 | bytes 13369344 | tf_op jit(solution)/shard_map/dot_general | solution.py:132
  158.7 3.4 %collective-permute-start.21 = (bf16[64,2048]{1,0:T(8,128)(2,1)S(1)}, bf16[64,2048]{1,0:T(8,128)(2,1)S(1)}, u32[]{:S(2)}, u32[]{:S(2)}) collective-permute-start(bf16[64,2048]{1,0:T(8,128)(2,1)S(1)} %pad_maximum_fusion.6), channel_id=1, source_target_pairs={{0,224},{32,0},{64,32},{96,64},{128,96},{160,128},{192,160},{224,1... | collective-permute-start | bytes 786440 | tf_op jit(solution)/shard_map/ppermute | solution.py:55
  170.1 5.3 %collective-permute-done.20 = bf16[64,2048]{1,0:T(8,128)(2,1)S(1)} collective-permute-done((bf16[64,2048]{1,0:T(8,128)(2,1)S(1)}, bf16[64,2048]{1,0:T(8,128)(2,1)S(1)}, u32[]{:S(2)}, u32[]{:S(2)}) %collective-permute-start.20) | collective-permute-done | bytes 262176 | tf_op jit(solution)/shard_map/ppermute | solution.py:55
  181.9 4.9 %collective-permute-done.24 = bf16[32,2048]{1,0:T(8,128)(2,1)S(1)} collective-permute-done((bf16[32,2048]{1,0:T(8,128)(2,1)S(1)}, bf16[32,2048]{1,0:T(8,128)(2,1)S(1)}, u32[]{:S(2)}, u32[]{:S(2)}) %collective-permute-start.24) | collective-permute-done | bytes 131104 | tf_op jit(solution)/shard_map/ppermute | solution.py:55
  189.0 3.7 %collective-permute-done.26 = bf16[16,2048]{1,0:T(8,128)(2,1)S(1)} collective-permute-done((bf16[16,2048]{1,0:T(8,128)(2,1)S(1)}, bf16[16,2048]{1,0:T(8,128)(2,1)S(1)}, u32[]{:S(2)}, u32[]{:S(2)}) %collective-permute-start.26) | collective-permute-done | bytes 65568 | tf_op jit(solution)/shard_map/ppermute | solution.py:51
  (96 shorter events, 43.8 us)
Async XLA Ops:
  1.5 6.8 %collective-permute-start = (bf16[32,2048]{1,0:T(8,128)(2,1)S(1)}, bf16[32,2048]{1,0:T(8,128)(2,1)S(1)}, u32[]{:S(2)}, u32[]{:S(2)}) collective-permute-start(bf16[32,2048]{1,0:T(8,128)(2,1)S(1)} %pad_maximum_fusion.8), channel_id=1, source_target_pairs={{0,16},{16,0},{1,17},{17,1},{2,18},{18,2},{3,19},{19,3},{4,20},{20... | collective-permute-start | bytes 393224 | tf_op jit(solution)/shard_map/ppermute | solution.py:51
  9.3 10.6 %collective-permute-start.1 = (bf16[64,2048]{1,0:T(8,128)(2,1)S(1)}, bf16[64,2048]{1,0:T(8,128)(2,1)S(1)}, u32[]{:S(2)}, u32[]{:S(2)}) collective-permute-start(bf16[64,2048]{1,0:T(8,128)(2,1)S(1)} %pad_maximum_fusion.2), channel_id=1, source_target_pairs={{0,224},{32,0},{64,32},{96,64},{128,96},{160,128},{192,160},{224,1... | collective-permute-start | bytes 786440 | tf_op jit(solution)/shard_map/ppermute | solution.py:55
  15.2 8.4 %collective-permute-start.5 = (bf16[64,2048]{1,0:T(8,128)(2,1)S(1)}, bf16[64,2048]{1,0:T(8,128)(2,1)S(1)}, u32[]{:S(2)}, u32[]{:S(2)}) collective-permute-start(bf16[64,2048]{1,0:T(8,128)(2,1)S(1)} %pad_maximum_fusion.2), channel_id=1, source_target_pairs={{0,32},{32,64},{64,96},{96,128},{128,160},{160,192},{192,224},{224... | collective-permute-start | bytes 786440 | tf_op jit(solution)/shard_map/ppermute | solution.py:55
  19.9 7.6 %collective-permute-start.2 = (bf16[64,2048]{1,0:T(8,128)(2,1)S(1)}, bf16[64,2048]{1,0:T(8,128)(2,1)S(1)}, u32[]{:S(2)}, u32[]{:S(2)}) collective-permute-start(bf16[64,2048]{1,0:T(8,128)(2,1)S(1)} %collective-permute-done.1), channel_id=1, source_target_pairs={{0,224},{32,0},{64,32},{96,64},{128,96},{160,128},{192,160},{224,1... | collective-permute-start | bytes 786440 | tf_op jit(solution)/shard_map/ppermute | solution.py:55
  23.6 7.6 %collective-permute-start.6 = (bf16[64,2048]{1,0:T(8,128)(2,1)S(1)}, bf16[64,2048]{1,0:T(8,128)(2,1)S(1)}, u32[]{:S(2)}, u32[]{:S(2)}) collective-permute-start(bf16[64,2048]{1,0:T(8,128)(2,1)S(1)} %collective-permute-done.5), channel_id=1, source_target_pairs={{0,32},{32,64},{64,96},{96,128},{128,160},{160,192},{192,224},{224... | collective-permute-start | bytes 786440 | tf_op jit(solution)/shard_map/ppermute | solution.py:55
  27.5 12.0 %collective-permute-start.3 = (bf16[64,2048]{1,0:T(8,128)(2,1)S(1)}, bf16[64,2048]{1,0:T(8,128)(2,1)S(1)}, u32[]{:S(2)}, u32[]{:S(2)}) collective-permute-start(bf16[64,2048]{1,0:T(8,128)(2,1)S(1)} %collective-permute-done.2), channel_id=1, source_target_pairs={{0,224},{32,0},{64,32},{96,64},{128,96},{160,128},{192,160},{224,1... | collective-permute-start | bytes 786440 | tf_op jit(solution)/shard_map/ppermute | solution.py:55
  31.2 8.2 %collective-permute-start.7 = (bf16[64,2048]{1,0:T(8,128)(2,1)S(1)}, bf16[64,2048]{1,0:T(8,128)(2,1)S(1)}, u32[]{:S(2)}, u32[]{:S(2)}) collective-permute-start(bf16[64,2048]{1,0:T(8,128)(2,1)S(1)} %collective-permute-done.6), channel_id=1, source_target_pairs={{0,32},{32,64},{64,96},{96,128},{128,160},{160,192},{192,224},{224... | collective-permute-start | bytes 786440 | tf_op jit(solution)/shard_map/ppermute | solution.py:55
  39.3 6.3 %collective-permute-start.9 = (bf16[32,2048]{1,0:T(8,128)(2,1)S(1)}, bf16[32,2048]{1,0:T(8,128)(2,1)S(1)}, u32[]{:S(2)}, u32[]{:S(2)}) collective-permute-start(bf16[32,2048]{1,0:T(8,128)(2,1)S(1)} %slice.264), channel_id=1, source_target_pairs={{0,32},{32,64},{64,96},{96,128},{128,160},{160,192},{192,224},{224... | collective-permute-start | bytes 393224 | tf_op jit(solution)/shard_map/ppermute | solution.py:55
  39.5 6.1 %collective-permute-start.4 = (bf16[32,2048]{1,0:T(8,128)(2,1)S(1)}, bf16[32,2048]{1,0:T(8,128)(2,1)S(1)}, u32[]{:S(2)}, u32[]{:S(2)}) collective-permute-start(bf16[32,2048]{1,0:T(8,128)(2,1)S(1)} %get-tuple-element.62), channel_id=1, source_target_pairs={{0,224},{32,0},{64,32},{96,64},{128,96},{160,128},{192,160},{224,1... | collective-permute-start | bytes 393224 | tf_op jit(solution)/shard_map/ppermute | solution.py:55
  55.7 29.3 %all-to-all-start = ((f16[8,64,1792]{2,1,0:T(8,128)(2,1)}), f16[8,64,1792]{2,1,0:T(8,128)(2,1)S(1)}, u32[]{:S(2)}, u32[]{:S(2)}) async-start(f16[8,64,1792]{2,1,0:T(8,128)(2,1)} %bitcast.17), calls=%async_computation | async-start | bytes 3670016 | tf_op jit(solution)/shard_map/all_to_all | solution.py:92
  119.1 29.4 %all-to-all-start.2 = ((bf16[8,64,1792]{2,1,0:T(8,128)(2,1)}), bf16[8,64,1792]{2,1,0:T(8,128)(2,1)}, u32[]{:S(2)}, u32[]{:S(2)}) async-start(bf16[8,64,1792]{2,1,0:T(8,128)(2,1)} %broadcast_in_dim.5), calls=%async_computation.2 | async-start | bytes 3670016 | tf_op jit(solution)/shard_map/all_to_all | solution.py:92
  126.5 11.3 %collective-permute-start.13 = (bf16[64,2048]{1,0:T(8,128)(2,1)S(1)}, bf16[64,2048]{1,0:T(8,128)(2,1)S(1)}, u32[]{:S(2)}, u32[]{:S(2)}) collective-permute-start(bf16[64,2048]{1,0:T(8,128)(2,1)S(1)} %pad_maximum_fusion.4), channel_id=1, source_target_pairs={{0,224},{32,0},{64,32},{96,64},{128,96},{160,128},{192,160},{224,1... | collective-permute-start | bytes 786440 | tf_op jit(solution)/shard_map/ppermute | solution.py:55
  129.9 11.5 %collective-permute-start.12 = (bf16[64,2048]{1,0:T(8,128)(2,1)S(1)}, bf16[64,2048]{1,0:T(8,128)(2,1)S(1)}, u32[]{:S(2)}, u32[]{:S(2)}) collective-permute-start(bf16[64,2048]{1,0:T(8,128)(2,1)S(1)} %pad_maximum_fusion.3), channel_id=1, source_target_pairs={{0,32},{32,64},{64,96},{96,128},{128,160},{160,192},{192,224},{224... | collective-permute-start | bytes 786440 | tf_op jit(solution)/shard_map/ppermute | solution.py:55
  130.0 11.5 %collective-permute-start.15 = (bf16[16,2048]{1,0:T(8,128)(2,1)S(1)}, bf16[16,2048]{1,0:T(8,128)(2,1)S(1)}, u32[]{:S(2)}, u32[]{:S(2)}) collective-permute-start(bf16[16,2048]{1,0:T(8,128)(2,1)S(1)} %get-tuple-element.42), channel_id=1, source_target_pairs={{0,192},{32,224},{64,0},{96,32},{128,64},{160,96},{192,128},{224,1... | collective-permute-start | bytes 196616 | tf_op jit(solution)/shard_map/ppermute | solution.py:55
  131.6 9.9 %collective-permute-start.14 = (bf16[16,2048]{1,0:T(8,128)(2,1)S(1)}, bf16[16,2048]{1,0:T(8,128)(2,1)S(1)}, u32[]{:S(2)}, u32[]{:S(2)}) collective-permute-start(bf16[16,2048]{1,0:T(8,128)(2,1)S(1)} %get-tuple-element.43), channel_id=1, source_target_pairs={{0,64},{32,96},{64,128},{96,160},{128,192},{160,224},{192,0},{224,... | collective-permute-start | bytes 196616 | tf_op jit(solution)/shard_map/ppermute | solution.py:55
  158.7 11.3 %collective-permute-start.21 = (bf16[64,2048]{1,0:T(8,128)(2,1)S(1)}, bf16[64,2048]{1,0:T(8,128)(2,1)S(1)}, u32[]{:S(2)}, u32[]{:S(2)}) collective-permute-start(bf16[64,2048]{1,0:T(8,128)(2,1)S(1)} %pad_maximum_fusion.6), channel_id=1, source_target_pairs={{0,224},{32,0},{64,32},{96,64},{128,96},{160,128},{192,160},{224,1... | collective-permute-start | bytes 786440 | tf_op jit(solution)/shard_map/ppermute | solution.py:55
  162.1 13.3 %collective-permute-start.20 = (bf16[64,2048]{1,0:T(8,128)(2,1)S(1)}, bf16[64,2048]{1,0:T(8,128)(2,1)S(1)}, u32[]{:S(2)}, u32[]{:S(2)}) collective-permute-start(bf16[64,2048]{1,0:T(8,128)(2,1)S(1)} %pad_maximum_fusion.5), channel_id=1, source_target_pairs={{0,32},{32,64},{64,96},{96,128},{128,160},{160,192},{192,224},{224... | collective-permute-start | bytes 786440 | tf_op jit(solution)/shard_map/ppermute | solution.py:55
  162.2 13.2 %collective-permute-start.23 = (bf16[16,2048]{1,0:T(8,128)(2,1)S(1)}, bf16[16,2048]{1,0:T(8,128)(2,1)S(1)}, u32[]{:S(2)}, u32[]{:S(2)}) collective-permute-start(bf16[16,2048]{1,0:T(8,128)(2,1)S(1)} %get-tuple-element.36), channel_id=1, source_target_pairs={{0,192},{32,224},{64,0},{96,32},{128,64},{160,96},{192,128},{224,1... | collective-permute-start | bytes 196616 | tf_op jit(solution)/shard_map/ppermute | solution.py:55
  164.0 11.5 %collective-permute-start.22 = (bf16[16,2048]{1,0:T(8,128)(2,1)S(1)}, bf16[16,2048]{1,0:T(8,128)(2,1)S(1)}, u32[]{:S(2)}, u32[]{:S(2)}) collective-permute-start(bf16[16,2048]{1,0:T(8,128)(2,1)S(1)} %get-tuple-element.37), channel_id=1, source_target_pairs={{0,64},{32,96},{64,128},{96,160},{128,192},{160,224},{192,0},{224,... | collective-permute-start | bytes 196616 | tf_op jit(solution)/shard_map/ppermute | solution.py:55
  165.5 13.1 %collective-permute-start.17 = (bf16[32,2048]{1,0:T(8,128)(2,1)S(1)}, bf16[32,2048]{1,0:T(8,128)(2,1)S(1)}, u32[]{:S(2)}, u32[]{:S(2)}) collective-permute-start(bf16[32,2048]{1,0:T(8,128)(2,1)S(1)} %get-tuple-element.22), channel_id=1, source_target_pairs={{0,192},{32,224},{64,0},{96,32},{128,64},{160,96},{192,128},{224,1... | collective-permute-start | bytes 393224 | tf_op jit(solution)/shard_map/ppermute | solution.py:55
  170.0 8.5 %collective-permute-start.16 = (bf16[32,2048]{1,0:T(8,128)(2,1)S(1)}, bf16[32,2048]{1,0:T(8,128)(2,1)S(1)}, u32[]{:S(2)}, u32[]{:S(2)}) collective-permute-start(bf16[32,2048]{1,0:T(8,128)(2,1)S(1)} %get-tuple-element.21), channel_id=1, source_target_pairs={{0,64},{32,96},{64,128},{96,160},{128,192},{160,224},{192,0},{224,... | collective-permute-start | bytes 393224 | tf_op jit(solution)/shard_map/ppermute | solution.py:55
  175.6 6.3 %collective-permute-start.25 = (bf16[32,2048]{1,0:T(8,128)(2,1)S(1)}, bf16[32,2048]{1,0:T(8,128)(2,1)S(1)}, u32[]{:S(2)}, u32[]{:S(2)}) collective-permute-start(bf16[32,2048]{1,0:T(8,128)(2,1)S(1)} %get-tuple-element.25), channel_id=1, source_target_pairs={{0,192},{32,224},{64,0},{96,32},{128,64},{160,96},{192,128},{224,1... | collective-permute-start | bytes 393224 | tf_op jit(solution)/shard_map/ppermute | solution.py:55
  178.3 8.5 %collective-permute-start.24 = (bf16[32,2048]{1,0:T(8,128)(2,1)S(1)}, bf16[32,2048]{1,0:T(8,128)(2,1)S(1)}, u32[]{:S(2)}, u32[]{:S(2)}) collective-permute-start(bf16[32,2048]{1,0:T(8,128)(2,1)S(1)} %get-tuple-element.24), channel_id=1, source_target_pairs={{0,64},{32,96},{64,128},{96,160},{128,192},{160,224},{192,0},{224,... | collective-permute-start | bytes 393224 | tf_op jit(solution)/shard_map/ppermute | solution.py:55
  179.6 8.7 %collective-permute-start.18 = (bf16[16,2048]{1,0:T(8,128)(2,1)S(1)}, bf16[16,2048]{1,0:T(8,128)(2,1)S(1)}, u32[]{:S(2)}, u32[]{:S(2)}) collective-permute-start(bf16[16,2048]{1,0:T(8,128)(2,1)S(1)} %slice.383), channel_id=1, source_target_pairs={{0,16},{16,0},{1,17},{17,1},{2,18},{18,2},{3,19},{19,3},{4,20},{20... | collective-permute-start | bytes 196616 | tf_op jit(solution)/shard_map/ppermute | solution.py:51
  (9 other events, 46.8 us)

commit v2 on v1

--- a/solution.py
+++ b/solution.py
@@ -40,8 +40,7 @@
         out_shape=[jax.ShapeDtypeStruct((x.shape[0], n), t) for x, t in zip(xs, types)],
         compiler_params=pltpu.CompilerParams(vmem_limit_bytes=40 << 20),
         cost_estimate=pl.CostEstimate(
-            flops=2 * rows * depth * n,
-            bytes_accessed=2 * (w.size + rows * depth + rows * n),
+            flops=rows, bytes_accessed=rows * depth,
             transcendentals=0,
         ),
     )(*xs, w)
@@ -55,17 +54,34 @@
     return lax.ppermute(x, "z", [(i, (i - by) % NZ) for i in range(NZ)])
 
 
-def gather_z(block):
-    half = block.shape[0] // 2
-    got = {0: block}
-    for step in (1, 2, 3):
-        got[step] = shift(got[step - 1], 1)
-        got[-step] = shift(got[1 - step], -1)
-    first = [got[r][:half] for r in range(4)] + [shift(got[3][:half], 1)]
-    second = [got[r][half:] for r in range(4)] + [shift(got[-3][half:], -1)]
-    first += [got[r][:half] for r in (-3, -2, -1)]
-    second += [got[r][half:] for r in (-3, -2, -1)]
-    return jnp.concatenate(first), jnp.concatenate(second)
+def together(first, second, ready):
+    n = first.shape[0]
+
+    def body(a_ref, b_ref, _, out_ref):
+        out_ref[:n] = a_ref[...]
+        out_ref[n:] = b_ref[...]
+
+    block = pl.BlockSpec(first.shape, lambda: (0, 0))
+    return pl.pallas_call(
+        body,
+        in_specs=[block, block, pl.BlockSpec(memory_space=pl.ANY)],
+        out_specs=pl.BlockSpec((2 * n, first.shape[1]), lambda: (0, 0)),
+        out_shape=jax.ShapeDtypeStruct((2 * n, first.shape[1]), first.dtype),
+        cost_estimate=pl.CostEstimate(flops=1, bytes_accessed=6 * first.size, transcendentals=0),
+    )(first, second, ready)
+
+
+def gather_z(pair, even):
+    half = pair.shape[0] // 2
+    got = {0: pair}
+    for r in (2, -2, 1, -1):
+        got[r] = shift(pair, r)
+    got[3], got[-3] = shift(got[2], 1), shift(got[-2], -1)
+    if even:
+        got[4] = jnp.concatenate([shift(got[2][:half], 2), shift(got[-2][half:], -2)])
+    else:
+        got[4] = shift(got[-2], -2)
+    return jnp.concatenate([got[r] if r <= 4 else got[r - NZ] for r in range(NZ)])
 
 
 def scatter_rows(mine, held=None):
@@ -98,21 +114,25 @@
 
 def per_device(tokens, gate_up, down_weight, out_grad):
     width = gate_up.shape[2]
-    n = tokens.shape[0]
     weights = gate_up.reshape(gate_up.shape[0], 2 * width)
 
-    other = swap(jnp.concatenate([tokens, out_grad]), "xh")
-    tok, grad = gather_z(jnp.concatenate([tokens, other[:n], out_grad, other[n:]]))
+    tok = gather_z(together(tokens, swap(tokens, "xh"), weights), True)
     half = tok.shape[0]
     chunk = half // 4
 
+    other, tok = lax.optimization_barrier((out_grad, tok))
+    other = swap(other, "xh")
     tok = jnp.concatenate([tok, swap(tok, "core")])
     parts = (jnp.dot(tok, weights, preferred_element_type=F32) * SCALE).astype(F16)
     both = exchange(parts.reshape(8, chunk, -1))
+
+    pair, _ = lax.optimization_barrier((jnp.concatenate([out_grad, other]), parts))
+    grad = gather_z(pair, False)
     part = jnp.concatenate(
         product([grad, swap(grad, "core")], down_weight, True, (BF, BF), width)
     ).reshape(8, chunk, width)
 
+    both, part = lax.optimization_barrier((both, part))
     both = both.astype(F32).sum(0) * (1.0 / SCALE)
     gate, up = both[:, :width], both[:, width:]
     squash = jax.nn.sigmoid(gate)
@@ -127,7 +147,7 @@
     send, hidden = lax.optimization_barrier((send, hidden))
     grads = exchange(send).reshape(2 * half, 2 * width)
 
-    kept, sent = product(hidden, down_weight, False, (F32, BF), 512)
+    kept, sent = product(hidden, down_weight, False, (F32, BF), 256)
     block_out, grads = scatter_rows(kept + swap(sent, "core").astype(F32), grads)
     out = lax.dot_general(grads, weights, LAST, preferred_element_type=F32)
     out = out[:half] + swap(out[half:].astype(BF), "core").astype(F32)

time: 194 us -> 196 us (1.010)
  waiting for transfers between devices: 77.3 us -> 59.7 us
  starting transfers between devices: 51.9 us -> 62.8 us
  matrix products: 12 us -> 15.8 us
  local copies, waits for them, and re-layouts: 10.9 us -> 14.3 us
  Pallas kernels: 5.68 us -> 8.15 us
    all_to_all x2, waiting for transfers between devices: 23.1 us -> 11.4 us  [exchange(): return lax.all_to_all(x, COL, 0, 0, tiled=True)]
    ppermute x20 -> x27, starting transfers between devices: 35.6 us -> 42.7 us  [shift(): return lax.ppermute(x, 'z', [(i, (i - by) % NZ) for i in range(NZ)])]
    ppermute x20 -> x27, waiting for transfers between devices: 40.7 us -> 36.2 us  [shift(): return lax.ppermute(x, 'z', [(i, (i - by) % NZ) for i in range(NZ)])]
    dot_general x1, matrix products: 5.14 us -> 8.97 us  [per_device(): jnp.dot(tok, weights, preferred_element_type=F32) * SCALE]
    ppermute x7 -> x8, starting transfers between devices: 4.76 us -> 8.48 us  [swap(): return lax.ppermute(x, axis, SWAP)]
    unnamed x18 -> x26, local copies, waits for them, and re-layouts: 8.85 us -> 12.4 us
    ppermute x7 -> x8, waiting for transfers between devices: 13.5 us -> 12.1 us  [swap(): return lax.ppermute(x, axis, SWAP)]
  transfers between devices with their start and end apart: 29 -> 37, of which waited for: 16 -> 21; matrix products, arithmetic and copies ran while one was open for 5% -> 6% of each run, Pallas kernels for 1% -> 1%
where the time goes in v2:
time: 196 us; the launch traced here: 195 us
  starting transfers between devices  62.8 us (32%)
  waiting for transfers between devices  59.7 us (30%)
  blocking collectives  27.1 us (14%)
  matrix products  15.8 us (8%)
  local copies, waits for them, and re-layouts  14.3 us (7%)
  Pallas kernels  8.15 us (4%)
  other arithmetic  5.61 us (3%)
    ppermute x27, starting transfers between devices, shift(): return lax.ppermute(x, 'z', [(i, (i - by) % NZ) for i in range(NZ)])  42.7 us
    ppermute x27, waiting for transfers between devices, shift(): return lax.ppermute(x, 'z', [(i, (i - by) % NZ) for i in range(NZ)])  36.2 us
    all_to_all x1, blocking collectives, exchange(): return lax.all_to_all(x, COL, 0, 0, tiled=True)  27.1 us
    unnamed x26, local copies, waits for them, and re-layouts  12.4 us
    ppermute x8, waiting for transfers between devices, swap(): return lax.ppermute(x, axis, SWAP)  12.1 us
    all_to_all x2, starting transfers between devices, exchange(): return lax.all_to_all(x, COL, 0, 0, tiled=True)  11.6 us
    all_to_all x2, waiting for transfers between devices, exchange(): return lax.all_to_all(x, COL, 0, 0, tiled=True)  11.4 us
    dot_general x1, matrix products, per_device(): jnp.dot(tok, weights, preferred_element_type=F32) * SCALE  8.97 us
  transfers between devices with their start and end apart: 37, of which 21 were waited for; matrix products, arithmetic and copies ran while one was open for 6% of the time, Pallas kernels for 1%

profile of v2, /device:TPU:6, one launch (start us, length us, event | category | flops | bytes accessed | tf_op | source)
XLA Modules:
  0.0 194.6 jit_solution(5473099029194661905)
XLA Ops:
  2.1 7.5 %copy.6 = bf16[256,8,2,896]{3,1,2,0:T(8,128)(2,1)} copy(bf16[256,8,2,896]{3,2,1,0:T(2,128)(2,1)} %bitcast.15) | data formatting | bytes 14680064
  11.8 5.9 %collective-permute-start.1 = (bf16[32,2048]{1,0:T(8,128)(2,1)}, bf16[32,2048]{1,0:T(8,128)(2,1)S(1)}, u32[]{:S(2)}, u32[]{:S(2)}) collective-permute-start(bf16[32,2048]{1,0:T(8,128)(2,1)} %shard_map.59), channel_id=1, source_target_pairs={{0,224},{32,0},{64,32},{96,64},{128,96},{160,128},{192,160},{224,1... | collective-permute-start | bytes 393224 | tf_op jit(solution)/shard_map/ppermute | solution.py:54
  21.5 4.5 %collective-permute-done.2 = bf16[32,2048]{1,0:T(8,128)(2,1)S(1)} collective-permute-done((bf16[32,2048]{1,0:T(8,128)(2,1)}, bf16[32,2048]{1,0:T(8,128)(2,1)S(1)}, u32[]{:S(2)}, u32[]{:S(2)}) %collective-permute-start.2) | collective-permute-done | bytes 131104 | tf_op jit(solution)/shard_map/ppermute | solution.py:54
  26.1 4.5 %collective-permute-start.4 = (bf16[16,2048]{1,0:T(8,128)(2,1)S(1)}, bf16[16,2048]{1,0:T(8,128)(2,1)S(1)}, u32[]{:S(2)}, u32[]{:S(2)}) collective-permute-start(bf16[16,2048]{1,0:T(8,128)(2,1)S(1)} %slice.197), channel_id=1, source_target_pairs={{0,192},{32,224},{64,0},{96,32},{128,64},{160,96},{192,128},{224,1... | collective-permute-start | bytes 196616 | tf_op jit(solution)/shard_map/ppermute | solution.py:54
  30.7 2.9 %collective-permute-start.3 = (bf16[32,2048]{1,0:T(8,128)(2,1)S(1)}, bf16[32,2048]{1,0:T(8,128)(2,1)S(1)}, u32[]{:S(2)}, u32[]{:S(2)}) collective-permute-start(bf16[32,2048]{1,0:T(8,128)(2,1)S(1)} %collective-permute-done.2), channel_id=1, source_target_pairs={{0,224},{32,0},{64,32},{96,64},{128,96},{160,128},{192,160},{224,1... | collective-permute-start | bytes 393224 | tf_op jit(solution)/shard_map/ppermute | solution.py:54
  37.1 2.8 %collective-permute-done.7 = bf16[32,2048]{1,0:T(8,128)(2,1)S(1)} collective-permute-done((bf16[32,2048]{1,0:T(8,128)(2,1)S(1)}, bf16[32,2048]{1,0:T(8,128)(2,1)S(1)}, u32[]{:S(2)}, u32[]{:S(2)}) %collective-permute-start.7) | collective-permute-done | bytes 131104 | tf_op jit(solution)/shard_map/ppermute | solution.py:54
  42.2 3.8 %collective-permute-done.10 = bf16[16,2048]{1,0:T(8,128)(2,1)S(1)} collective-permute-done((bf16[16,2048]{1,0:T(8,128)(2,1)S(1)}, bf16[16,2048]{1,0:T(8,128)(2,1)S(1)}, u32[]{:S(2)}, u32[]{:S(2)}) %collective-permute-start.10) | collective-permute-done | bytes 65568 | tf_op jit(solution)/shard_map/ppermute | solution.py:50
  46.1 9.0 %multiply_convert_fusion = f16[512,1792]{1,0:T(8,128)(2,1)} fusion(bf16[2048,1792]{1,0:T(8,128)(2,1)} %bitcast.13, bf16[256,2048]{1,0:T(8,128)(2,1)S(1)} %collective-permute-done.9, bf16[256,2048]{1,0:T(8,128)(2,1)S(1)} %constant_dynamic-update-slice_fusion), kind=kOutput, calls=%fused_computation.1 | convolution fusion | flops 3764125696 | bytes 11272192 | tf_op jit(solution)/shard_map/dot_general | solution.py:126
  55.6 2.9 %collective-permute-start.14 = (bf16[32,2048]{1,0:T(8,128)(2,1)S(1)}, bf16[32,2048]{1,0:T(8,128)(2,1)S(1)}, u32[]{:S(2)}, u32[]{:S(2)}) collective-permute-start(bf16[32,2048]{1,0:T(8,128)(2,1)S(1)} %pad_maximum_fusion.7), channel_id=1, source_target_pairs={{0,64},{32,96},{64,128},{96,160},{128,192},{160,224},{192,0},{224,... | collective-permute-start | bytes 393224 | tf_op jit(solution)/shard_map/ppermute | solution.py:54
  60.0 5.9 %all-to-all-start = ((f16[8,64,1792]{2,1,0:T(8,128)(2,1)}), f16[8,64,1792]{2,1,0:T(8,128)(2,1)S(1)}, u32[]{:S(2)}, u32[]{:S(2)}) async-start(f16[8,64,1792]{2,1,0:T(8,128)(2,1)} %bitcast.17), calls=%async_computation | async-start | bytes 3670016 | tf_op jit(solution)/shard_map/all_to_all | solution.py:108
  68.4 3.2 %collective-permute-start.13 = (bf16[32,2048]{1,0:T(8,128)(2,1)S(1)}, bf16[32,2048]{1,0:T(8,128)(2,1)S(1)}, u32[]{:S(2)}, u32[]{:S(2)}) collective-permute-start(bf16[32,2048]{1,0:T(8,128)(2,1)S(1)} %collective-permute-done.12), channel_id=1, source_target_pairs={{0,224},{32,0},{64,32},{96,64},{128,96},{160,128},{192,160},{224,1... | collective-permute-start | bytes 393224 | tf_op jit(solution)/shard_map/ppermute | solution.py:54
  84.4 2.9 %all-to-all-done = f16[8,64,1792]{2,1,0:T(8,128)(2,1)S(1)} async-done(((f16[8,64,1792]{2,1,0:T(8,128)(2,1)}), f16[8,64,1792]{2,1,0:T(8,128)(2,1)S(1)}, u32[]{:S(2)}, u32[]{:S(2)}) %all-to-all-start) | async-done | bytes 1835040 | tf_op jit(solution)/shard_map/all_to_all | solution.py:108
  87.9 27.1 %all_to_all.15 = bf16[8,128,896]{2,1,0:T(8,128)(2,1)S(1)} all-to-all(bf16[8,128,896]{2,1,0:T(8,128)(2,1)S(1)} %pad_maximum_fusion), channel_id=1, replica_groups=mesh['z'=8,'xh'=2,'core'=2,'xl'=2,'y'=4] {'xl','y'}, dimensions={0} | all-to-all | bytes 3670016 | tf_op jit(solution)/shard_map/all_to_all | solution.py:108
  118.0 4.3 %shard_map.61 = (f32[256,2048]{1,0:T(8,128)S(1)}, bf16[256,2048]{1,0:T(8,128)(2,1)S(1)}) custom-call(bf16[256,896]{1,0:T(8,128)(2,1)S(1)} %bitcast.11, bf16[256,896]{1,0:T(8,128)(2,1)S(1)} %bitcast.10, bf16[896,2048]{1,0:T(8,128)(2,1)S(1)} %copy-done.1), custom_call_target="tpu_custom_call" | custom-call | flops 512 | bytes 458752 | tf_op jit(solution)/shard_map/pallas_call | solution.py:35
  122.4 5.7 %all-to-all-start.2 = ((bf16[8,64,1792]{2,1,0:T(8,128)(2,1)}), bf16[8,64,1792]{2,1,0:T(8,128)(2,1)}, u32[]{:S(2)}, u32[]{:S(2)}) async-start(bf16[8,64,1792]{2,1,0:T(8,128)(2,1)} %broadcast_in_dim.5), calls=%async_computation.2 | async-start | bytes 3670016 | tf_op jit(solution)/shard_map/all_to_all | solution.py:108
  135.1 4.2 %collective-permute-done.21 = bf16[64,2048]{1,0:T(8,128)(2,1)S(1)} collective-permute-done((bf16[64,2048]{1,0:T(8,128)(2,1)S(1)}, bf16[64,2048]{1,0:T(8,128)(2,1)S(1)}, u32[]{:S(2)}, u32[]{:S(2)}) %collective-permute-start.21) | collective-permute-done | bytes 262176 | tf_op jit(solution)/shard_map/ppermute | solution.py:54
  139.3 3.7 %collective-permute-done.20 = bf16[64,2048]{1,0:T(8,128)(2,1)S(1)} collective-permute-done((bf16[64,2048]{1,0:T(8,128)(2,1)S(1)}, bf16[64,2048]{1,0:T(8,128)(2,1)S(1)}, u32[]{:S(2)}, u32[]{:S(2)}) %collective-permute-start.20) | collective-permute-done | bytes 262176 | tf_op jit(solution)/shard_map/ppermute | solution.py:54
  143.2 8.5 %all-to-all-done.2 = bf16[8,64,1792]{2,1,0:T(8,128)(2,1)} async-done(((bf16[8,64,1792]{2,1,0:T(8,128)(2,1)}), bf16[8,64,1792]{2,1,0:T(8,128)(2,1)}, u32[]{:S(2)}, u32[]{:S(2)}) %all-to-all-start.2) | async-done | bytes 1835040 | tf_op jit(solution)/shard_map/all_to_all | solution.py:108
  151.7 6.8 %fusion.25 = f32[512,2048]{1,0:T(8,128)S(1)} fusion(bf16[512,1792]{1,0:T(8,128)(2,1)} %bitcast.4, bf16[2048,1792]{1,0:T(8,128)(2,1)} %bitcast.14), kind=kOutput, calls=%fused_computation.73 | convolution fusion | flops 3758096384 | bytes 13369344 | tf_op jit(solution)/shard_map/dot_general | solution.py:152
  169.8 3.2 %collective-permute-done.29 = bf16[64,2048]{1,0:T(8,128)(2,1)S(1)} collective-permute-done((bf16[64,2048]{1,0:T(8,128)(2,1)S(1)}, bf16[64,2048]{1,0:T(8,128)(2,1)S(1)}, u32[]{:S(2)}, u32[]{:S(2)}) %collective-permute-start.29) | collective-permute-done | bytes 262176 | tf_op jit(solution)/shard_map/ppermute | solution.py:54
  173.1 4.0 %collective-permute-done.28 = bf16[64,2048]{1,0:T(8,128)(2,1)S(1)} collective-permute-done((bf16[64,2048]{1,0:T(8,128)(2,1)S(1)}, bf16[64,2048]{1,0:T(8,128)(2,1)S(1)}, u32[]{:S(2)}, u32[]{:S(2)}) %collective-permute-start.28) | collective-permute-done | bytes 262176 | tf_op jit(solution)/shard_map/ppermute | solution.py:54
  177.2 3.1 %collective-permute-start.33 = (bf16[32,2048]{1,0:T(8,128)(2,1)S(1)}, bf16[32,2048]{1,0:T(8,128)(2,1)S(1)}, u32[]{:S(2)}, u32[]{:S(2)}) collective-permute-start(bf16[32,2048]{1,0:T(8,128)(2,1)S(1)} %get-tuple-element.35), channel_id=1, source_target_pairs={{0,192},{32,224},{64,0},{96,32},{128,64},{160,96},{192,128},{224,1... | collective-permute-start | bytes 393224 | tf_op jit(solution)/shard_map/ppermute | solution.py:54
  184.5 3.4 %collective-permute-done.32 = bf16[32,2048]{1,0:T(8,128)(2,1)S(1)} collective-permute-done((bf16[32,2048]{1,0:T(8,128)(2,1)S(1)}, bf16[32,2048]{1,0:T(8,128)(2,1)S(1)}, u32[]{:S(2)}, u32[]{:S(2)}) %collective-permute-start.32) | collective-permute-done | bytes 131104 | tf_op jit(solution)/shard_map/ppermute | solution.py:54
  190.9 3.0 %collective-permute-done.34 = bf16[16,2048]{1,0:T(8,128)(2,1)S(1)} collective-permute-done((bf16[16,2048]{1,0:T(8,128)(2,1)S(1)}, bf16[16,2048]{1,0:T(8,128)(2,1)S(1)}, u32[]{:S(2)}, u32[]{:S(2)}) %collective-permute-start.34) | collective-permute-done | bytes 65568 | tf_op jit(solution)/shard_map/ppermute | solution.py:50
  (121 shorter events, 60.7 us)
Async XLA Ops:
  0.6 9.0 %collective-permute-start = (bf16[16,2048]{1,0:T(8,128)(2,1)}, bf16[16,2048]{1,0:T(8,128)(2,1)S(1)}, u32[]{:S(2)}, u32[]{:S(2)}) collective-permute-start(bf16[16,2048]{1,0:T(8,128)(2,1)} %a_ref.1), channel_id=1, source_target_pairs={{0,16},{16,0},{1,17},{17,1},{2,18},{18,2},{3,19},{19,3},{4,20},{20... | collective-permute-start | bytes 196616 | tf_op jit(solution)/shard_map/ppermute | solution.py:50
  11.8 21.9 %collective-permute-start.1 = (bf16[32,2048]{1,0:T(8,128)(2,1)}, bf16[32,2048]{1,0:T(8,128)(2,1)S(1)}, u32[]{:S(2)}, u32[]{:S(2)}) collective-permute-start(bf16[32,2048]{1,0:T(8,128)(2,1)} %shard_map.59), channel_id=1, source_target_pairs={{0,224},{32,0},{64,32},{96,64},{128,96},{160,128},{192,160},{224,1... | collective-permute-start | bytes 393224 | tf_op jit(solution)/shard_map/ppermute | solution.py:54
  17.6 8.4 %collective-permute-start.2 = (bf16[32,2048]{1,0:T(8,128)(2,1)}, bf16[32,2048]{1,0:T(8,128)(2,1)S(1)}, u32[]{:S(2)}, u32[]{:S(2)}) collective-permute-start(bf16[32,2048]{1,0:T(8,128)(2,1)} %shard_map.59), channel_id=1, source_target_pairs={{0,192},{32,224},{64,0},{96,32},{128,64},{160,96},{192,128},{224,1... | collective-permute-start | bytes 393224 | tf_op jit(solution)/shard_map/ppermute | solution.py:54
  19.1 11.5 %collective-permute-start.5 = (bf16[32,2048]{1,0:T(8,128)(2,1)}, bf16[32,2048]{1,0:T(8,128)(2,1)S(1)}, u32[]{:S(2)}, u32[]{:S(2)}) collective-permute-start(bf16[32,2048]{1,0:T(8,128)(2,1)} %shard_map.59), channel_id=1, source_target_pairs={{0,64},{32,96},{64,128},{96,160},{128,192},{160,224},{192,0},{224,... | collective-permute-start | bytes 393224 | tf_op jit(solution)/shard_map/ppermute | solution.py:54
  20.6 19.3 %collective-permute-start.8 = (bf16[32,2048]{1,0:T(8,128)(2,1)}, bf16[32,2048]{1,0:T(8,128)(2,1)S(1)}, u32[]{:S(2)}, u32[]{:S(2)}) collective-permute-start(bf16[32,2048]{1,0:T(8,128)(2,1)} %shard_map.59), channel_id=1, source_target_pairs={{0,32},{32,64},{64,96},{96,128},{128,160},{160,192},{192,224},{224... | collective-permute-start | bytes 393224 | tf_op jit(solution)/shard_map/ppermute | solution.py:54
  26.1 10.1 %collective-permute-start.4 = (bf16[16,2048]{1,0:T(8,128)(2,1)S(1)}, bf16[16,2048]{1,0:T(8,128)(2,1)S(1)}, u32[]{:S(2)}, u32[]{:S(2)}) collective-permute-start(bf16[16,2048]{1,0:T(8,128)(2,1)S(1)} %slice.197), channel_id=1, source_target_pairs={{0,192},{32,224},{64,0},{96,32},{128,64},{160,96},{192,128},{224,1... | collective-permute-start | bytes 196616 | tf_op jit(solution)/shard_map/ppermute | solution.py:54
  55.0 16.6 %collective-permute-start.11 = (bf16[32,2048]{1,0:T(8,128)(2,1)S(1)}, bf16[32,2048]{1,0:T(8,128)(2,1)S(1)}, u32[]{:S(2)}, u32[]{:S(2)}) collective-permute-start(bf16[32,2048]{1,0:T(8,128)(2,1)S(1)} %pad_maximum_fusion.7), channel_id=1, source_target_pairs={{0,224},{32,0},{64,32},{96,64},{128,96},{160,128},{192,160},{224,1... | collective-permute-start | bytes 393224 | tf_op jit(solution)/shard_map/ppermute | solution.py:54
  55.6 12.9 %collective-permute-start.12 = (bf16[32,2048]{1,0:T(8,128)(2,1)S(1)}, bf16[32,2048]{1,0:T(8,128)(2,1)S(1)}, u32[]{:S(2)}, u32[]{:S(2)}) collective-permute-start(bf16[32,2048]{1,0:T(8,128)(2,1)S(1)} %pad_maximum_fusion.7), channel_id=1, source_target_pairs={{0,192},{32,224},{64,0},{96,32},{128,64},{160,96},{192,128},{224,1... | collective-permute-start | bytes 393224 | tf_op jit(solution)/shard_map/ppermute | solution.py:54
  55.6 11.1 %collective-permute-start.14 = (bf16[32,2048]{1,0:T(8,128)(2,1)S(1)}, bf16[32,2048]{1,0:T(8,128)(2,1)S(1)}, u32[]{:S(2)}, u32[]{:S(2)}) collective-permute-start(bf16[32,2048]{1,0:T(8,128)(2,1)S(1)} %pad_maximum_fusion.7), channel_id=1, source_target_pairs={{0,64},{32,96},{64,128},{96,160},{128,192},{160,224},{192,0},{224,... | collective-permute-start | bytes 393224 | tf_op jit(solution)/shard_map/ppermute | solution.py:54
  58.5 18.7 %collective-permute-start.17 = (bf16[32,2048]{1,0:T(8,128)(2,1)S(1)}, bf16[32,2048]{1,0:T(8,128)(2,1)S(1)}, u32[]{:S(2)}, u32[]{:S(2)}) collective-permute-start(bf16[32,2048]{1,0:T(8,128)(2,1)S(1)} %pad_maximum_fusion.7), channel_id=1, source_target_pairs={{0,32},{32,64},{64,96},{96,128},{128,160},{160,192},{192,224},{224... | collective-permute-start | bytes 393224 | tf_op jit(solution)/shard_map/ppermute | solution.py:54
  60.0 27.3 %all-to-all-start = ((f16[8,64,1792]{2,1,0:T(8,128)(2,1)}), f16[8,64,1792]{2,1,0:T(8,128)(2,1)S(1)}, u32[]{:S(2)}, u32[]{:S(2)}) async-start(f16[8,64,1792]{2,1,0:T(8,128)(2,1)} %bitcast.17), calls=%async_computation | async-start | bytes 3670016 | tf_op jit(solution)/shard_map/all_to_all | solution.py:108
  66.7 9.0 %collective-permute-start.15 = (bf16[32,2048]{1,0:T(8,128)(2,1)S(1)}, bf16[32,2048]{1,0:T(8,128)(2,1)S(1)}, u32[]{:S(2)}, u32[]{:S(2)}) collective-permute-start(bf16[32,2048]{1,0:T(8,128)(2,1)S(1)} %collective-permute-done.14), channel_id=1, source_target_pairs={{0,64},{32,96},{64,128},{96,160},{128,192},{160,224},{192,0},{224,... | collective-permute-start | bytes 393224 | tf_op jit(solution)/shard_map/ppermute | solution.py:54
  68.4 8.7 %collective-permute-start.16 = (bf16[32,2048]{1,0:T(8,128)(2,1)S(1)}, bf16[32,2048]{1,0:T(8,128)(2,1)S(1)}, u32[]{:S(2)}, u32[]{:S(2)}) collective-permute-start(bf16[32,2048]{1,0:T(8,128)(2,1)S(1)} %collective-permute-done.14), channel_id=1, source_target_pairs={{0,32},{32,64},{64,96},{96,128},{128,160},{160,192},{192,224},{224... | collective-permute-start | bytes 393224 | tf_op jit(solution)/shard_map/ppermute | solution.py:54
  122.4 29.4 %all-to-all-start.2 = ((bf16[8,64,1792]{2,1,0:T(8,128)(2,1)}), bf16[8,64,1792]{2,1,0:T(8,128)(2,1)}, u32[]{:S(2)}, u32[]{:S(2)}) async-start(bf16[8,64,1792]{2,1,0:T(8,128)(2,1)} %broadcast_in_dim.5), calls=%async_computation.2 | async-start | bytes 3670016 | tf_op jit(solution)/shard_map/all_to_all | solution.py:108
  129.7 9.6 %collective-permute-start.21 = (bf16[64,2048]{1,0:T(8,128)(2,1)S(1)}, bf16[64,2048]{1,0:T(8,128)(2,1)S(1)}, u32[]{:S(2)}, u32[]{:S(2)}) collective-permute-start(bf16[64,2048]{1,0:T(8,128)(2,1)S(1)} %pad_maximum_fusion.3), channel_id=1, source_target_pairs={{0,224},{32,0},{64,32},{96,64},{128,96},{160,128},{192,160},{224,1... | collective-permute-start | bytes 786440 | tf_op jit(solution)/shard_map/ppermute | solution.py:54
  131.5 11.5 %collective-permute-start.20 = (bf16[64,2048]{1,0:T(8,128)(2,1)S(1)}, bf16[64,2048]{1,0:T(8,128)(2,1)S(1)}, u32[]{:S(2)}, u32[]{:S(2)}) collective-permute-start(bf16[64,2048]{1,0:T(8,128)(2,1)S(1)} %pad_maximum_fusion.2), channel_id=1, source_target_pairs={{0,32},{32,64},{64,96},{96,128},{128,160},{160,192},{192,224},{224... | collective-permute-start | bytes 786440 | tf_op jit(solution)/shard_map/ppermute | solution.py:54
  131.9 11.2 %collective-permute-start.23 = (bf16[16,2048]{1,0:T(8,128)(2,1)S(1)}, bf16[16,2048]{1,0:T(8,128)(2,1)S(1)}, u32[]{:S(2)}, u32[]{:S(2)}) collective-permute-start(bf16[16,2048]{1,0:T(8,128)(2,1)S(1)} %get-tuple-element.52), channel_id=1, source_target_pairs={{0,192},{32,224},{64,0},{96,32},{128,64},{160,96},{192,128},{224,1... | collective-permute-start | bytes 196616 | tf_op jit(solution)/shard_map/ppermute | solution.py:54
  133.7 9.4 %collective-permute-start.22 = (bf16[16,2048]{1,0:T(8,128)(2,1)S(1)}, bf16[16,2048]{1,0:T(8,128)(2,1)S(1)}, u32[]{:S(2)}, u32[]{:S(2)}) collective-permute-start(bf16[16,2048]{1,0:T(8,128)(2,1)S(1)} %get-tuple-element.53), channel_id=1, source_target_pairs={{0,64},{32,96},{64,128},{96,160},{128,192},{160,224},{192,0},{224,... | collective-permute-start | bytes 196616 | tf_op jit(solution)/shard_map/ppermute | solution.py:54
  161.9 11.1 %collective-permute-start.29 = (bf16[64,2048]{1,0:T(8,128)(2,1)S(1)}, bf16[64,2048]{1,0:T(8,128)(2,1)S(1)}, u32[]{:S(2)}, u32[]{:S(2)}) collective-permute-start(bf16[64,2048]{1,0:T(8,128)(2,1)S(1)} %pad_maximum_fusion.5), channel_id=1, source_target_pairs={{0,224},{32,0},{64,32},{96,64},{128,96},{160,128},{192,160},{224,1... | collective-permute-start | bytes 786440 | tf_op jit(solution)/shard_map/ppermute | solution.py:54
  163.7 13.3 %collective-permute-start.28 = (bf16[64,2048]{1,0:T(8,128)(2,1)S(1)}, bf16[64,2048]{1,0:T(8,128)(2,1)S(1)}, u32[]{:S(2)}, u32[]{:S(2)}) collective-permute-start(bf16[64,2048]{1,0:T(8,128)(2,1)S(1)} %pad_maximum_fusion.4), channel_id=1, source_target_pairs={{0,32},{32,64},{64,96},{96,128},{128,160},{160,192},{192,224},{224... | collective-permute-start | bytes 786440 | tf_op jit(solution)/shard_map/ppermute | solution.py:54
  164.1 13.0 %collective-permute-start.31 = (bf16[16,2048]{1,0:T(8,128)(2,1)S(1)}, bf16[16,2048]{1,0:T(8,128)(2,1)S(1)}, u32[]{:S(2)}, u32[]{:S(2)}) collective-permute-start(bf16[16,2048]{1,0:T(8,128)(2,1)S(1)} %get-tuple-element.46), channel_id=1, source_target_pairs={{0,192},{32,224},{64,0},{96,32},{128,64},{160,96},{192,128},{224,1... | collective-permute-start | bytes 196616 | tf_op jit(solution)/shard_map/ppermute | solution.py:54
  165.7 11.4 %collective-permute-start.30 = (bf16[16,2048]{1,0:T(8,128)(2,1)S(1)}, bf16[16,2048]{1,0:T(8,128)(2,1)S(1)}, u32[]{:S(2)}, u32[]{:S(2)}) collective-permute-start(bf16[16,2048]{1,0:T(8,128)(2,1)S(1)} %get-tuple-element.47), channel_id=1, source_target_pairs={{0,64},{32,96},{64,128},{96,160},{128,192},{160,224},{192,0},{224,... | collective-permute-start | bytes 196616 | tf_op jit(solution)/shard_map/ppermute | solution.py:54
  167.1 13.2 %collective-permute-start.25 = (bf16[32,2048]{1,0:T(8,128)(2,1)S(1)}, bf16[32,2048]{1,0:T(8,128)(2,1)S(1)}, u32[]{:S(2)}, u32[]{:S(2)}) collective-permute-start(bf16[32,2048]{1,0:T(8,128)(2,1)S(1)} %get-tuple-element.32), channel_id=1, source_target_pairs={{0,192},{32,224},{64,0},{96,32},{128,64},{160,96},{192,128},{224,1... | collective-permute-start | bytes 393224 | tf_op jit(solution)/shard_map/ppermute | solution.py:54
  181.9 8.3 %collective-permute-start.26 = (bf16[16,2048]{1,0:T(8,128)(2,1)S(1)}, bf16[16,2048]{1,0:T(8,128)(2,1)S(1)}, u32[]{:S(2)}, u32[]{:S(2)}) collective-permute-start(bf16[16,2048]{1,0:T(8,128)(2,1)S(1)} %slice.296), channel_id=1, source_target_pairs={{0,16},{16,0},{1,17},{17,1},{2,18},{18,2},{3,19},{19,3},{4,20},{20... | collective-permute-start | bytes 196616 | tf_op jit(solution)/shard_map/ppermute | solution.py:50
  (18 other events, 123.1 us)

commit v3 on v2

--- a/solution.py
+++ b/solution.py
@@ -54,23 +54,6 @@
     return lax.ppermute(x, "z", [(i, (i - by) % NZ) for i in range(NZ)])
 
 
-def together(first, second, ready):
-    n = first.shape[0]
-
-    def body(a_ref, b_ref, _, out_ref):
-        out_ref[:n] = a_ref[...]
-        out_ref[n:] = b_ref[...]
-
-    block = pl.BlockSpec(first.shape, lambda: (0, 0))
-    return pl.pallas_call(
-        body,
-        in_specs=[block, block, pl.BlockSpec(memory_space=pl.ANY)],
-        out_specs=pl.BlockSpec((2 * n, first.shape[1]), lambda: (0, 0)),
-        out_shape=jax.ShapeDtypeStruct((2 * n, first.shape[1]), first.dtype),
-        cost_estimate=pl.CostEstimate(flops=1, bytes_accessed=6 * first.size, transcendentals=0),
-    )(first, second, ready)
-
-
 def gather_z(pair, even):
     half = pair.shape[0] // 2
     got = {0: pair}
@@ -84,7 +67,7 @@
     return jnp.concatenate([got[r] if r <= 4 else got[r - NZ] for r in range(NZ)])
 
 
-def scatter_rows(mine, held=None):
+def first_round(mine):
     block = mine.reshape(NZ, mine.shape[0] // NZ, -1)
     rows = block.shape[1] // 2
     total = block[0]
@@ -98,10 +81,17 @@
         zero = jnp.zeros_like(far)
         relayed = jnp.concatenate([far, zero] if way == 1 else [zero, far])
         seconds.append((block[2 * way % NZ] + near[2 * rows :] + relayed).astype(BF))
-    seconds, held = lax.optimization_barrier((seconds, held))
-    for way, second in zip((1, -1), seconds):
-        total = total + shift(second, -2 * way).astype(F32)
-    return (total[:rows] + swap(total[rows:].astype(BF), "xh").astype(F32)).astype(BF), held
+    return total, seconds
+
+
+def second_round(seconds):
+    return [shift(second, -2 * way) for way, second in zip((1, -1), seconds)]
+
+
+def last_round(total, seconds):
+    total = total + seconds[0].astype(F32) + seconds[1].astype(F32)
+    rows = total.shape[0] // 2
+    return (total[:rows] + swap(total[rows:].astype(BF), "xh").astype(F32)).astype(BF)
 
 
 def exchange(x):
@@ -116,17 +106,17 @@
     width = gate_up.shape[2]
     weights = gate_up.reshape(gate_up.shape[0], 2 * width)
 
-    tok = gather_z(together(tokens, swap(tokens, "xh"), weights), True)
+    n = tokens.shape[0]
+    other = swap(jnp.concatenate([tokens, out_grad]), "xh")
+    tok = gather_z(jnp.concatenate([tokens, other[:n]]), True)
     half = tok.shape[0]
     chunk = half // 4
 
-    other, tok = lax.optimization_barrier((out_grad, tok))
-    other = swap(other, "xh")
     tok = jnp.concatenate([tok, swap(tok, "core")])
     parts = (jnp.dot(tok, weights, preferred_element_type=F32) * SCALE).astype(F16)
     both = exchange(parts.reshape(8, chunk, -1))
 
-    pair, _ = lax.optimization_barrier((jnp.concatenate([out_grad, other]), parts))
+    pair, _ = lax.optimization_barrier((jnp.concatenate([out_grad, other[n:]]), parts))
     grad = gather_z(pair, False)
     part = jnp.concatenate(
         product([grad, swap(grad, "core")], down_weight, True, (BF, BF), width)
@@ -147,12 +137,16 @@
     send, hidden = lax.optimization_barrier((send, hidden))
     grads = exchange(send).reshape(2 * half, 2 * width)
 
-    kept, sent = product(hidden, down_weight, False, (F32, BF), 256)
-    block_out, grads = scatter_rows(kept + swap(sent, "core").astype(F32), grads)
+    kept, sent = product(hidden, down_weight, False, (F32, BF), 512)
+    total, seconds = first_round(kept + swap(sent, "core").astype(F32))
+    seconds, grads = lax.optimization_barrier((seconds, grads))
+    seconds = second_round(seconds)
     out = lax.dot_general(grads, weights, LAST, preferred_element_type=F32)
-    out = out[:half] + swap(out[half:].astype(BF), "core").astype(F32)
-    grad_tokens, _ = scatter_rows(out)
-    return block_out, grad_tokens
+    come = swap(out[half:].astype(BF), "core")
+    seconds, come = lax.optimization_barrier((seconds, come))
+    block_out = last_round(total, seconds)
+    total, seconds = first_round(out[:half] + come.astype(F32))
+    return block_out, last_round(total, second_round(seconds))
 
 
 def solution(mesh):

time: 196 us -> 191 us (0.974)
  matrix products: 15.8 us -> 11.9 us
  local copies, waits for them, and re-layouts: 14.3 us -> 10.9 us
  Pallas kernels: 8.15 us -> 5.68 us
  waiting for transfers between devices: 59.7 us -> 62.1 us
    ppermute x27, starting transfers between devices: 42.7 us -> 47.7 us  [shift(): return lax.ppermute(x, 'z', [(i, (i - by) % NZ) for i in range(NZ)])]
    dot_general x1, matrix products: 8.97 us -> 5.09 us  [per_device(): jnp.dot(tok, weights, preferred_element_type=F32) * SCALE]
    ppermute x27, waiting for transfers between devices: 36.2 us -> 40 us  [shift(): return lax.ppermute(x, 'z', [(i, (i - by) % NZ) for i in range(NZ)])]
    ppermute x8 -> x7, starting transfers between devices: 8.48 us -> 4.84 us  [swap(): return lax.ppermute(x, axis, SWAP)]
    unnamed x26, local copies, waits for them, and re-layouts: 12.4 us -> 8.83 us
    ppermute x8 -> x7, waiting for transfers between devices: 12.1 us -> 10.9 us  [swap(): return lax.ppermute(x, axis, SWAP)]
  transfers between devices with their start and end apart: 37 -> 36, of which waited for: 21 -> 20; matrix products, arithmetic and copies ran while one was open for 6% -> 5% of each run, Pallas kernels for 1% -> 1%
where the time goes in v3:
time: 191 us; the launch traced here: 190 us
  starting transfers between devices  64.2 us (34%)
  waiting for transfers between devices  62.1 us (33%)
  blocking collectives  27.1 us (14%)
  matrix products  11.9 us (6%)
  local copies, waits for them, and re-layouts  10.9 us (6%)
  other arithmetic  7.37 us (4%)
  Pallas kernels  5.68 us (3%)
    ppermute x27, starting transfers between devices, shift(): return lax.ppermute(x, 'z', [(i, (i - by) % NZ) for i in range(NZ)])  47.7 us
    ppermute x27, waiting for transfers between devices, shift(): return lax.ppermute(x, 'z', [(i, (i - by) % NZ) for i in range(NZ)])  40 us
    all_to_all x1, blocking collectives, exchange(): return lax.all_to_all(x, COL, 0, 0, tiled=True)  27.1 us
    all_to_all x2, starting transfers between devices, exchange(): return lax.all_to_all(x, COL, 0, 0, tiled=True)  11.6 us
    all_to_all x2, waiting for transfers between devices, exchange(): return lax.all_to_all(x, COL, 0, 0, tiled=True)  11.1 us
    ppermute x7, waiting for transfers between devices, swap(): return lax.ppermute(x, axis, SWAP)  10.9 us
    unnamed x26, local copies, waits for them, and re-layouts  8.83 us
    dot_general x1, matrix products, per_device(): out = lax.dot_general(grads, weights, LAST, preferred_element_type=F32)  6.82 us
  transfers between devices with their start and end apart: 36, of which 20 were waited for; matrix products, arithmetic and copies ran while one was open for 5% of the time, Pallas kernels for 1%

profile of v3, /device:TPU:6, one launch (start us, length us, event | category | flops | bytes accessed | tf_op | source)
XLA Modules:
  0.0 190.3 jit_solution(6933811930211743659)
XLA Ops:
  3.9 4.5 %collective-permute-done = bf16[32,2048]{1,0:T(8,128)(2,1)S(1)} collective-permute-done((bf16[32,2048]{1,0:T(8,128)(2,1)S(1)}, bf16[32,2048]{1,0:T(8,128)(2,1)S(1)}, u32[]{:S(2)}, u32[]{:S(2)}) %collective-permute-start) | collective-permute-done | bytes 131104 | tf_op jit(solution)/shard_map/ppermute | solution.py:50
  9.2 6.4 %collective-permute-start.2 = (bf16[32,2048]{1,0:T(8,128)(2,1)S(1)}, bf16[32,2048]{1,0:T(8,128)(2,1)S(1)}, u32[]{:S(2)}, u32[]{:S(2)}) collective-permute-start(bf16[32,2048]{1,0:T(8,128)(2,1)S(1)} %pad_maximum_fusion.7), channel_id=1, source_target_pairs={{0,192},{32,224},{64,0},{96,32},{128,64},{160,96},{192,128},{224,1... | collective-permute-start | bytes 393224 | tf_op jit(solution)/shard_map/ppermute | solution.py:54
  15.6 3.7 %collective-permute-start.1 = (bf16[32,2048]{1,0:T(8,128)(2,1)S(1)}, bf16[32,2048]{1,0:T(8,128)(2,1)S(1)}, u32[]{:S(2)}, u32[]{:S(2)}) collective-permute-start(bf16[32,2048]{1,0:T(8,128)(2,1)S(1)} %pad_maximum_fusion.7), channel_id=1, source_target_pairs={{0,224},{32,0},{64,32},{96,64},{128,96},{160,128},{192,160},{224,1... | collective-permute-start | bytes 393224 | tf_op jit(solution)/shard_map/ppermute | solution.py:54
  21.5 4.6 %collective-permute-start.4 = (bf16[16,2048]{1,0:T(8,128)(2,1)S(1)}, bf16[16,2048]{1,0:T(8,128)(2,1)S(1)}, u32[]{:S(2)}, u32[]{:S(2)}) collective-permute-start(bf16[16,2048]{1,0:T(8,128)(2,1)S(1)} %slice.206), channel_id=1, source_target_pairs={{0,192},{32,224},{64,0},{96,32},{128,64},{160,96},{192,128},{224,1... | collective-permute-start | bytes 196616 | tf_op jit(solution)/shard_map/ppermute | solution.py:54
  26.2 3.4 %collective-permute-start.3 = (bf16[32,2048]{1,0:T(8,128)(2,1)S(1)}, bf16[32,2048]{1,0:T(8,128)(2,1)S(1)}, u32[]{:S(2)}, u32[]{:S(2)}) collective-permute-start(bf16[32,2048]{1,0:T(8,128)(2,1)S(1)} %collective-permute-done.2), channel_id=1, source_target_pairs={{0,224},{32,0},{64,32},{96,64},{128,96},{160,128},{192,160},{224,1... | collective-permute-start | bytes 393224 | tf_op jit(solution)/shard_map/ppermute | solution.py:54
  32.6 3.2 %collective-permute-done.7 = bf16[32,2048]{1,0:T(8,128)(2,1)S(1)} collective-permute-done((bf16[32,2048]{1,0:T(8,128)(2,1)S(1)}, bf16[32,2048]{1,0:T(8,128)(2,1)S(1)}, u32[]{:S(2)}, u32[]{:S(2)}) %collective-permute-start.7) | collective-permute-done | bytes 131104 | tf_op jit(solution)/shard_map/ppermute | solution.py:54
  36.0 4.6 %copy.6 = bf16[256,8,2,896]{3,1,2,0:T(8,128)(2,1)S(1)} copy(bf16[256,8,2,896]{3,2,1,0:T(2,128)(2,1)} %bitcast.13) | data formatting | bytes 14680064
  40.7 5.1 %multiply_convert_fusion = f16[512,1792]{1,0:T(8,128)(2,1)} fusion(bf16[512,2048]{1,0:T(8,128)(2,1)S(1)} %constant_dynamic-update-slice_fusion.10, bf16[2048,1792]{1,0:T(8,128)(2,1)S(1)} %bitcast.14), kind=kOutput, calls=%fused_computation.1 | convolution fusion | flops 3759931392 | bytes 11272192 | tf_op jit(solution)/shard_map/dot_general | solution.py:116
  45.9 3.0 %collective-permute-start.13 = (bf16[32,2048]{1,0:T(8,128)(2,1)S(1)}, bf16[32,2048]{1,0:T(8,128)(2,1)S(1)}, u32[]{:S(2)}, u32[]{:S(2)}) collective-permute-start(bf16[32,2048]{1,0:T(8,128)(2,1)S(1)} %pad_maximum_fusion.9), channel_id=1, source_target_pairs={{0,64},{32,96},{64,128},{96,160},{128,192},{160,224},{192,0},{224,... | collective-permute-start | bytes 393224 | tf_op jit(solution)/shard_map/ppermute | solution.py:54
  50.8 5.9 %all-to-all-start = ((f16[8,64,1792]{2,1,0:T(8,128)(2,1)}), f16[8,64,1792]{2,1,0:T(8,128)(2,1)S(1)}, u32[]{:S(2)}, u32[]{:S(2)}) async-start(f16[8,64,1792]{2,1,0:T(8,128)(2,1)} %bitcast.17), calls=%async_computation | async-start | bytes 3670016 | tf_op jit(solution)/shard_map/all_to_all | solution.py:98
  62.2 3.0 %collective-permute-done.12 = bf16[32,2048]{1,0:T(8,128)(2,1)S(1)} collective-permute-done((bf16[32,2048]{1,0:T(8,128)(2,1)S(1)}, bf16[32,2048]{1,0:T(8,128)(2,1)S(1)}, u32[]{:S(2)}, u32[]{:S(2)}) %collective-permute-start.12) | collective-permute-done | bytes 131104 | tf_op jit(solution)/shard_map/ppermute | solution.py:54
  79.6 27.1 %all_to_all.15 = bf16[8,128,896]{2,1,0:T(8,128)(2,1)S(1)} all-to-all(bf16[8,128,896]{2,1,0:T(8,128)(2,1)S(1)} %pad_maximum_fusion), channel_id=1, replica_groups=mesh['z'=8,'xh'=2,'core'=2,'xl'=2,'y'=4] {'xl','y'}, dimensions={0} | all-to-all | bytes 3670016 | tf_op jit(solution)/shard_map/all_to_all | solution.py:98
  109.6 3.3 %shard_map.60 = (f32[256,2048]{1,0:T(8,128)S(1)}, bf16[256,2048]{1,0:T(8,128)(2,1)S(1)}) custom-call(bf16[256,896]{1,0:T(8,128)(2,1)S(1)} %bitcast.12, bf16[256,896]{1,0:T(8,128)(2,1)S(1)} %bitcast.11, bf16[896,2048]{1,0:T(8,128)(2,1)S(1)} %copy-done.1), custom_call_target="tpu_custom_call" | custom-call | flops 512 | bytes 458752 | tf_op jit(solution)/shard_map/pallas_call | solution.py:35
  113.1 5.7 %all-to-all-start.2 = ((bf16[8,64,1792]{2,1,0:T(8,128)(2,1)}), bf16[8,64,1792]{2,1,0:T(8,128)(2,1)}, u32[]{:S(2)}, u32[]{:S(2)}) async-start(bf16[8,64,1792]{2,1,0:T(8,128)(2,1)} %broadcast_in_dim.5), calls=%async_computation.2 | async-start | bytes 3670016 | tf_op jit(solution)/shard_map/all_to_all | solution.py:98
  125.6 4.5 %collective-permute-done.20 = bf16[64,2048]{1,0:T(8,128)(2,1)S(1)} collective-permute-done((bf16[64,2048]{1,0:T(8,128)(2,1)S(1)}, bf16[64,2048]{1,0:T(8,128)(2,1)S(1)}, u32[]{:S(2)}, u32[]{:S(2)}) %collective-permute-start.20) | collective-permute-done | bytes 262176 | tf_op jit(solution)/shard_map/ppermute | solution.py:54
  130.2 3.3 %collective-permute-done.19 = bf16[64,2048]{1,0:T(8,128)(2,1)S(1)} collective-permute-done((bf16[64,2048]{1,0:T(8,128)(2,1)S(1)}, bf16[64,2048]{1,0:T(8,128)(2,1)S(1)}, u32[]{:S(2)}, u32[]{:S(2)}) %collective-permute-start.19) | collective-permute-done | bytes 262176 | tf_op jit(solution)/shard_map/ppermute | solution.py:54
  133.7 8.8 %all-to-all-done.2 = bf16[8,64,1792]{2,1,0:T(8,128)(2,1)} async-done(((bf16[8,64,1792]{2,1,0:T(8,128)(2,1)}), bf16[8,64,1792]{2,1,0:T(8,128)(2,1)}, u32[]{:S(2)}, u32[]{:S(2)}) %all-to-all-start.2) | async-done | bytes 1835040 | tf_op jit(solution)/shard_map/all_to_all | solution.py:98
  142.4 6.8 %fusion.22 = f32[512,2048]{1,0:T(8,128)S(1)} fusion(bf16[512,1792]{1,0:T(8,128)(2,1)} %bitcast.4, bf16[2048,1792]{1,0:T(8,128)(2,1)} %bitcast.15), kind=kOutput, calls=%fused_computation.84 | convolution fusion | flops 3758096384 | bytes 13369344 | tf_op jit(solution)/shard_map/dot_general | solution.py:144
  149.9 3.9 %collective-permute-start.24 = (bf16[32,2048]{1,0:T(8,128)(2,1)S(1)}, bf16[32,2048]{1,0:T(8,128)(2,1)S(1)}, u32[]{:S(2)}, u32[]{:S(2)}) collective-permute-start(bf16[32,2048]{1,0:T(8,128)(2,1)S(1)} %get-tuple-element.29), channel_id=1, source_target_pairs={{0,192},{32,224},{64,0},{96,32},{128,64},{160,96},{192,128},{224,1... | collective-permute-start | bytes 393224 | tf_op jit(solution)/shard_map/ppermute | solution.py:54
  153.7 6.5 %collective-permute-done.23 = bf16[32,2048]{1,0:T(8,128)(2,1)S(1)} collective-permute-done((bf16[32,2048]{1,0:T(8,128)(2,1)S(1)}, bf16[32,2048]{1,0:T(8,128)(2,1)S(1)}, u32[]{:S(2)}, u32[]{:S(2)}) %collective-permute-start.23) | collective-permute-done | bytes 131104 | tf_op jit(solution)/shard_map/ppermute | solution.py:54
  164.3 3.5 %collective-permute-start.31 = (bf16[16,2048]{1,0:T(8,128)(2,1)S(1)}, bf16[16,2048]{1,0:T(8,128)(2,1)S(1)}, u32[]{:S(2)}, u32[]{:S(2)}) collective-permute-start(bf16[16,2048]{1,0:T(8,128)(2,1)S(1)} %get-tuple-element.45), channel_id=1, source_target_pairs={{0,192},{32,224},{64,0},{96,32},{128,64},{160,96},{192,128},{224,1... | collective-permute-start | bytes 196616 | tf_op jit(solution)/shard_map/ppermute | solution.py:54
  170.7 3.4 %collective-permute-done.27 = bf16[64,2048]{1,0:T(8,128)(2,1)S(1)} collective-permute-done((bf16[64,2048]{1,0:T(8,128)(2,1)S(1)}, bf16[64,2048]{1,0:T(8,128)(2,1)S(1)}, u32[]{:S(2)}, u32[]{:S(2)}) %collective-permute-start.27) | collective-permute-done | bytes 262176 | tf_op jit(solution)/shard_map/ppermute | solution.py:54
  180.4 3.4 %collective-permute-done.30 = bf16[32,2048]{1,0:T(8,128)(2,1)S(1)} collective-permute-done((bf16[32,2048]{1,0:T(8,128)(2,1)S(1)}, bf16[32,2048]{1,0:T(8,128)(2,1)S(1)}, u32[]{:S(2)}, u32[]{:S(2)}) %collective-permute-start.30) | collective-permute-done | bytes 131104 | tf_op jit(solution)/shard_map/ppermute | solution.py:54
  185.9 3.7 %collective-permute-done.33 = bf16[16,2048]{1,0:T(8,128)(2,1)S(1)} collective-permute-done((bf16[16,2048]{1,0:T(8,128)(2,1)S(1)}, bf16[16,2048]{1,0:T(8,128)(2,1)S(1)}, u32[]{:S(2)}, u32[]{:S(2)}) %collective-permute-start.33) | collective-permute-done | bytes 65568 | tf_op jit(solution)/shard_map/ppermute | solution.py:50
  (122 shorter events, 58.0 us)
Async XLA Ops:
  9.2 12.3 %collective-permute-start.2 = (bf16[32,2048]{1,0:T(8,128)(2,1)S(1)}, bf16[32,2048]{1,0:T(8,128)(2,1)S(1)}, u32[]{:S(2)}, u32[]{:S(2)}) collective-permute-start(bf16[32,2048]{1,0:T(8,128)(2,1)S(1)} %pad_maximum_fusion.7), channel_id=1, source_target_pairs={{0,192},{32,224},{64,0},{96,32},{128,64},{160,96},{192,128},{224,1... | collective-permute-start | bytes 393224 | tf_op jit(solution)/shard_map/ppermute | solution.py:54
  15.6 10.5 %collective-permute-start.5 = (bf16[32,2048]{1,0:T(8,128)(2,1)S(1)}, bf16[32,2048]{1,0:T(8,128)(2,1)S(1)}, u32[]{:S(2)}, u32[]{:S(2)}) collective-permute-start(bf16[32,2048]{1,0:T(8,128)(2,1)S(1)} %pad_maximum_fusion.7), channel_id=1, source_target_pairs={{0,64},{32,96},{64,128},{96,160},{128,192},{160,224},{192,0},{224,... | collective-permute-start | bytes 393224 | tf_op jit(solution)/shard_map/ppermute | solution.py:54
  15.6 14.0 %collective-permute-start.1 = (bf16[32,2048]{1,0:T(8,128)(2,1)S(1)}, bf16[32,2048]{1,0:T(8,128)(2,1)S(1)}, u32[]{:S(2)}, u32[]{:S(2)}) collective-permute-start(bf16[32,2048]{1,0:T(8,128)(2,1)S(1)} %pad_maximum_fusion.7), channel_id=1, source_target_pairs={{0,224},{32,0},{64,32},{96,64},{128,96},{160,128},{192,160},{224,1... | collective-permute-start | bytes 393224 | tf_op jit(solution)/shard_map/ppermute | solution.py:54
  19.3 16.6 %collective-permute-start.8 = (bf16[32,2048]{1,0:T(8,128)(2,1)S(1)}, bf16[32,2048]{1,0:T(8,128)(2,1)S(1)}, u32[]{:S(2)}, u32[]{:S(2)}) collective-permute-start(bf16[32,2048]{1,0:T(8,128)(2,1)S(1)} %pad_maximum_fusion.7), channel_id=1, source_target_pairs={{0,32},{32,64},{64,96},{96,128},{128,160},{160,192},{192,224},{224... | collective-permute-start | bytes 393224 | tf_op jit(solution)/shard_map/ppermute | solution.py:54
  21.5 10.6 %collective-permute-start.4 = (bf16[16,2048]{1,0:T(8,128)(2,1)S(1)}, bf16[16,2048]{1,0:T(8,128)(2,1)S(1)}, u32[]{:S(2)}, u32[]{:S(2)}) collective-permute-start(bf16[16,2048]{1,0:T(8,128)(2,1)S(1)} %slice.206), channel_id=1, source_target_pairs={{0,192},{32,224},{64,0},{96,32},{128,64},{160,96},{192,128},{224,1... | collective-permute-start | bytes 196616 | tf_op jit(solution)/shard_map/ppermute | solution.py:54
  45.8 16.3 %collective-permute-start.10 = (bf16[32,2048]{1,0:T(8,128)(2,1)S(1)}, bf16[32,2048]{1,0:T(8,128)(2,1)S(1)}, u32[]{:S(2)}, u32[]{:S(2)}) collective-permute-start(bf16[32,2048]{1,0:T(8,128)(2,1)S(1)} %pad_maximum_fusion.9), channel_id=1, source_target_pairs={{0,224},{32,0},{64,32},{96,64},{128,96},{160,128},{192,160},{224,1... | collective-permute-start | bytes 393224 | tf_op jit(solution)/shard_map/ppermute | solution.py:54
  45.9 13.6 %collective-permute-start.11 = (bf16[32,2048]{1,0:T(8,128)(2,1)S(1)}, bf16[32,2048]{1,0:T(8,128)(2,1)S(1)}, u32[]{:S(2)}, u32[]{:S(2)}) collective-permute-start(bf16[32,2048]{1,0:T(8,128)(2,1)S(1)} %pad_maximum_fusion.9), channel_id=1, source_target_pairs={{0,192},{32,224},{64,0},{96,32},{128,64},{160,96},{192,128},{224,1... | collective-permute-start | bytes 393224 | tf_op jit(solution)/shard_map/ppermute | solution.py:54
  45.9 11.0 %collective-permute-start.13 = (bf16[32,2048]{1,0:T(8,128)(2,1)S(1)}, bf16[32,2048]{1,0:T(8,128)(2,1)S(1)}, u32[]{:S(2)}, u32[]{:S(2)}) collective-permute-start(bf16[32,2048]{1,0:T(8,128)(2,1)S(1)} %pad_maximum_fusion.9), channel_id=1, source_target_pairs={{0,64},{32,96},{64,128},{96,160},{128,192},{160,224},{192,0},{224,... | collective-permute-start | bytes 393224 | tf_op jit(solution)/shard_map/ppermute | solution.py:54
  48.9 20.4 %collective-permute-start.16 = (bf16[32,2048]{1,0:T(8,128)(2,1)S(1)}, bf16[32,2048]{1,0:T(8,128)(2,1)S(1)}, u32[]{:S(2)}, u32[]{:S(2)}) collective-permute-start(bf16[32,2048]{1,0:T(8,128)(2,1)S(1)} %pad_maximum_fusion.9), channel_id=1, source_target_pairs={{0,32},{32,64},{64,96},{96,128},{128,160},{160,192},{192,224},{224... | collective-permute-start | bytes 393224 | tf_op jit(solution)/shard_map/ppermute | solution.py:54
  50.8 28.1 %all-to-all-start = ((f16[8,64,1792]{2,1,0:T(8,128)(2,1)}), f16[8,64,1792]{2,1,0:T(8,128)(2,1)S(1)}, u32[]{:S(2)}, u32[]{:S(2)}) async-start(f16[8,64,1792]{2,1,0:T(8,128)(2,1)} %bitcast.17), calls=%async_computation | async-start | bytes 3670016 | tf_op jit(solution)/shard_map/all_to_all | solution.py:98
  57.0 10.3 %collective-permute-start.14 = (bf16[32,2048]{1,0:T(8,128)(2,1)S(1)}, bf16[32,2048]{1,0:T(8,128)(2,1)S(1)}, u32[]{:S(2)}, u32[]{:S(2)}) collective-permute-start(bf16[32,2048]{1,0:T(8,128)(2,1)S(1)} %collective-permute-done.13), channel_id=1, source_target_pairs={{0,64},{32,96},{64,128},{96,160},{128,192},{160,224},{192,0},{224,... | collective-permute-start | bytes 393224 | tf_op jit(solution)/shard_map/ppermute | solution.py:54
  58.9 10.3 %collective-permute-start.15 = (bf16[32,2048]{1,0:T(8,128)(2,1)S(1)}, bf16[32,2048]{1,0:T(8,128)(2,1)S(1)}, u32[]{:S(2)}, u32[]{:S(2)}) collective-permute-start(bf16[32,2048]{1,0:T(8,128)(2,1)S(1)} %collective-permute-done.13), channel_id=1, source_target_pairs={{0,32},{32,64},{64,96},{96,128},{128,160},{160,192},{192,224},{224... | collective-permute-start | bytes 393224 | tf_op jit(solution)/shard_map/ppermute | solution.py:54
  113.1 29.4 %all-to-all-start.2 = ((bf16[8,64,1792]{2,1,0:T(8,128)(2,1)}), bf16[8,64,1792]{2,1,0:T(8,128)(2,1)}, u32[]{:S(2)}, u32[]{:S(2)}) async-start(bf16[8,64,1792]{2,1,0:T(8,128)(2,1)} %broadcast_in_dim.5), calls=%async_computation.2 | async-start | bytes 3670016 | tf_op jit(solution)/shard_map/all_to_all | solution.py:98
  120.4 9.7 %collective-permute-start.20 = (bf16[64,2048]{1,0:T(8,128)(2,1)S(1)}, bf16[64,2048]{1,0:T(8,128)(2,1)S(1)}, u32[]{:S(2)}, u32[]{:S(2)}) collective-permute-start(bf16[64,2048]{1,0:T(8,128)(2,1)S(1)} %pad_maximum_fusion.3), channel_id=1, source_target_pairs={{0,224},{32,0},{64,32},{96,64},{128,96},{160,128},{192,160},{224,1... | collective-permute-start | bytes 786440 | tf_op jit(solution)/shard_map/ppermute | solution.py:54
  122.0 11.5 %collective-permute-start.19 = (bf16[64,2048]{1,0:T(8,128)(2,1)S(1)}, bf16[64,2048]{1,0:T(8,128)(2,1)S(1)}, u32[]{:S(2)}, u32[]{:S(2)}) collective-permute-start(bf16[64,2048]{1,0:T(8,128)(2,1)S(1)} %pad_maximum_fusion.2), channel_id=1, source_target_pairs={{0,32},{32,64},{64,96},{96,128},{128,160},{160,192},{192,224},{224... | collective-permute-start | bytes 786440 | tf_op jit(solution)/shard_map/ppermute | solution.py:54
  122.6 10.9 %collective-permute-start.22 = (bf16[16,2048]{1,0:T(8,128)(2,1)S(1)}, bf16[16,2048]{1,0:T(8,128)(2,1)S(1)}, u32[]{:S(2)}, u32[]{:S(2)}) collective-permute-start(bf16[16,2048]{1,0:T(8,128)(2,1)S(1)} %get-tuple-element.50), channel_id=1, source_target_pairs={{0,192},{32,224},{64,0},{96,32},{128,64},{160,96},{192,128},{224,1... | collective-permute-start | bytes 196616 | tf_op jit(solution)/shard_map/ppermute | solution.py:54
  124.2 9.4 %collective-permute-start.21 = (bf16[16,2048]{1,0:T(8,128)(2,1)S(1)}, bf16[16,2048]{1,0:T(8,128)(2,1)S(1)}, u32[]{:S(2)}, u32[]{:S(2)}) collective-permute-start(bf16[16,2048]{1,0:T(8,128)(2,1)S(1)} %get-tuple-element.51), channel_id=1, source_target_pairs={{0,64},{32,96},{64,128},{96,160},{128,192},{160,224},{192,0},{224,... | collective-permute-start | bytes 196616 | tf_op jit(solution)/shard_map/ppermute | solution.py:54
  149.4 10.8 %collective-permute-start.25 = (bf16[256,2048]{1,0:T(8,128)(2,1)S(1)}, bf16[256,2048]{1,0:T(8,128)(2,1)S(1)}, u32[]{:S(2)}, u32[]{:S(2)}) collective-permute-start(bf16[256,2048]{1,0:T(8,128)(2,1)S(1)} %slice.306), channel_id=1, source_target_pairs={{0,8},{8,0},{1,9},{9,1},{2,10},{10,2},{3,11},{11,3},{4,12},{12,4},... | collective-permute-start | bytes 3145736 | tf_op jit(solution)/shard_map/ppermute | solution.py:50
  149.5 10.7 %collective-permute-start.23 = (bf16[32,2048]{1,0:T(8,128)(2,1)S(1)}, bf16[32,2048]{1,0:T(8,128)(2,1)S(1)}, u32[]{:S(2)}, u32[]{:S(2)}) collective-permute-start(bf16[32,2048]{1,0:T(8,128)(2,1)S(1)} %get-tuple-element.28), channel_id=1, source_target_pairs={{0,64},{32,96},{64,128},{96,160},{128,192},{160,224},{192,0},{224,... | collective-permute-start | bytes 393224 | tf_op jit(solution)/shard_map/ppermute | solution.py:54
  149.9 10.4 %collective-permute-start.24 = (bf16[32,2048]{1,0:T(8,128)(2,1)S(1)}, bf16[32,2048]{1,0:T(8,128)(2,1)S(1)}, u32[]{:S(2)}, u32[]{:S(2)}) collective-permute-start(bf16[32,2048]{1,0:T(8,128)(2,1)S(1)} %get-tuple-element.29), channel_id=1, source_target_pairs={{0,192},{32,224},{64,0},{96,32},{128,64},{160,96},{192,128},{224,1... | collective-permute-start | bytes 393224 | tf_op jit(solution)/shard_map/ppermute | solution.py:54
  160.7 10.0 %collective-permute-start.28 = (bf16[64,2048]{1,0:T(8,128)(2,1)S(1)}, bf16[64,2048]{1,0:T(8,128)(2,1)S(1)}, u32[]{:S(2)}, u32[]{:S(2)}) collective-permute-start(bf16[64,2048]{1,0:T(8,128)(2,1)S(1)} %pad_maximum_fusion.5), channel_id=1, source_target_pairs={{0,224},{32,0},{64,32},{96,64},{128,96},{160,128},{192,160},{224,1... | collective-permute-start | bytes 786440 | tf_op jit(solution)/shard_map/ppermute | solution.py:54
  163.5 10.7 %collective-permute-start.27 = (bf16[64,2048]{1,0:T(8,128)(2,1)S(1)}, bf16[64,2048]{1,0:T(8,128)(2,1)S(1)}, u32[]{:S(2)}, u32[]{:S(2)}) collective-permute-start(bf16[64,2048]{1,0:T(8,128)(2,1)S(1)} %pad_maximum_fusion.4), channel_id=1, source_target_pairs={{0,32},{32,64},{64,96},{96,128},{128,160},{160,192},{192,224},{224... | collective-permute-start | bytes 786440 | tf_op jit(solution)/shard_map/ppermute | solution.py:54
  163.6 10.6 %collective-permute-start.29 = (bf16[16,2048]{1,0:T(8,128)(2,1)S(1)}, bf16[16,2048]{1,0:T(8,128)(2,1)S(1)}, u32[]{:S(2)}, u32[]{:S(2)}) collective-permute-start(bf16[16,2048]{1,0:T(8,128)(2,1)S(1)} %get-tuple-element.44), channel_id=1, source_target_pairs={{0,64},{32,96},{64,128},{96,160},{128,192},{160,224},{192,0},{224,... | collective-permute-start | bytes 196616 | tf_op jit(solution)/shard_map/ppermute | solution.py:54
  164.3 9.9 %collective-permute-start.31 = (bf16[16,2048]{1,0:T(8,128)(2,1)S(1)}, bf16[16,2048]{1,0:T(8,128)(2,1)S(1)}, u32[]{:S(2)}, u32[]{:S(2)}) collective-permute-start(bf16[16,2048]{1,0:T(8,128)(2,1)S(1)} %get-tuple-element.45), channel_id=1, source_target_pairs={{0,192},{32,224},{64,0},{96,32},{128,64},{160,96},{192,128},{224,1... | collective-permute-start | bytes 196616 | tf_op jit(solution)/shard_map/ppermute | solution.py:54
  (17 other events, 98.6 us)

commit v4 on v3

--- a/solution.py
+++ b/solution.py
@@ -88,10 +88,14 @@
     return [shift(second, -2 * way) for way, second in zip((1, -1), seconds)]
 
 
-def last_round(total, seconds):
-    total = total + seconds[0].astype(F32) + seconds[1].astype(F32)
-    rows = total.shape[0] // 2
-    return (total[:rows] + swap(total[rows:].astype(BF), "xh").astype(F32)).astype(BF)
+def added(total, seconds):
+    return total + seconds[0].astype(F32) + seconds[1].astype(F32)
+
+
+def last_round(sums):
+    rows = sums[0].shape[0] // 2
+    come = swap(jnp.concatenate([x[rows:] for x in sums]).astype(BF), "xh").astype(F32)
+    return [(x[:rows] + come[i * rows : (i + 1) * rows]).astype(BF) for i, x in enumerate(sums)]
 
 
 def exchange(x):
@@ -139,14 +143,13 @@
 
     kept, sent = product(hidden, down_weight, False, (F32, BF), 512)
     total, seconds = first_round(kept + swap(sent, "core").astype(F32))
-    seconds, grads = lax.optimization_barrier((seconds, grads))
-    seconds = second_round(seconds)
+    seconds, grads = lax.optimization_barrier((second_round(seconds), grads))
+    total = added(total, seconds)
     out = lax.dot_general(grads, weights, LAST, preferred_element_type=F32)
-    come = swap(out[half:].astype(BF), "core")
-    seconds, come = lax.optimization_barrier((seconds, come))
-    block_out = last_round(total, seconds)
-    total, seconds = first_round(out[:half] + come.astype(F32))
-    return block_out, last_round(total, second_round(seconds))
+    out = out[:half] + swap(out[half:].astype(BF), "core").astype(F32)
+    last, seconds = first_round(out)
+    block_out, grad_tokens = last_round([total, added(last, second_round(seconds))])
+    return block_out, grad_tokens
 
 
 def solution(mesh):

time: 191 us -> 185 us (0.969)
  waiting for transfers between devices: 62.1 us -> 53.4 us
  starting transfers between devices: 64.2 us -> 67.5 us
    all_to_all x2, waiting for transfers between devices: 11.1 us -> 2.87 us  [exchange(): return lax.all_to_all(x, COL, 0, 0, tiled=True)]
    ppermute x27, starting transfers between devices: 47.7 us -> 52.5 us  [shift(): return lax.ppermute(x, 'z', [(i, (i - by) % NZ) for i in range(NZ)])]
    ppermute x27, waiting for transfers between devices: 40 us -> 35.7 us  [shift(): return lax.ppermute(x, 'z', [(i, (i - by) % NZ) for i in range(NZ)])]
    ppermute x7 -> x6, waiting for transfers between devices: 10.9 us -> 14.9 us  [swap(): return lax.ppermute(x, axis, SWAP)]
    ppermute x7 -> x6, starting transfers between devices: 4.84 us -> 3.35 us  [swap(): return lax.ppermute(x, axis, SWAP)]
  transfers between devices with their start and end apart: 36 -> 35, of which waited for: 20 -> 21; matrix products, arithmetic and copies ran while one was open for 5% -> 5% of each run, Pallas kernels for 1% -> 1%
where the time goes in v4:
time: 185 us; the launch traced here: 184 us
  starting transfers between devices  67.5 us (36%)
  waiting for transfers between devices  53.4 us (29%)
  blocking collectives  27.1 us (15%)
  matrix products  11.9 us (6%)
  local copies, waits for them, and re-layouts  10.9 us (6%)
  other arithmetic  6.77 us (4%)
  Pallas kernels  5.68 us (3%)
    ppermute x27, starting transfers between devices, shift(): return lax.ppermute(x, 'z', [(i, (i - by) % NZ) for i in range(NZ)])  52.5 us
    ppermute x27, waiting for transfers between devices, shift(): return lax.ppermute(x, 'z', [(i, (i - by) % NZ) for i in range(NZ)])  35.7 us
    all_to_all x1, blocking collectives, exchange(): return lax.all_to_all(x, COL, 0, 0, tiled=True)  27.1 us
    ppermute x6, waiting for transfers between devices, swap(): return lax.ppermute(x, axis, SWAP)  14.9 us
    all_to_all x2, starting transfers between devices, exchange(): return lax.all_to_all(x, COL, 0, 0, tiled=True)  11.6 us
    unnamed x26, local copies, waits for them, and re-layouts  8.83 us
    dot_general x1, matrix products, per_device(): out = lax.dot_general(grads, weights, LAST, preferred_element_type=F32)  6.82 us
    pallas_call x2, Pallas kernels, product(): pl.pallas_call(body, grid=(n // width,), in_specs=[pl.BlockSpec(x.shape,...  5.68 us
  transfers between devices with their start and end apart: 35, of which 21 were waited for; matrix products, arithmetic and copies ran while one was open for 5% of the time, Pallas kernels for 1%

profile of v4, /device:TPU:6, one launch (start us, length us, event | category | flops | bytes accessed | tf_op | source)
XLA Modules:
  0.0 184.3 jit_solution(3681524606990402354)
XLA Ops:
  3.9 4.5 %collective-permute-done = bf16[32,2048]{1,0:T(8,128)(2,1)S(1)} collective-permute-done((bf16[32,2048]{1,0:T(8,128)(2,1)S(1)}, bf16[32,2048]{1,0:T(8,128)(2,1)S(1)}, u32[]{:S(2)}, u32[]{:S(2)}) %collective-permute-start) | collective-permute-done | bytes 131104 | tf_op jit(solution)/shard_map/ppermute | solution.py:50
  9.2 6.4 %collective-permute-start.2 = (bf16[32,2048]{1,0:T(8,128)(2,1)S(1)}, bf16[32,2048]{1,0:T(8,128)(2,1)S(1)}, u32[]{:S(2)}, u32[]{:S(2)}) collective-permute-start(bf16[32,2048]{1,0:T(8,128)(2,1)S(1)} %pad_maximum_fusion.7), channel_id=1, source_target_pairs={{0,192},{32,224},{64,0},{96,32},{128,64},{160,96},{192,128},{224,1... | collective-permute-start | bytes 393224 | tf_op jit(solution)/shard_map/ppermute | solution.py:54
  15.6 3.7 %collective-permute-start.1 = (bf16[32,2048]{1,0:T(8,128)(2,1)S(1)}, bf16[32,2048]{1,0:T(8,128)(2,1)S(1)}, u32[]{:S(2)}, u32[]{:S(2)}) collective-permute-start(bf16[32,2048]{1,0:T(8,128)(2,1)S(1)} %pad_maximum_fusion.7), channel_id=1, source_target_pairs={{0,224},{32,0},{64,32},{96,64},{128,96},{160,128},{192,160},{224,1... | collective-permute-start | bytes 393224 | tf_op jit(solution)/shard_map/ppermute | solution.py:54
  21.5 4.6 %collective-permute-start.4 = (bf16[16,2048]{1,0:T(8,128)(2,1)S(1)}, bf16[16,2048]{1,0:T(8,128)(2,1)S(1)}, u32[]{:S(2)}, u32[]{:S(2)}) collective-permute-start(bf16[16,2048]{1,0:T(8,128)(2,1)S(1)} %slice.214), channel_id=1, source_target_pairs={{0,192},{32,224},{64,0},{96,32},{128,64},{160,96},{192,128},{224,1... | collective-permute-start | bytes 196616 | tf_op jit(solution)/shard_map/ppermute | solution.py:54
  26.2 3.4 %collective-permute-start.3 = (bf16[32,2048]{1,0:T(8,128)(2,1)S(1)}, bf16[32,2048]{1,0:T(8,128)(2,1)S(1)}, u32[]{:S(2)}, u32[]{:S(2)}) collective-permute-start(bf16[32,2048]{1,0:T(8,128)(2,1)S(1)} %collective-permute-done.2), channel_id=1, source_target_pairs={{0,224},{32,0},{64,32},{96,64},{128,96},{160,128},{192,160},{224,1... | collective-permute-start | bytes 393224 | tf_op jit(solution)/shard_map/ppermute | solution.py:54
  32.6 3.2 %collective-permute-done.7 = bf16[32,2048]{1,0:T(8,128)(2,1)S(1)} collective-permute-done((bf16[32,2048]{1,0:T(8,128)(2,1)S(1)}, bf16[32,2048]{1,0:T(8,128)(2,1)S(1)}, u32[]{:S(2)}, u32[]{:S(2)}) %collective-permute-start.7) | collective-permute-done | bytes 131104 | tf_op jit(solution)/shard_map/ppermute | solution.py:54
  36.0 4.6 %copy.6 = bf16[256,8,2,896]{3,1,2,0:T(8,128)(2,1)S(1)} copy(bf16[256,8,2,896]{3,2,1,0:T(2,128)(2,1)} %bitcast.13) | data formatting | bytes 14680064
  40.7 5.1 %multiply_convert_fusion = f16[512,1792]{1,0:T(8,128)(2,1)} fusion(bf16[512,2048]{1,0:T(8,128)(2,1)S(1)} %constant_dynamic-update-slice_fusion.10, bf16[2048,1792]{1,0:T(8,128)(2,1)S(1)} %bitcast.14), kind=kOutput, calls=%fused_computation.1 | convolution fusion | flops 3759931392 | bytes 11272192 | tf_op jit(solution)/shard_map/dot_general | solution.py:120
  45.9 3.0 %collective-permute-start.13 = (bf16[32,2048]{1,0:T(8,128)(2,1)S(1)}, bf16[32,2048]{1,0:T(8,128)(2,1)S(1)}, u32[]{:S(2)}, u32[]{:S(2)}) collective-permute-start(bf16[32,2048]{1,0:T(8,128)(2,1)S(1)} %pad_maximum_fusion.9), channel_id=1, source_target_pairs={{0,64},{32,96},{64,128},{96,160},{128,192},{160,224},{192,0},{224,... | collective-permute-start | bytes 393224 | tf_op jit(solution)/shard_map/ppermute | solution.py:54
  50.8 5.9 %all-to-all-start = ((f16[8,64,1792]{2,1,0:T(8,128)(2,1)}), f16[8,64,1792]{2,1,0:T(8,128)(2,1)S(1)}, u32[]{:S(2)}, u32[]{:S(2)}) async-start(f16[8,64,1792]{2,1,0:T(8,128)(2,1)} %bitcast.17), calls=%async_computation | async-start | bytes 3670016 | tf_op jit(solution)/shard_map/all_to_all | solution.py:102
  62.2 3.0 %collective-permute-done.12 = bf16[32,2048]{1,0:T(8,128)(2,1)S(1)} collective-permute-done((bf16[32,2048]{1,0:T(8,128)(2,1)S(1)}, bf16[32,2048]{1,0:T(8,128)(2,1)S(1)}, u32[]{:S(2)}, u32[]{:S(2)}) %collective-permute-start.12) | collective-permute-done | bytes 131104 | tf_op jit(solution)/shard_map/ppermute | solution.py:54
  79.6 27.1 %all_to_all.15 = bf16[8,128,896]{2,1,0:T(8,128)(2,1)S(1)} all-to-all(bf16[8,128,896]{2,1,0:T(8,128)(2,1)S(1)} %pad_maximum_fusion), channel_id=1, replica_groups=mesh['z'=8,'xh'=2,'core'=2,'xl'=2,'y'=4] {'xl','y'}, dimensions={0} | all-to-all | bytes 3670016 | tf_op jit(solution)/shard_map/all_to_all | solution.py:102
  109.6 3.3 %shard_map.60 = (f32[256,2048]{1,0:T(8,128)S(1)}, bf16[256,2048]{1,0:T(8,128)(2,1)S(1)}) custom-call(bf16[256,896]{1,0:T(8,128)(2,1)S(1)} %bitcast.12, bf16[256,896]{1,0:T(8,128)(2,1)S(1)} %bitcast.11, bf16[896,2048]{1,0:T(8,128)(2,1)S(1)} %copy-done.1), custom_call_target="tpu_custom_call" | custom-call | flops 512 | bytes 458752 | tf_op jit(solution)/shard_map/pallas_call | solution.py:35
  113.1 5.7 %all-to-all-start.2 = ((bf16[8,64,1792]{2,1,0:T(8,128)(2,1)}), bf16[8,64,1792]{2,1,0:T(8,128)(2,1)}, u32[]{:S(2)}, u32[]{:S(2)}) async-start(bf16[8,64,1792]{2,1,0:T(8,128)(2,1)} %broadcast_in_dim.5), calls=%async_computation.2 | async-start | bytes 3670016 | tf_op jit(solution)/shard_map/all_to_all | solution.py:102
  120.8 3.0 %collective-permute-start.20 = (bf16[64,2048]{1,0:T(8,128)(2,1)S(1)}, bf16[64,2048]{1,0:T(8,128)(2,1)S(1)}, u32[]{:S(2)}, u32[]{:S(2)}) collective-permute-start(bf16[64,2048]{1,0:T(8,128)(2,1)S(1)} %pad_maximum_fusion.3), channel_id=1, source_target_pairs={{0,224},{32,0},{64,32},{96,64},{128,96},{160,128},{192,160},{224,1... | collective-permute-start | bytes 786440 | tf_op jit(solution)/shard_map/ppermute | solution.py:54
  123.9 4.1 %collective-permute-start.23 = (bf16[16,2048]{1,0:T(8,128)(2,1)S(1)}, bf16[16,2048]{1,0:T(8,128)(2,1)S(1)}, u32[]{:S(2)}, u32[]{:S(2)}) collective-permute-start(bf16[16,2048]{1,0:T(8,128)(2,1)S(1)} %get-tuple-element.44), channel_id=1, source_target_pairs={{0,192},{32,224},{64,0},{96,32},{128,64},{160,96},{192,128},{224,1... | collective-permute-start | bytes 196616 | tf_op jit(solution)/shard_map/ppermute | solution.py:54
  128.0 4.2 %collective-permute-done.19 = bf16[64,2048]{1,0:T(8,128)(2,1)S(1)} collective-permute-done((bf16[64,2048]{1,0:T(8,128)(2,1)S(1)}, bf16[64,2048]{1,0:T(8,128)(2,1)S(1)}, u32[]{:S(2)}, u32[]{:S(2)}) %collective-permute-start.19) | collective-permute-done | bytes 262176 | tf_op jit(solution)/shard_map/ppermute | solution.py:54
  134.4 2.7 %collective-permute-start.24 = (bf16[32,2048]{1,0:T(8,128)(2,1)S(1)}, bf16[32,2048]{1,0:T(8,128)(2,1)S(1)}, u32[]{:S(2)}, u32[]{:S(2)}) collective-permute-start(bf16[32,2048]{1,0:T(8,128)(2,1)S(1)} %get-tuple-element.34), channel_id=1, source_target_pairs={{0,192},{32,224},{64,0},{96,32},{128,64},{160,96},{192,128},{224,1... | collective-permute-start | bytes 393224 | tf_op jit(solution)/shard_map/ppermute | solution.py:54
  137.1 4.8 %collective-permute-done.22 = bf16[32,2048]{1,0:T(8,128)(2,1)S(1)} collective-permute-done((bf16[32,2048]{1,0:T(8,128)(2,1)S(1)}, bf16[32,2048]{1,0:T(8,128)(2,1)S(1)}, u32[]{:S(2)}, u32[]{:S(2)}) %collective-permute-start.22) | collective-permute-done | bytes 131104 | tf_op jit(solution)/shard_map/ppermute | solution.py:54
  142.4 6.8 %fusion.22 = f32[512,2048]{1,0:T(8,128)S(1)} fusion(bf16[512,1792]{1,0:T(8,128)(2,1)} %bitcast.4, bf16[2048,1792]{1,0:T(8,128)(2,1)} %bitcast.15), kind=kOutput, calls=%fused_computation.85 | convolution fusion | flops 3758096384 | bytes 13369344 | tf_op jit(solution)/shard_map/dot_general | solution.py:148
  157.5 2.9 %collective-permute-start.30 = (bf16[16,2048]{1,0:T(8,128)(2,1)S(1)}, bf16[16,2048]{1,0:T(8,128)(2,1)S(1)}, u32[]{:S(2)}, u32[]{:S(2)}) collective-permute-start(bf16[16,2048]{1,0:T(8,128)(2,1)S(1)} %get-tuple-element.39), channel_id=1, source_target_pairs={{0,192},{32,224},{64,0},{96,32},{128,64},{160,96},{192,128},{224,1... | collective-permute-start | bytes 196616 | tf_op jit(solution)/shard_map/ppermute | solution.py:54
  160.4 2.7 %collective-permute-done.26 = bf16[64,2048]{1,0:T(8,128)(2,1)S(1)} collective-permute-done((bf16[64,2048]{1,0:T(8,128)(2,1)S(1)}, bf16[64,2048]{1,0:T(8,128)(2,1)S(1)}, u32[]{:S(2)}, u32[]{:S(2)}) %collective-permute-start.26) | collective-permute-done | bytes 262176 | tf_op jit(solution)/shard_map/ppermute | solution.py:54
  166.7 3.1 %collective-permute-start.29 = (bf16[32,2048]{1,0:T(8,128)(2,1)S(1)}, bf16[32,2048]{1,0:T(8,128)(2,1)S(1)}, u32[]{:S(2)}, u32[]{:S(2)}) collective-permute-start(bf16[32,2048]{1,0:T(8,128)(2,1)S(1)} %get-tuple-element.32), channel_id=1, source_target_pairs={{0,64},{32,96},{64,128},{96,160},{128,192},{160,224},{192,0},{224,... | collective-permute-start | bytes 393224 | tf_op jit(solution)/shard_map/ppermute | solution.py:54
  178.5 5.1 %collective-permute-done.32 = bf16[32,2048]{1,0:T(8,128)(2,1)S(1)} collective-permute-done((bf16[32,2048]{1,0:T(8,128)(2,1)S(1)}, bf16[32,2048]{1,0:T(8,128)(2,1)S(1)}, u32[]{:S(2)}, u32[]{:S(2)}) %collective-permute-start.32) | collective-permute-done | bytes 131104 | tf_op jit(solution)/shard_map/ppermute | solution.py:50
  (121 shorter events, 60.3 us)
Async XLA Ops:
  9.2 12.3 %collective-permute-start.2 = (bf16[32,2048]{1,0:T(8,128)(2,1)S(1)}, bf16[32,2048]{1,0:T(8,128)(2,1)S(1)}, u32[]{:S(2)}, u32[]{:S(2)}) collective-permute-start(bf16[32,2048]{1,0:T(8,128)(2,1)S(1)} %pad_maximum_fusion.7), channel_id=1, source_target_pairs={{0,192},{32,224},{64,0},{96,32},{128,64},{160,96},{192,128},{224,1... | collective-permute-start | bytes 393224 | tf_op jit(solution)/shard_map/ppermute | solution.py:54
  15.6 10.5 %collective-permute-start.5 = (bf16[32,2048]{1,0:T(8,128)(2,1)S(1)}, bf16[32,2048]{1,0:T(8,128)(2,1)S(1)}, u32[]{:S(2)}, u32[]{:S(2)}) collective-permute-start(bf16[32,2048]{1,0:T(8,128)(2,1)S(1)} %pad_maximum_fusion.7), channel_id=1, source_target_pairs={{0,64},{32,96},{64,128},{96,160},{128,192},{160,224},{192,0},{224,... | collective-permute-start | bytes 393224 | tf_op jit(solution)/shard_map/ppermute | solution.py:54
  15.6 14.0 %collective-permute-start.1 = (bf16[32,2048]{1,0:T(8,128)(2,1)S(1)}, bf16[32,2048]{1,0:T(8,128)(2,1)S(1)}, u32[]{:S(2)}, u32[]{:S(2)}) collective-permute-start(bf16[32,2048]{1,0:T(8,128)(2,1)S(1)} %pad_maximum_fusion.7), channel_id=1, source_target_pairs={{0,224},{32,0},{64,32},{96,64},{128,96},{160,128},{192,160},{224,1... | collective-permute-start | bytes 393224 | tf_op jit(solution)/shard_map/ppermute | solution.py:54
  19.3 16.6 %collective-permute-start.8 = (bf16[32,2048]{1,0:T(8,128)(2,1)S(1)}, bf16[32,2048]{1,0:T(8,128)(2,1)S(1)}, u32[]{:S(2)}, u32[]{:S(2)}) collective-permute-start(bf16[32,2048]{1,0:T(8,128)(2,1)S(1)} %pad_maximum_fusion.7), channel_id=1, source_target_pairs={{0,32},{32,64},{64,96},{96,128},{128,160},{160,192},{192,224},{224... | collective-permute-start | bytes 393224 | tf_op jit(solution)/shard_map/ppermute | solution.py:54
  21.5 10.6 %collective-permute-start.4 = (bf16[16,2048]{1,0:T(8,128)(2,1)S(1)}, bf16[16,2048]{1,0:T(8,128)(2,1)S(1)}, u32[]{:S(2)}, u32[]{:S(2)}) collective-permute-start(bf16[16,2048]{1,0:T(8,128)(2,1)S(1)} %slice.214), channel_id=1, source_target_pairs={{0,192},{32,224},{64,0},{96,32},{128,64},{160,96},{192,128},{224,1... | collective-permute-start | bytes 196616 | tf_op jit(solution)/shard_map/ppermute | solution.py:54
  45.8 16.3 %collective-permute-start.10 = (bf16[32,2048]{1,0:T(8,128)(2,1)S(1)}, bf16[32,2048]{1,0:T(8,128)(2,1)S(1)}, u32[]{:S(2)}, u32[]{:S(2)}) collective-permute-start(bf16[32,2048]{1,0:T(8,128)(2,1)S(1)} %pad_maximum_fusion.9), channel_id=1, source_target_pairs={{0,224},{32,0},{64,32},{96,64},{128,96},{160,128},{192,160},{224,1... | collective-permute-start | bytes 393224 | tf_op jit(solution)/shard_map/ppermute | solution.py:54
  45.9 13.6 %collective-permute-start.11 = (bf16[32,2048]{1,0:T(8,128)(2,1)S(1)}, bf16[32,2048]{1,0:T(8,128)(2,1)S(1)}, u32[]{:S(2)}, u32[]{:S(2)}) collective-permute-start(bf16[32,2048]{1,0:T(8,128)(2,1)S(1)} %pad_maximum_fusion.9), channel_id=1, source_target_pairs={{0,192},{32,224},{64,0},{96,32},{128,64},{160,96},{192,128},{224,1... | collective-permute-start | bytes 393224 | tf_op jit(solution)/shard_map/ppermute | solution.py:54
  45.9 11.0 %collective-permute-start.13 = (bf16[32,2048]{1,0:T(8,128)(2,1)S(1)}, bf16[32,2048]{1,0:T(8,128)(2,1)S(1)}, u32[]{:S(2)}, u32[]{:S(2)}) collective-permute-start(bf16[32,2048]{1,0:T(8,128)(2,1)S(1)} %pad_maximum_fusion.9), channel_id=1, source_target_pairs={{0,64},{32,96},{64,128},{96,160},{128,192},{160,224},{192,0},{224,... | collective-permute-start | bytes 393224 | tf_op jit(solution)/shard_map/ppermute | solution.py:54
  48.9 20.4 %collective-permute-start.16 = (bf16[32,2048]{1,0:T(8,128)(2,1)S(1)}, bf16[32,2048]{1,0:T(8,128)(2,1)S(1)}, u32[]{:S(2)}, u32[]{:S(2)}) collective-permute-start(bf16[32,2048]{1,0:T(8,128)(2,1)S(1)} %pad_maximum_fusion.9), channel_id=1, source_target_pairs={{0,32},{32,64},{64,96},{96,128},{128,160},{160,192},{192,224},{224... | collective-permute-start | bytes 393224 | tf_op jit(solution)/shard_map/ppermute | solution.py:54
  50.8 28.1 %all-to-all-start = ((f16[8,64,1792]{2,1,0:T(8,128)(2,1)}), f16[8,64,1792]{2,1,0:T(8,128)(2,1)S(1)}, u32[]{:S(2)}, u32[]{:S(2)}) async-start(f16[8,64,1792]{2,1,0:T(8,128)(2,1)} %bitcast.17), calls=%async_computation | async-start | bytes 3670016 | tf_op jit(solution)/shard_map/all_to_all | solution.py:102
  57.0 10.3 %collective-permute-start.14 = (bf16[32,2048]{1,0:T(8,128)(2,1)S(1)}, bf16[32,2048]{1,0:T(8,128)(2,1)S(1)}, u32[]{:S(2)}, u32[]{:S(2)}) collective-permute-start(bf16[32,2048]{1,0:T(8,128)(2,1)S(1)} %collective-permute-done.13), channel_id=1, source_target_pairs={{0,64},{32,96},{64,128},{96,160},{128,192},{160,224},{192,0},{224,... | collective-permute-start | bytes 393224 | tf_op jit(solution)/shard_map/ppermute | solution.py:54
  58.9 10.3 %collective-permute-start.15 = (bf16[32,2048]{1,0:T(8,128)(2,1)S(1)}, bf16[32,2048]{1,0:T(8,128)(2,1)S(1)}, u32[]{:S(2)}, u32[]{:S(2)}) collective-permute-start(bf16[32,2048]{1,0:T(8,128)(2,1)S(1)} %collective-permute-done.13), channel_id=1, source_target_pairs={{0,32},{32,64},{64,96},{96,128},{128,160},{160,192},{192,224},{224... | collective-permute-start | bytes 393224 | tf_op jit(solution)/shard_map/ppermute | solution.py:54
  113.1 29.4 %all-to-all-start.2 = ((bf16[8,64,1792]{2,1,0:T(8,128)(2,1)}), bf16[8,64,1792]{2,1,0:T(8,128)(2,1)}, u32[]{:S(2)}, u32[]{:S(2)}) async-start(bf16[8,64,1792]{2,1,0:T(8,128)(2,1)} %broadcast_in_dim.5), calls=%async_computation.2 | async-start | bytes 3670016 | tf_op jit(solution)/shard_map/all_to_all | solution.py:102
  120.4 11.8 %collective-permute-start.19 = (bf16[64,2048]{1,0:T(8,128)(2,1)S(1)}, bf16[64,2048]{1,0:T(8,128)(2,1)S(1)}, u32[]{:S(2)}, u32[]{:S(2)}) collective-permute-start(bf16[64,2048]{1,0:T(8,128)(2,1)S(1)} %pad_maximum_fusion.2), channel_id=1, source_target_pairs={{0,32},{32,64},{64,96},{96,128},{128,160},{160,192},{192,224},{224... | collective-permute-start | bytes 786440 | tf_op jit(solution)/shard_map/ppermute | solution.py:54
  120.8 11.5 %collective-permute-start.20 = (bf16[64,2048]{1,0:T(8,128)(2,1)S(1)}, bf16[64,2048]{1,0:T(8,128)(2,1)S(1)}, u32[]{:S(2)}, u32[]{:S(2)}) collective-permute-start(bf16[64,2048]{1,0:T(8,128)(2,1)S(1)} %pad_maximum_fusion.3), channel_id=1, source_target_pairs={{0,224},{32,0},{64,32},{96,64},{128,96},{160,128},{192,160},{224,1... | collective-permute-start | bytes 786440 | tf_op jit(solution)/shard_map/ppermute | solution.py:54
  123.8 8.5 %collective-permute-start.21 = (bf16[16,2048]{1,0:T(8,128)(2,1)S(1)}, bf16[16,2048]{1,0:T(8,128)(2,1)S(1)}, u32[]{:S(2)}, u32[]{:S(2)}) collective-permute-start(bf16[16,2048]{1,0:T(8,128)(2,1)S(1)} %get-tuple-element.45), channel_id=1, source_target_pairs={{0,64},{32,96},{64,128},{96,160},{128,192},{160,224},{192,0},{224,... | collective-permute-start | bytes 196616 | tf_op jit(solution)/shard_map/ppermute | solution.py:54
  123.9 8.4 %collective-permute-start.23 = (bf16[16,2048]{1,0:T(8,128)(2,1)S(1)}, bf16[16,2048]{1,0:T(8,128)(2,1)S(1)}, u32[]{:S(2)}, u32[]{:S(2)}) collective-permute-start(bf16[16,2048]{1,0:T(8,128)(2,1)S(1)} %get-tuple-element.44), channel_id=1, source_target_pairs={{0,192},{32,224},{64,0},{96,32},{128,64},{160,96},{192,128},{224,1... | collective-permute-start | bytes 196616 | tf_op jit(solution)/shard_map/ppermute | solution.py:54
  132.4 9.5 %collective-permute-start.22 = (bf16[32,2048]{1,0:T(8,128)(2,1)S(1)}, bf16[32,2048]{1,0:T(8,128)(2,1)S(1)}, u32[]{:S(2)}, u32[]{:S(2)}) collective-permute-start(bf16[32,2048]{1,0:T(8,128)(2,1)S(1)} %get-tuple-element.35), channel_id=1, source_target_pairs={{0,64},{32,96},{64,128},{96,160},{128,192},{160,224},{192,0},{224,... | collective-permute-start | bytes 393224 | tf_op jit(solution)/shard_map/ppermute | solution.py:54
  134.4 7.6 %collective-permute-start.24 = (bf16[32,2048]{1,0:T(8,128)(2,1)S(1)}, bf16[32,2048]{1,0:T(8,128)(2,1)S(1)}, u32[]{:S(2)}, u32[]{:S(2)}) collective-permute-start(bf16[32,2048]{1,0:T(8,128)(2,1)S(1)} %get-tuple-element.34), channel_id=1, source_target_pairs={{0,192},{32,224},{64,0},{96,32},{128,64},{160,96},{192,128},{224,1... | collective-permute-start | bytes 393224 | tf_op jit(solution)/shard_map/ppermute | solution.py:54
  152.6 10.5 %collective-permute-start.26 = (bf16[64,2048]{1,0:T(8,128)(2,1)S(1)}, bf16[64,2048]{1,0:T(8,128)(2,1)S(1)}, u32[]{:S(2)}, u32[]{:S(2)}) collective-permute-start(bf16[64,2048]{1,0:T(8,128)(2,1)S(1)} %pad_maximum_fusion.4), channel_id=1, source_target_pairs={{0,32},{32,64},{64,96},{96,128},{128,160},{160,192},{192,224},{224... | collective-permute-start | bytes 786440 | tf_op jit(solution)/shard_map/ppermute | solution.py:54
  154.6 9.5 %collective-permute-start.27 = (bf16[64,2048]{1,0:T(8,128)(2,1)S(1)}, bf16[64,2048]{1,0:T(8,128)(2,1)S(1)}, u32[]{:S(2)}, u32[]{:S(2)}) collective-permute-start(bf16[64,2048]{1,0:T(8,128)(2,1)S(1)} %pad_maximum_fusion.5), channel_id=1, source_target_pairs={{0,224},{32,0},{64,32},{96,64},{128,96},{160,128},{192,160},{224,1... | collective-permute-start | bytes 786440 | tf_op jit(solution)/shard_map/ppermute | solution.py:54
  156.2 10.5 %collective-permute-start.28 = (bf16[16,2048]{1,0:T(8,128)(2,1)S(1)}, bf16[16,2048]{1,0:T(8,128)(2,1)S(1)}, u32[]{:S(2)}, u32[]{:S(2)}) collective-permute-start(bf16[16,2048]{1,0:T(8,128)(2,1)S(1)} %get-tuple-element.38), channel_id=1, source_target_pairs={{0,64},{32,96},{64,128},{96,160},{128,192},{160,224},{192,0},{224,... | collective-permute-start | bytes 196616 | tf_op jit(solution)/shard_map/ppermute | solution.py:54
  157.5 9.1 %collective-permute-start.30 = (bf16[16,2048]{1,0:T(8,128)(2,1)S(1)}, bf16[16,2048]{1,0:T(8,128)(2,1)S(1)}, u32[]{:S(2)}, u32[]{:S(2)}) collective-permute-start(bf16[16,2048]{1,0:T(8,128)(2,1)S(1)} %get-tuple-element.39), channel_id=1, source_target_pairs={{0,192},{32,224},{64,0},{96,32},{128,64},{160,96},{192,128},{224,1... | collective-permute-start | bytes 196616 | tf_op jit(solution)/shard_map/ppermute | solution.py:54
  166.7 7.9 %collective-permute-start.29 = (bf16[32,2048]{1,0:T(8,128)(2,1)S(1)}, bf16[32,2048]{1,0:T(8,128)(2,1)S(1)}, u32[]{:S(2)}, u32[]{:S(2)}) collective-permute-start(bf16[32,2048]{1,0:T(8,128)(2,1)S(1)} %get-tuple-element.32), channel_id=1, source_target_pairs={{0,64},{32,96},{64,128},{96,160},{128,192},{160,224},{192,0},{224,... | collective-permute-start | bytes 393224 | tf_op jit(solution)/shard_map/ppermute | solution.py:54
  (16 other events, 87.5 us)

commit v5 on v4

--- a/solution.py
+++ b/solution.py
@@ -59,6 +59,7 @@
     got = {0: pair}
     for r in (2, -2, 1, -1):
         got[r] = shift(pair, r)
+    got = lax.optimization_barrier(got)
     got[3], got[-3] = shift(got[2], 1), shift(got[-2], -1)
     if even:
         got[4] = jnp.concatenate([shift(got[2][:half], 2), shift(got[-2][half:], -2)])
@@ -92,10 +93,13 @@
     return total + seconds[0].astype(F32) + seconds[1].astype(F32)
 
 
-def last_round(sums):
-    rows = sums[0].shape[0] // 2
-    come = swap(jnp.concatenate([x[rows:] for x in sums]).astype(BF), "xh").astype(F32)
-    return [(x[:rows] + come[i * rows : (i + 1) * rows]).astype(BF) for i, x in enumerate(sums)]
+def halves(total):
+    rows = total.shape[0] // 2
+    return total[:rows], swap(total[rows:].astype(BF), "xh")
+
+
+def joined(kept, come):
+    return (kept + come.astype(F32)).astype(BF)
 
 
 def exchange(x):
@@ -144,12 +148,11 @@
     kept, sent = product(hidden, down_weight, False, (F32, BF), 512)
     total, seconds = first_round(kept + swap(sent, "core").astype(F32))
     seconds, grads = lax.optimization_barrier((second_round(seconds), grads))
-    total = added(total, seconds)
+    kept, come = halves(added(total, seconds))
     out = lax.dot_general(grads, weights, LAST, preferred_element_type=F32)
-    out = out[:half] + swap(out[half:].astype(BF), "core").astype(F32)
-    last, seconds = first_round(out)
-    block_out, grad_tokens = last_round([total, added(last, second_round(seconds))])
-    return block_out, grad_tokens
+    sent, come = lax.optimization_barrier((swap(out[half:].astype(BF), "core"), come))
+    total, seconds = first_round(out[:half] + sent.astype(F32))
+    return joined(kept, come), joined(*halves(added(total, second_round(seconds))))
 
 
 def solution(mesh):

time: 185 us -> 199 us (1.076)
  waiting for transfers between devices: 53.4 us -> 63.7 us
  matrix products: 11.9 us -> 15.2 us
  starting transfers between devices: 67.5 us -> 65.1 us
    ppermute x27, waiting for transfers between devices: 35.7 us -> 46.4 us  [shift(): return lax.ppermute(x, 'z', [(i, (i - by) % NZ) for i in range(NZ)])]
    ppermute x27, starting transfers between devices: 52.5 us -> 48 us  [shift(): return lax.ppermute(x, 'z', [(i, (i - by) % NZ) for i in range(NZ)])]
    dot_general x1, matrix products: 5.09 us -> 8.35 us  [per_device(): jnp.dot(tok, weights, preferred_element_type=F32) * SCALE]
    ppermute x6 -> x7, starting transfers between devices: 3.35 us -> 5.53 us  [swap(): return lax.ppermute(x, axis, SWAP)]
    ppermute x6 -> x7, waiting for transfers between devices: 14.9 us -> 16.3 us  [swap(): return lax.ppermute(x, axis, SWAP)]
    unnamed x26 -> x28, local copies, waits for them, and re-layouts: 8.83 us -> 9.12 us
  transfers between devices with their start and end apart: 35 -> 36, of which waited for: 21 -> 22; matrix products, arithmetic and copies ran while one was open for 5% -> 4% of each run, Pallas kernels for 1% -> 1%
where the time goes in v5:
time: 199 us; the launch traced here: 198 us
  starting transfers between devices  65.1 us (33%)
  waiting for transfers between devices  63.7 us (32%)
  blocking collectives  27.7 us (14%)
  matrix products  15.2 us (8%)
  local copies, waits for them, and re-layouts  12.3 us (6%)
  other arithmetic  7.34 us (4%)
  Pallas kernels  5.68 us (3%)
    ppermute x27, starting transfers between devices, shift(): return lax.ppermute(x, 'z', [(i, (i - by) % NZ) for i in range(NZ)])  48 us
    ppermute x27, waiting for transfers between devices, shift(): return lax.ppermute(x, 'z', [(i, (i - by) % NZ) for i in range(NZ)])  46.4 us
    all_to_all x1, blocking collectives, exchange(): return lax.all_to_all(x, COL, 0, 0, tiled=True)  27.7 us
    ppermute x7, waiting for transfers between devices, swap(): return lax.ppermute(x, axis, SWAP)  16.3 us
    all_to_all x2, starting transfers between devices, exchange(): return lax.all_to_all(x, COL, 0, 0, tiled=True)  11.6 us
    unnamed x28, local copies, waits for them, and re-layouts  9.12 us
    dot_general x1, matrix products, per_device(): jnp.dot(tok, weights, preferred_element_type=F32) * SCALE  8.35 us
    dot_general x1, matrix products, per_device(): out = lax.dot_general(grads, weights, LAST, preferred_element_type=F32)  6.82 us
  transfers between devices with their start and end apart: 36, of which 22 were waited for; matrix products, arithmetic and copies ran while one was open for 4% of the time, Pallas kernels for 1%

profile of v5, /device:TPU:6, one launch (start us, length us, event | category | flops | bytes accessed | tf_op | source)
XLA Modules:
  0.0 198.1 jit_solution(751368906612618468)
XLA Ops:
  3.0 5.3 %collective-permute-done = bf16[32,2048]{1,0:T(8,128)(2,1)S(1)} collective-permute-done((bf16[32,2048]{1,0:T(8,128)(2,1)S(1)}, bf16[32,2048]{1,0:T(8,128)(2,1)S(1)}, u32[]{:S(2)}, u32[]{:S(2)}) %collective-permute-start) | collective-permute-done | bytes 131104 | tf_op jit(solution)/shard_map/ppermute | solution.py:50
  9.2 3.3 %collective-permute-start.1 = (bf16[32,2048]{1,0:T(8,128)(2,1)S(1)}, bf16[32,2048]{1,0:T(8,128)(2,1)S(1)}, u32[]{:S(2)}, u32[]{:S(2)}) collective-permute-start(bf16[32,2048]{1,0:T(8,128)(2,1)S(1)} %pad_maximum_fusion.8), channel_id=1, source_target_pairs={{0,64},{32,96},{64,128},{96,160},{128,192},{160,224},{192,0},{224,... | collective-permute-start | bytes 393224 | tf_op jit(solution)/shard_map/ppermute | solution.py:54
  18.1 4.3 %collective-permute-done.1 = bf16[32,2048]{1,0:T(8,128)(2,1)S(1)} collective-permute-done((bf16[32,2048]{1,0:T(8,128)(2,1)S(1)}, bf16[32,2048]{1,0:T(8,128)(2,1)S(1)}, u32[]{:S(2)}, u32[]{:S(2)}) %collective-permute-start.1) | collective-permute-done | bytes 131104 | tf_op jit(solution)/shard_map/ppermute | solution.py:54
  23.4 3.5 %collective-permute-done.4 = bf16[32,2048]{1,0:T(8,128)(2,1)S(1)} collective-permute-done((bf16[32,2048]{1,0:T(8,128)(2,1)S(1)}, bf16[32,2048]{1,0:T(8,128)(2,1)S(1)}, u32[]{:S(2)}, u32[]{:S(2)}) %collective-permute-start.4) | collective-permute-done | bytes 131104 | tf_op jit(solution)/shard_map/ppermute | solution.py:54
  38.4 4.6 %copy.6 = bf16[256,8,2,896]{3,1,2,0:T(8,128)(2,1)S(1)} copy(bf16[256,8,2,896]{3,2,1,0:T(2,128)(2,1)} %bitcast.13) | data formatting | bytes 14680064
  44.3 8.4 %multiply_convert_fusion = f16[512,1792]{1,0:T(8,128)(2,1)} fusion(bf16[512,2048]{1,0:T(8,128)(2,1)} %constant_dynamic-update-slice_fusion.9, bf16[2048,1792]{1,0:T(8,128)(2,1)S(1)} %bitcast.14), kind=kOutput, calls=%fused_computation.1 | convolution fusion | flops 3759931392 | bytes 11272192 | tf_op jit(solution)/shard_map/dot_general | solution.py:124
  58.8 5.9 %all-to-all-start = ((f16[8,64,1792]{2,1,0:T(8,128)(2,1)}), f16[8,64,1792]{2,1,0:T(8,128)(2,1)S(1)}, u32[]{:S(2)}, u32[]{:S(2)}) async-start(f16[8,64,1792]{2,1,0:T(8,128)(2,1)} %bitcast.17), calls=%async_computation | async-start | bytes 3670016 | tf_op jit(solution)/shard_map/all_to_all | solution.py:106
  68.0 2.8 %collective-permute-start.15 = (bf16[32,2048]{1,0:T(8,128)(2,1)S(1)}, bf16[32,2048]{1,0:T(8,128)(2,1)S(1)}, u32[]{:S(2)}, u32[]{:S(2)}) collective-permute-start(bf16[32,2048]{1,0:T(8,128)(2,1)S(1)} %collective-permute-done.10), channel_id=1, source_target_pairs={{0,64},{32,96},{64,128},{96,160},{128,192},{160,224},{192,0},{224,... | collective-permute-start | bytes 393224 | tf_op jit(solution)/shard_map/ppermute | solution.py:54
  70.8 3.3 %collective-permute-start.14 = (bf16[32,2048]{1,0:T(8,128)(2,1)S(1)}, bf16[32,2048]{1,0:T(8,128)(2,1)S(1)}, u32[]{:S(2)}, u32[]{:S(2)}) collective-permute-start(bf16[32,2048]{1,0:T(8,128)(2,1)S(1)} %collective-permute-done.13), channel_id=1, source_target_pairs={{0,224},{32,0},{64,32},{96,64},{128,96},{160,128},{192,160},{224,1... | collective-permute-start | bytes 393224 | tf_op jit(solution)/shard_map/ppermute | solution.py:54
  86.9 27.7 %all_to_all.15 = bf16[8,128,896]{2,1,0:T(8,128)(2,1)S(1)} all-to-all(bf16[8,128,896]{2,1,0:T(8,128)(2,1)S(1)} %pad_maximum_fusion), channel_id=1, replica_groups=mesh['z'=8,'xh'=2,'core'=2,'xl'=2,'y'=4] {'xl','y'}, dimensions={0} | all-to-all | bytes 3670016 | tf_op jit(solution)/shard_map/all_to_all | solution.py:106
  117.6 3.3 %shard_map.60 = (f32[256,2048]{1,0:T(8,128)S(1)}, bf16[256,2048]{1,0:T(8,128)(2,1)S(1)}) custom-call(bf16[256,896]{1,0:T(8,128)(2,1)S(1)} %bitcast.12, bf16[256,896]{1,0:T(8,128)(2,1)S(1)} %bitcast.11, bf16[896,2048]{1,0:T(8,128)(2,1)S(1)} %copy-done.1), custom_call_target="tpu_custom_call" | custom-call | flops 512 | bytes 458752 | tf_op jit(solution)/shard_map/pallas_call | solution.py:35
  121.0 5.6 %all-to-all-start.2 = ((bf16[8,64,1792]{2,1,0:T(8,128)(2,1)}), bf16[8,64,1792]{2,1,0:T(8,128)(2,1)}, u32[]{:S(2)}, u32[]{:S(2)}) async-start(bf16[8,64,1792]{2,1,0:T(8,128)(2,1)} %broadcast_in_dim.5), calls=%async_computation.2 | async-start | bytes 3670016 | tf_op jit(solution)/shard_map/all_to_all | solution.py:106
  134.2 4.8 %collective-permute-done.20 = bf16[64,2048]{1,0:T(8,128)(2,1)S(1)} collective-permute-done((bf16[64,2048]{1,0:T(8,128)(2,1)S(1)}, bf16[64,2048]{1,0:T(8,128)(2,1)S(1)}, u32[]{:S(2)}, u32[]{:S(2)}) %collective-permute-start.20) | collective-permute-done | bytes 262176 | tf_op jit(solution)/shard_map/ppermute | solution.py:54
  139.0 3.6 %collective-permute-done.19 = bf16[64,2048]{1,0:T(8,128)(2,1)S(1)} collective-permute-done((bf16[64,2048]{1,0:T(8,128)(2,1)S(1)}, bf16[64,2048]{1,0:T(8,128)(2,1)S(1)}, u32[]{:S(2)}, u32[]{:S(2)}) %collective-permute-start.19) | collective-permute-done | bytes 262176 | tf_op jit(solution)/shard_map/ppermute | solution.py:54
  143.6 3.4 %collective-permute-start.24 = (bf16[32,2048]{1,0:T(8,128)(2,1)S(1)}, bf16[32,2048]{1,0:T(8,128)(2,1)S(1)}, u32[]{:S(2)}, u32[]{:S(2)}) collective-permute-start(bf16[32,2048]{1,0:T(8,128)(2,1)S(1)} %get-tuple-element.58), channel_id=1, source_target_pairs={{0,192},{32,224},{64,0},{96,32},{128,64},{160,96},{192,128},{224,1... | collective-permute-start | bytes 393224 | tf_op jit(solution)/shard_map/ppermute | solution.py:54
  147.0 3.0 %collective-permute-done.22 = bf16[32,2048]{1,0:T(8,128)(2,1)S(1)} collective-permute-done((bf16[32,2048]{1,0:T(8,128)(2,1)S(1)}, bf16[32,2048]{1,0:T(8,128)(2,1)S(1)}, u32[]{:S(2)}, u32[]{:S(2)}) %collective-permute-start.22) | collective-permute-done | bytes 131104 | tf_op jit(solution)/shard_map/ppermute | solution.py:54
  151.4 6.8 %fusion.22 = f32[512,2048]{1,0:T(8,128)S(1)} fusion(bf16[512,1792]{1,0:T(8,128)(2,1)} %bitcast.4, bf16[2048,1792]{1,0:T(8,128)(2,1)} %bitcast.15), kind=kOutput, calls=%fused_computation.82 | convolution fusion | flops 3758096384 | bytes 13369344 | tf_op jit(solution)/shard_map/dot_general | solution.py:152
  161.3 4.6 %collective-permute-done.26 = bf16[16,2048]{1,0:T(8,128)(2,1)S(1)} collective-permute-done((bf16[16,2048]{1,0:T(8,128)(2,1)S(1)}, bf16[16,2048]{1,0:T(8,128)(2,1)S(1)}, u32[]{:S(2)}, u32[]{:S(2)}) %collective-permute-start.26) | collective-permute-done | bytes 65568 | tf_op jit(solution)/shard_map/ppermute | solution.py:50
  166.3 4.4 %collective-permute-start.28 = (bf16[64,2048]{1,0:T(8,128)(2,1)S(1)}, bf16[64,2048]{1,0:T(8,128)(2,1)S(1)}, u32[]{:S(2)}, u32[]{:S(2)}) collective-permute-start(bf16[64,2048]{1,0:T(8,128)(2,1)S(1)} %pad_maximum_fusion.5), channel_id=1, source_target_pairs={{0,224},{32,0},{64,32},{96,64},{128,96},{160,128},{192,160},{224,1... | collective-permute-start | bytes 786440 | tf_op jit(solution)/shard_map/ppermute | solution.py:54
  175.1 3.2 %collective-permute-done.28 = bf16[64,2048]{1,0:T(8,128)(2,1)S(1)} collective-permute-done((bf16[64,2048]{1,0:T(8,128)(2,1)S(1)}, bf16[64,2048]{1,0:T(8,128)(2,1)S(1)}, u32[]{:S(2)}, u32[]{:S(2)}) %collective-permute-start.28) | collective-permute-done | bytes 262176 | tf_op jit(solution)/shard_map/ppermute | solution.py:54
  178.4 3.4 %collective-permute-done.27 = bf16[64,2048]{1,0:T(8,128)(2,1)S(1)} collective-permute-done((bf16[64,2048]{1,0:T(8,128)(2,1)S(1)}, bf16[64,2048]{1,0:T(8,128)(2,1)S(1)}, u32[]{:S(2)}, u32[]{:S(2)}) %collective-permute-start.27) | collective-permute-done | bytes 262176 | tf_op jit(solution)/shard_map/ppermute | solution.py:54
  185.0 3.1 %collective-permute-done.32 = bf16[32,2048]{1,0:T(8,128)(2,1)S(1)} collective-permute-done((bf16[32,2048]{1,0:T(8,128)(2,1)S(1)}, bf16[32,2048]{1,0:T(8,128)(2,1)S(1)}, u32[]{:S(2)}, u32[]{:S(2)}) %collective-permute-start.32) | collective-permute-done | bytes 131104 | tf_op jit(solution)/shard_map/ppermute | solution.py:54
  188.1 3.5 %collective-permute-done.30 = bf16[32,2048]{1,0:T(8,128)(2,1)S(1)} collective-permute-done((bf16[32,2048]{1,0:T(8,128)(2,1)S(1)}, bf16[32,2048]{1,0:T(8,128)(2,1)S(1)}, u32[]{:S(2)}, u32[]{:S(2)}) %collective-permute-start.30) | collective-permute-done | bytes 131104 | tf_op jit(solution)/shard_map/ppermute | solution.py:54
  193.8 3.7 %collective-permute-done.33 = bf16[16,2048]{1,0:T(8,128)(2,1)S(1)} collective-permute-done((bf16[16,2048]{1,0:T(8,128)(2,1)S(1)}, bf16[16,2048]{1,0:T(8,128)(2,1)S(1)}, u32[]{:S(2)}, u32[]{:S(2)}) %collective-permute-start.33) | collective-permute-done | bytes 65568 | tf_op jit(solution)/shard_map/ppermute | solution.py:50
  (124 shorter events, 71.3 us)
Async XLA Ops:
  9.2 13.1 %collective-permute-start.1 = (bf16[32,2048]{1,0:T(8,128)(2,1)S(1)}, bf16[32,2048]{1,0:T(8,128)(2,1)S(1)}, u32[]{:S(2)}, u32[]{:S(2)}) collective-permute-start(bf16[32,2048]{1,0:T(8,128)(2,1)S(1)} %pad_maximum_fusion.8), channel_id=1, source_target_pairs={{0,64},{32,96},{64,128},{96,160},{128,192},{160,224},{192,0},{224,... | collective-permute-start | bytes 393224 | tf_op jit(solution)/shard_map/ppermute | solution.py:54
  12.6 10.8 %collective-permute-start.2 = (bf16[32,2048]{1,0:T(8,128)(2,1)S(1)}, bf16[32,2048]{1,0:T(8,128)(2,1)S(1)}, u32[]{:S(2)}, u32[]{:S(2)}) collective-permute-start(bf16[32,2048]{1,0:T(8,128)(2,1)S(1)} %pad_maximum_fusion.8), channel_id=1, source_target_pairs={{0,32},{32,64},{64,96},{96,128},{128,160},{160,192},{192,224},{224... | collective-permute-start | bytes 393224 | tf_op jit(solution)/shard_map/ppermute | solution.py:54
  14.5 8.9 %collective-permute-start.3 = (bf16[32,2048]{1,0:T(8,128)(2,1)S(1)}, bf16[32,2048]{1,0:T(8,128)(2,1)S(1)}, u32[]{:S(2)}, u32[]{:S(2)}) collective-permute-start(bf16[32,2048]{1,0:T(8,128)(2,1)S(1)} %pad_maximum_fusion.8), channel_id=1, source_target_pairs={{0,224},{32,0},{64,32},{96,64},{128,96},{160,128},{192,160},{224,1... | collective-permute-start | bytes 393224 | tf_op jit(solution)/shard_map/ppermute | solution.py:54
  15.8 11.1 %collective-permute-start.4 = (bf16[32,2048]{1,0:T(8,128)(2,1)S(1)}, bf16[32,2048]{1,0:T(8,128)(2,1)S(1)}, u32[]{:S(2)}, u32[]{:S(2)}) collective-permute-start(bf16[32,2048]{1,0:T(8,128)(2,1)S(1)} %pad_maximum_fusion.8), channel_id=1, source_target_pairs={{0,192},{32,224},{64,0},{96,32},{128,64},{160,96},{192,128},{224,1... | collective-permute-start | bytes 393224 | tf_op jit(solution)/shard_map/ppermute | solution.py:54
  26.9 10.0 %collective-permute-start.8 = (bf16[32,2048]{1,0:T(8,128)(2,1)S(1)}, bf16[32,2048]{1,0:T(8,128)(2,1)S(1)}, u32[]{:S(2)}, u32[]{:S(2)}) collective-permute-start(bf16[32,2048]{1,0:T(8,128)(2,1)S(1)} %collective-permute-done.1), channel_id=1, source_target_pairs={{0,32},{32,64},{64,96},{96,128},{128,160},{160,192},{192,224},{224... | collective-permute-start | bytes 393224 | tf_op jit(solution)/shard_map/ppermute | solution.py:54
  52.6 12.1 %collective-permute-start.10 = (bf16[32,2048]{1,0:T(8,128)(2,1)S(1)}, bf16[32,2048]{1,0:T(8,128)(2,1)S(1)}, u32[]{:S(2)}, u32[]{:S(2)}) collective-permute-start(bf16[32,2048]{1,0:T(8,128)(2,1)S(1)} %pad_maximum_fusion.9), channel_id=1, source_target_pairs={{0,64},{32,96},{64,128},{96,160},{128,192},{160,224},{192,0},{224,... | collective-permute-start | bytes 393224 | tf_op jit(solution)/shard_map/ppermute | solution.py:54
  53.3 11.9 %collective-permute-start.11 = (bf16[32,2048]{1,0:T(8,128)(2,1)S(1)}, bf16[32,2048]{1,0:T(8,128)(2,1)S(1)}, u32[]{:S(2)}, u32[]{:S(2)}) collective-permute-start(bf16[32,2048]{1,0:T(8,128)(2,1)S(1)} %pad_maximum_fusion.9), channel_id=1, source_target_pairs={{0,32},{32,64},{64,96},{96,128},{128,160},{160,192},{192,224},{224... | collective-permute-start | bytes 393224 | tf_op jit(solution)/shard_map/ppermute | solution.py:54
  55.5 9.7 %collective-permute-start.12 = (bf16[32,2048]{1,0:T(8,128)(2,1)S(1)}, bf16[32,2048]{1,0:T(8,128)(2,1)S(1)}, u32[]{:S(2)}, u32[]{:S(2)}) collective-permute-start(bf16[32,2048]{1,0:T(8,128)(2,1)S(1)} %pad_maximum_fusion.9), channel_id=1, source_target_pairs={{0,224},{32,0},{64,32},{96,64},{128,96},{160,128},{192,160},{224,1... | collective-permute-start | bytes 393224 | tf_op jit(solution)/shard_map/ppermute | solution.py:54
  57.3 10.7 %collective-permute-start.13 = (bf16[32,2048]{1,0:T(8,128)(2,1)S(1)}, bf16[32,2048]{1,0:T(8,128)(2,1)S(1)}, u32[]{:S(2)}, u32[]{:S(2)}) collective-permute-start(bf16[32,2048]{1,0:T(8,128)(2,1)S(1)} %pad_maximum_fusion.9), channel_id=1, source_target_pairs={{0,192},{32,224},{64,0},{96,32},{128,64},{160,96},{192,128},{224,1... | collective-permute-start | bytes 393224 | tf_op jit(solution)/shard_map/ppermute | solution.py:54
  58.8 27.4 %all-to-all-start = ((f16[8,64,1792]{2,1,0:T(8,128)(2,1)}), f16[8,64,1792]{2,1,0:T(8,128)(2,1)S(1)}, u32[]{:S(2)}, u32[]{:S(2)}) async-start(f16[8,64,1792]{2,1,0:T(8,128)(2,1)} %bitcast.17), calls=%async_computation | async-start | bytes 3670016 | tf_op jit(solution)/shard_map/all_to_all | solution.py:106
  68.0 8.7 %collective-permute-start.15 = (bf16[32,2048]{1,0:T(8,128)(2,1)S(1)}, bf16[32,2048]{1,0:T(8,128)(2,1)S(1)}, u32[]{:S(2)}, u32[]{:S(2)}) collective-permute-start(bf16[32,2048]{1,0:T(8,128)(2,1)S(1)} %collective-permute-done.10), channel_id=1, source_target_pairs={{0,64},{32,96},{64,128},{96,160},{128,192},{160,224},{192,0},{224,... | collective-permute-start | bytes 393224 | tf_op jit(solution)/shard_map/ppermute | solution.py:54
  121.0 30.4 %all-to-all-start.2 = ((bf16[8,64,1792]{2,1,0:T(8,128)(2,1)}), bf16[8,64,1792]{2,1,0:T(8,128)(2,1)}, u32[]{:S(2)}, u32[]{:S(2)}) async-start(bf16[8,64,1792]{2,1,0:T(8,128)(2,1)} %broadcast_in_dim.5), calls=%async_computation.2 | async-start | bytes 3670016 | tf_op jit(solution)/shard_map/all_to_all | solution.py:106
  128.4 10.6 %collective-permute-start.20 = (bf16[64,2048]{1,0:T(8,128)(2,1)S(1)}, bf16[64,2048]{1,0:T(8,128)(2,1)S(1)}, u32[]{:S(2)}, u32[]{:S(2)}) collective-permute-start(bf16[64,2048]{1,0:T(8,128)(2,1)S(1)} %pad_maximum_fusion.3), channel_id=1, source_target_pairs={{0,224},{32,0},{64,32},{96,64},{128,96},{160,128},{192,160},{224,1... | collective-permute-start | bytes 786440 | tf_op jit(solution)/shard_map/ppermute | solution.py:54
  131.1 11.5 %collective-permute-start.19 = (bf16[64,2048]{1,0:T(8,128)(2,1)S(1)}, bf16[64,2048]{1,0:T(8,128)(2,1)S(1)}, u32[]{:S(2)}, u32[]{:S(2)}) collective-permute-start(bf16[64,2048]{1,0:T(8,128)(2,1)S(1)} %pad_maximum_fusion.2), channel_id=1, source_target_pairs={{0,32},{32,64},{64,96},{96,128},{128,160},{160,192},{192,224},{224... | collective-permute-start | bytes 786440 | tf_op jit(solution)/shard_map/ppermute | solution.py:54
  131.2 11.5 %collective-permute-start.23 = (bf16[16,2048]{1,0:T(8,128)(2,1)S(1)}, bf16[16,2048]{1,0:T(8,128)(2,1)S(1)}, u32[]{:S(2)}, u32[]{:S(2)}) collective-permute-start(bf16[16,2048]{1,0:T(8,128)(2,1)S(1)} %get-tuple-element.68), channel_id=1, source_target_pairs={{0,192},{32,224},{64,0},{96,32},{128,64},{160,96},{192,128},{224,1... | collective-permute-start | bytes 196616 | tf_op jit(solution)/shard_map/ppermute | solution.py:54
  133.8 8.8 %collective-permute-start.21 = (bf16[16,2048]{1,0:T(8,128)(2,1)S(1)}, bf16[16,2048]{1,0:T(8,128)(2,1)S(1)}, u32[]{:S(2)}, u32[]{:S(2)}) collective-permute-start(bf16[16,2048]{1,0:T(8,128)(2,1)S(1)} %get-tuple-element.69), channel_id=1, source_target_pairs={{0,64},{32,96},{64,128},{96,160},{128,192},{160,224},{192,0},{224,... | collective-permute-start | bytes 196616 | tf_op jit(solution)/shard_map/ppermute | solution.py:54
  142.8 7.3 %collective-permute-start.22 = (bf16[32,2048]{1,0:T(8,128)(2,1)S(1)}, bf16[32,2048]{1,0:T(8,128)(2,1)S(1)}, u32[]{:S(2)}, u32[]{:S(2)}) collective-permute-start(bf16[32,2048]{1,0:T(8,128)(2,1)S(1)} %get-tuple-element.59), channel_id=1, source_target_pairs={{0,64},{32,96},{64,128},{96,160},{128,192},{160,224},{192,0},{224,... | collective-permute-start | bytes 393224 | tf_op jit(solution)/shard_map/ppermute | solution.py:54
  143.6 7.8 %collective-permute-start.24 = (bf16[32,2048]{1,0:T(8,128)(2,1)S(1)}, bf16[32,2048]{1,0:T(8,128)(2,1)S(1)}, u32[]{:S(2)}, u32[]{:S(2)}) collective-permute-start(bf16[32,2048]{1,0:T(8,128)(2,1)S(1)} %get-tuple-element.58), channel_id=1, source_target_pairs={{0,192},{32,224},{64,0},{96,32},{128,64},{160,96},{192,128},{224,1... | collective-permute-start | bytes 393224 | tf_op jit(solution)/shard_map/ppermute | solution.py:54
  158.4 7.5 %collective-permute-start.25 = (bf16[256,2048]{1,0:T(8,128)(2,1)S(1)}, bf16[256,2048]{1,0:T(8,128)(2,1)S(1)}, u32[]{:S(2)}, u32[]{:S(2)}) collective-permute-start(bf16[256,2048]{1,0:T(8,128)(2,1)S(1)} %slice.302), channel_id=1, source_target_pairs={{0,8},{8,0},{1,9},{9,1},{2,10},{10,2},{3,11},{11,3},{4,12},{12,4},... | collective-permute-start | bytes 3145736 | tf_op jit(solution)/shard_map/ppermute | solution.py:50
  166.3 12.0 %collective-permute-start.28 = (bf16[64,2048]{1,0:T(8,128)(2,1)S(1)}, bf16[64,2048]{1,0:T(8,128)(2,1)S(1)}, u32[]{:S(2)}, u32[]{:S(2)}) collective-permute-start(bf16[64,2048]{1,0:T(8,128)(2,1)S(1)} %pad_maximum_fusion.5), channel_id=1, source_target_pairs={{0,224},{32,0},{64,32},{96,64},{128,96},{160,128},{192,160},{224,1... | collective-permute-start | bytes 786440 | tf_op jit(solution)/shard_map/ppermute | solution.py:54
  170.8 11.0 %collective-permute-start.27 = (bf16[64,2048]{1,0:T(8,128)(2,1)S(1)}, bf16[64,2048]{1,0:T(8,128)(2,1)S(1)}, u32[]{:S(2)}, u32[]{:S(2)}) collective-permute-start(bf16[64,2048]{1,0:T(8,128)(2,1)S(1)} %pad_maximum_fusion.4), channel_id=1, source_target_pairs={{0,32},{32,64},{64,96},{96,128},{128,160},{160,192},{192,224},{224... | collective-permute-start | bytes 786440 | tf_op jit(solution)/shard_map/ppermute | solution.py:54
  170.9 11.0 %collective-permute-start.29 = (bf16[16,2048]{1,0:T(8,128)(2,1)S(1)}, bf16[16,2048]{1,0:T(8,128)(2,1)S(1)}, u32[]{:S(2)}, u32[]{:S(2)}) collective-permute-start(bf16[16,2048]{1,0:T(8,128)(2,1)S(1)} %get-tuple-element.62), channel_id=1, source_target_pairs={{0,64},{32,96},{64,128},{96,160},{128,192},{160,224},{192,0},{224,... | collective-permute-start | bytes 196616 | tf_op jit(solution)/shard_map/ppermute | solution.py:54
  173.1 8.8 %collective-permute-start.31 = (bf16[16,2048]{1,0:T(8,128)(2,1)S(1)}, bf16[16,2048]{1,0:T(8,128)(2,1)S(1)}, u32[]{:S(2)}, u32[]{:S(2)}) collective-permute-start(bf16[16,2048]{1,0:T(8,128)(2,1)S(1)} %get-tuple-element.63), channel_id=1, source_target_pairs={{0,192},{32,224},{64,0},{96,32},{128,64},{160,96},{192,128},{224,1... | collective-permute-start | bytes 196616 | tf_op jit(solution)/shard_map/ppermute | solution.py:54
  183.7 7.8 %collective-permute-start.30 = (bf16[32,2048]{1,0:T(8,128)(2,1)S(1)}, bf16[32,2048]{1,0:T(8,128)(2,1)S(1)}, u32[]{:S(2)}, u32[]{:S(2)}) collective-permute-start(bf16[32,2048]{1,0:T(8,128)(2,1)S(1)} %get-tuple-element.56), channel_id=1, source_target_pairs={{0,64},{32,96},{64,128},{96,160},{128,192},{160,224},{192,0},{224,... | collective-permute-start | bytes 393224 | tf_op jit(solution)/shard_map/ppermute | solution.py:54
  (18 other events, 104.6 us)

commit v6 on v4

--- a/solution.py
+++ b/solution.py
@@ -126,7 +126,6 @@
         product([grad, swap(grad, "core")], down_weight, True, (BF, BF), width)
     ).reshape(8, chunk, width)
 
-    both, part = lax.optimization_barrier((both, part))
     both = both.astype(F32).sum(0) * (1.0 / SCALE)
     gate, up = both[:, :width], both[:, width:]
     squash = jax.nn.sigmoid(gate)

time: 185 us -> 185 us (level)
    unnamed x26 -> x27, local copies, waits for them, and re-layouts: 8.83 us -> 8.85 us
where the time goes in v6:
time: 185 us; the launch traced here: 184 us
  starting transfers between devices  67.5 us (36%)
  waiting for transfers between devices  53.4 us (29%)
  blocking collectives  27.1 us (15%)
  matrix products  11.9 us (6%)
  local copies, waits for them, and re-layouts  10.9 us (6%)
  other arithmetic  6.77 us (4%)
  Pallas kernels  5.68 us (3%)
    ppermute x27, starting transfers between devices, shift(): return lax.ppermute(x, 'z', [(i, (i - by) % NZ) for i in range(NZ)])  52.5 us
    ppermute x27, waiting for transfers between devices, shift(): return lax.ppermute(x, 'z', [(i, (i - by) % NZ) for i in range(NZ)])  35.7 us
    all_to_all x1, blocking collectives, exchange(): return lax.all_to_all(x, COL, 0, 0, tiled=True)  27.1 us
    ppermute x6, waiting for transfers between devices, swap(): return lax.ppermute(x, axis, SWAP)  14.9 us
    all_to_all x2, starting transfers between devices, exchange(): return lax.all_to_all(x, COL, 0, 0, tiled=True)  11.6 us
    unnamed x27, local copies, waits for them, and re-layouts  8.85 us
    dot_general x1, matrix products, per_device(): out = lax.dot_general(grads, weights, LAST, preferred_element_type=F32)  6.82 us
    pallas_call x2, Pallas kernels, product(): pl.pallas_call(body, grid=(n // width,), in_specs=[pl.BlockSpec(x.shape,...  5.68 us
  transfers between devices with their start and end apart: 35, of which 21 were waited for; matrix products, arithmetic and copies ran while one was open for 5% of the time, Pallas kernels for 1%

profile of v6, /device:TPU:6, one launch (start us, length us, event | category | flops | bytes accessed | tf_op | source)
XLA Modules:
  0.0 184.3 jit_solution(2880807789722448519)
XLA Ops:
  3.9 4.5 %collective-permute-done = bf16[32,2048]{1,0:T(8,128)(2,1)S(1)} collective-permute-done((bf16[32,2048]{1,0:T(8,128)(2,1)S(1)}, bf16[32,2048]{1,0:T(8,128)(2,1)S(1)}, u32[]{:S(2)}, u32[]{:S(2)}) %collective-permute-start) | collective-permute-done | bytes 131104 | tf_op jit(solution)/shard_map/ppermute | solution.py:50
  9.2 6.4 %collective-permute-start.2 = (bf16[32,2048]{1,0:T(8,128)(2,1)S(1)}, bf16[32,2048]{1,0:T(8,128)(2,1)S(1)}, u32[]{:S(2)}, u32[]{:S(2)}) collective-permute-start(bf16[32,2048]{1,0:T(8,128)(2,1)S(1)} %pad_maximum_fusion.7), channel_id=1, source_target_pairs={{0,192},{32,224},{64,0},{96,32},{128,64},{160,96},{192,128},{224,1... | collective-permute-start | bytes 393224 | tf_op jit(solution)/shard_map/ppermute | solution.py:54
  15.6 3.7 %collective-permute-start.1 = (bf16[32,2048]{1,0:T(8,128)(2,1)S(1)}, bf16[32,2048]{1,0:T(8,128)(2,1)S(1)}, u32[]{:S(2)}, u32[]{:S(2)}) collective-permute-start(bf16[32,2048]{1,0:T(8,128)(2,1)S(1)} %pad_maximum_fusion.7), channel_id=1, source_target_pairs={{0,224},{32,0},{64,32},{96,64},{128,96},{160,128},{192,160},{224,1... | collective-permute-start | bytes 393224 | tf_op jit(solution)/shard_map/ppermute | solution.py:54
  21.5 4.6 %collective-permute-start.4 = (bf16[16,2048]{1,0:T(8,128)(2,1)S(1)}, bf16[16,2048]{1,0:T(8,128)(2,1)S(1)}, u32[]{:S(2)}, u32[]{:S(2)}) collective-permute-start(bf16[16,2048]{1,0:T(8,128)(2,1)S(1)} %slice.214), channel_id=1, source_target_pairs={{0,192},{32,224},{64,0},{96,32},{128,64},{160,96},{192,128},{224,1... | collective-permute-start | bytes 196616 | tf_op jit(solution)/shard_map/ppermute | solution.py:54
  26.2 3.4 %collective-permute-start.3 = (bf16[32,2048]{1,0:T(8,128)(2,1)S(1)}, bf16[32,2048]{1,0:T(8,128)(2,1)S(1)}, u32[]{:S(2)}, u32[]{:S(2)}) collective-permute-start(bf16[32,2048]{1,0:T(8,128)(2,1)S(1)} %collective-permute-done.2), channel_id=1, source_target_pairs={{0,224},{32,0},{64,32},{96,64},{128,96},{160,128},{192,160},{224,1... | collective-permute-start | bytes 393224 | tf_op jit(solution)/shard_map/ppermute | solution.py:54
  32.6 3.2 %collective-permute-done.7 = bf16[32,2048]{1,0:T(8,128)(2,1)S(1)} collective-permute-done((bf16[32,2048]{1,0:T(8,128)(2,1)S(1)}, bf16[32,2048]{1,0:T(8,128)(2,1)S(1)}, u32[]{:S(2)}, u32[]{:S(2)}) %collective-permute-start.7) | collective-permute-done | bytes 131104 | tf_op jit(solution)/shard_map/ppermute | solution.py:54
  36.0 4.6 %copy.6 = bf16[256,8,2,896]{3,1,2,0:T(8,128)(2,1)S(1)} copy(bf16[256,8,2,896]{3,2,1,0:T(2,128)(2,1)} %bitcast.13) | data formatting | bytes 14680064
  40.7 5.1 %multiply_convert_fusion = f16[512,1792]{1,0:T(8,128)(2,1)} fusion(bf16[512,2048]{1,0:T(8,128)(2,1)S(1)} %constant_dynamic-update-slice_fusion.10, bf16[2048,1792]{1,0:T(8,128)(2,1)S(1)} %bitcast.14), kind=kOutput, calls=%fused_computation.1 | convolution fusion | flops 3759931392 | bytes 11272192 | tf_op jit(solution)/shard_map/dot_general | solution.py:120
  45.9 3.0 %collective-permute-start.13 = (bf16[32,2048]{1,0:T(8,128)(2,1)S(1)}, bf16[32,2048]{1,0:T(8,128)(2,1)S(1)}, u32[]{:S(2)}, u32[]{:S(2)}) collective-permute-start(bf16[32,2048]{1,0:T(8,128)(2,1)S(1)} %pad_maximum_fusion.9), channel_id=1, source_target_pairs={{0,64},{32,96},{64,128},{96,160},{128,192},{160,224},{192,0},{224,... | collective-permute-start | bytes 393224 | tf_op jit(solution)/shard_map/ppermute | solution.py:54
  50.8 5.9 %all-to-all-start = ((f16[8,64,1792]{2,1,0:T(8,128)(2,1)}), f16[8,64,1792]{2,1,0:T(8,128)(2,1)S(1)}, u32[]{:S(2)}, u32[]{:S(2)}) async-start(f16[8,64,1792]{2,1,0:T(8,128)(2,1)} %bitcast.17), calls=%async_computation | async-start | bytes 3670016 | tf_op jit(solution)/shard_map/all_to_all | solution.py:102
  62.2 3.0 %collective-permute-done.12 = bf16[32,2048]{1,0:T(8,128)(2,1)S(1)} collective-permute-done((bf16[32,2048]{1,0:T(8,128)(2,1)S(1)}, bf16[32,2048]{1,0:T(8,128)(2,1)S(1)}, u32[]{:S(2)}, u32[]{:S(2)}) %collective-permute-start.12) | collective-permute-done | bytes 131104 | tf_op jit(solution)/shard_map/ppermute | solution.py:54
  79.6 27.1 %all_to_all.15 = bf16[8,128,896]{2,1,0:T(8,128)(2,1)S(1)} all-to-all(bf16[8,128,896]{2,1,0:T(8,128)(2,1)S(1)} %pad_maximum_fusion), channel_id=1, replica_groups=mesh['z'=8,'xh'=2,'core'=2,'xl'=2,'y'=4] {'xl','y'}, dimensions={0} | all-to-all | bytes 3670016 | tf_op jit(solution)/shard_map/all_to_all | solution.py:102
  109.6 3.3 %shard_map.60 = (f32[256,2048]{1,0:T(8,128)S(1)}, bf16[256,2048]{1,0:T(8,128)(2,1)S(1)}) custom-call(bf16[256,896]{1,0:T(8,128)(2,1)S(1)} %bitcast.12, bf16[256,896]{1,0:T(8,128)(2,1)S(1)} %bitcast.11, bf16[896,2048]{1,0:T(8,128)(2,1)S(1)} %copy-done.1), custom_call_target="tpu_custom_call" | custom-call | flops 512 | bytes 458752 | tf_op jit(solution)/shard_map/pallas_call | solution.py:35
  113.1 5.7 %all-to-all-start.2 = ((bf16[8,64,1792]{2,1,0:T(8,128)(2,1)}), bf16[8,64,1792]{2,1,0:T(8,128)(2,1)}, u32[]{:S(2)}, u32[]{:S(2)}) async-start(bf16[8,64,1792]{2,1,0:T(8,128)(2,1)} %broadcast_in_dim.5), calls=%async_computation.2 | async-start | bytes 3670016 | tf_op jit(solution)/shard_map/all_to_all | solution.py:102
  120.8 3.0 %collective-permute-start.20 = (bf16[64,2048]{1,0:T(8,128)(2,1)S(1)}, bf16[64,2048]{1,0:T(8,128)(2,1)S(1)}, u32[]{:S(2)}, u32[]{:S(2)}) collective-permute-start(bf16[64,2048]{1,0:T(8,128)(2,1)S(1)} %pad_maximum_fusion.3), channel_id=1, source_target_pairs={{0,224},{32,0},{64,32},{96,64},{128,96},{160,128},{192,160},{224,1... | collective-permute-start | bytes 786440 | tf_op jit(solution)/shard_map/ppermute | solution.py:54
  123.9 4.1 %collective-permute-start.23 = (bf16[16,2048]{1,0:T(8,128)(2,1)S(1)}, bf16[16,2048]{1,0:T(8,128)(2,1)S(1)}, u32[]{:S(2)}, u32[]{:S(2)}) collective-permute-start(bf16[16,2048]{1,0:T(8,128)(2,1)S(1)} %get-tuple-element.40), channel_id=1, source_target_pairs={{0,192},{32,224},{64,0},{96,32},{128,64},{160,96},{192,128},{224,1... | collective-permute-start | bytes 196616 | tf_op jit(solution)/shard_map/ppermute | solution.py:54
  128.0 4.2 %collective-permute-done.19 = bf16[64,2048]{1,0:T(8,128)(2,1)S(1)} collective-permute-done((bf16[64,2048]{1,0:T(8,128)(2,1)S(1)}, bf16[64,2048]{1,0:T(8,128)(2,1)S(1)}, u32[]{:S(2)}, u32[]{:S(2)}) %collective-permute-start.19) | collective-permute-done | bytes 262176 | tf_op jit(solution)/shard_map/ppermute | solution.py:54
  134.4 2.7 %collective-permute-start.24 = (bf16[32,2048]{1,0:T(8,128)(2,1)S(1)}, bf16[32,2048]{1,0:T(8,128)(2,1)S(1)}, u32[]{:S(2)}, u32[]{:S(2)}) collective-permute-start(bf16[32,2048]{1,0:T(8,128)(2,1)S(1)} %get-tuple-element.30), channel_id=1, source_target_pairs={{0,192},{32,224},{64,0},{96,32},{128,64},{160,96},{192,128},{224,1... | collective-permute-start | bytes 393224 | tf_op jit(solution)/shard_map/ppermute | solution.py:54
  137.1 4.8 %collective-permute-done.22 = bf16[32,2048]{1,0:T(8,128)(2,1)S(1)} collective-permute-done((bf16[32,2048]{1,0:T(8,128)(2,1)S(1)}, bf16[32,2048]{1,0:T(8,128)(2,1)S(1)}, u32[]{:S(2)}, u32[]{:S(2)}) %collective-permute-start.22) | collective-permute-done | bytes 131104 | tf_op jit(solution)/shard_map/ppermute | solution.py:54
  142.4 6.8 %fusion.21 = f32[512,2048]{1,0:T(8,128)S(1)} fusion(bf16[512,1792]{1,0:T(8,128)(2,1)} %bitcast.4, bf16[2048,1792]{1,0:T(8,128)(2,1)} %bitcast.15), kind=kOutput, calls=%fused_computation.84 | convolution fusion | flops 3758096384 | bytes 13369344 | tf_op jit(solution)/shard_map/dot_general | solution.py:147
  157.5 2.9 %collective-permute-start.30 = (bf16[16,2048]{1,0:T(8,128)(2,1)S(1)}, bf16[16,2048]{1,0:T(8,128)(2,1)S(1)}, u32[]{:S(2)}, u32[]{:S(2)}) collective-permute-start(bf16[16,2048]{1,0:T(8,128)(2,1)S(1)} %get-tuple-element.35), channel_id=1, source_target_pairs={{0,192},{32,224},{64,0},{96,32},{128,64},{160,96},{192,128},{224,1... | collective-permute-start | bytes 196616 | tf_op jit(solution)/shard_map/ppermute | solution.py:54
  160.4 2.7 %collective-permute-done.26 = bf16[64,2048]{1,0:T(8,128)(2,1)S(1)} collective-permute-done((bf16[64,2048]{1,0:T(8,128)(2,1)S(1)}, bf16[64,2048]{1,0:T(8,128)(2,1)S(1)}, u32[]{:S(2)}, u32[]{:S(2)}) %collective-permute-start.26) | collective-permute-done | bytes 262176 | tf_op jit(solution)/shard_map/ppermute | solution.py:54
  166.7 3.1 %collective-permute-start.29 = (bf16[32,2048]{1,0:T(8,128)(2,1)S(1)}, bf16[32,2048]{1,0:T(8,128)(2,1)S(1)}, u32[]{:S(2)}, u32[]{:S(2)}) collective-permute-start(bf16[32,2048]{1,0:T(8,128)(2,1)S(1)} %get-tuple-element.28), channel_id=1, source_target_pairs={{0,64},{32,96},{64,128},{96,160},{128,192},{160,224},{192,0},{224,... | collective-permute-start | bytes 393224 | tf_op jit(solution)/shard_map/ppermute | solution.py:54
  178.5 5.1 %collective-permute-done.32 = bf16[32,2048]{1,0:T(8,128)(2,1)S(1)} collective-permute-done((bf16[32,2048]{1,0:T(8,128)(2,1)S(1)}, bf16[32,2048]{1,0:T(8,128)(2,1)S(1)}, u32[]{:S(2)}, u32[]{:S(2)}) %collective-permute-start.32) | collective-permute-done | bytes 131104 | tf_op jit(solution)/shard_map/ppermute | solution.py:50
  (121 shorter events, 60.3 us)
Async XLA Ops:
  9.2 12.3 %collective-permute-start.2 = (bf16[32,2048]{1,0:T(8,128)(2,1)S(1)}, bf16[32,2048]{1,0:T(8,128)(2,1)S(1)}, u32[]{:S(2)}, u32[]{:S(2)}) collective-permute-start(bf16[32,2048]{1,0:T(8,128)(2,1)S(1)} %pad_maximum_fusion.7), channel_id=1, source_target_pairs={{0,192},{32,224},{64,0},{96,32},{128,64},{160,96},{192,128},{224,1... | collective-permute-start | bytes 393224 | tf_op jit(solution)/shard_map/ppermute | solution.py:54
  15.6 10.5 %collective-permute-start.5 = (bf16[32,2048]{1,0:T(8,128)(2,1)S(1)}, bf16[32,2048]{1,0:T(8,128)(2,1)S(1)}, u32[]{:S(2)}, u32[]{:S(2)}) collective-permute-start(bf16[32,2048]{1,0:T(8,128)(2,1)S(1)} %pad_maximum_fusion.7), channel_id=1, source_target_pairs={{0,64},{32,96},{64,128},{96,160},{128,192},{160,224},{192,0},{224,... | collective-permute-start | bytes 393224 | tf_op jit(solution)/shard_map/ppermute | solution.py:54
  15.6 14.0 %collective-permute-start.1 = (bf16[32,2048]{1,0:T(8,128)(2,1)S(1)}, bf16[32,2048]{1,0:T(8,128)(2,1)S(1)}, u32[]{:S(2)}, u32[]{:S(2)}) collective-permute-start(bf16[32,2048]{1,0:T(8,128)(2,1)S(1)} %pad_maximum_fusion.7), channel_id=1, source_target_pairs={{0,224},{32,0},{64,32},{96,64},{128,96},{160,128},{192,160},{224,1... | collective-permute-start | bytes 393224 | tf_op jit(solution)/shard_map/ppermute | solution.py:54
  19.3 16.6 %collective-permute-start.8 = (bf16[32,2048]{1,0:T(8,128)(2,1)S(1)}, bf16[32,2048]{1,0:T(8,128)(2,1)S(1)}, u32[]{:S(2)}, u32[]{:S(2)}) collective-permute-start(bf16[32,2048]{1,0:T(8,128)(2,1)S(1)} %pad_maximum_fusion.7), channel_id=1, source_target_pairs={{0,32},{32,64},{64,96},{96,128},{128,160},{160,192},{192,224},{224... | collective-permute-start | bytes 393224 | tf_op jit(solution)/shard_map/ppermute | solution.py:54
  21.5 10.6 %collective-permute-start.4 = (bf16[16,2048]{1,0:T(8,128)(2,1)S(1)}, bf16[16,2048]{1,0:T(8,128)(2,1)S(1)}, u32[]{:S(2)}, u32[]{:S(2)}) collective-permute-start(bf16[16,2048]{1,0:T(8,128)(2,1)S(1)} %slice.214), channel_id=1, source_target_pairs={{0,192},{32,224},{64,0},{96,32},{128,64},{160,96},{192,128},{224,1... | collective-permute-start | bytes 196616 | tf_op jit(solution)/shard_map/ppermute | solution.py:54
  45.8 16.3 %collective-permute-start.10 = (bf16[32,2048]{1,0:T(8,128)(2,1)S(1)}, bf16[32,2048]{1,0:T(8,128)(2,1)S(1)}, u32[]{:S(2)}, u32[]{:S(2)}) collective-permute-start(bf16[32,2048]{1,0:T(8,128)(2,1)S(1)} %pad_maximum_fusion.9), channel_id=1, source_target_pairs={{0,224},{32,0},{64,32},{96,64},{128,96},{160,128},{192,160},{224,1... | collective-permute-start | bytes 393224 | tf_op jit(solution)/shard_map/ppermute | solution.py:54
  45.9 13.6 %collective-permute-start.11 = (bf16[32,2048]{1,0:T(8,128)(2,1)S(1)}, bf16[32,2048]{1,0:T(8,128)(2,1)S(1)}, u32[]{:S(2)}, u32[]{:S(2)}) collective-permute-start(bf16[32,2048]{1,0:T(8,128)(2,1)S(1)} %pad_maximum_fusion.9), channel_id=1, source_target_pairs={{0,192},{32,224},{64,0},{96,32},{128,64},{160,96},{192,128},{224,1... | collective-permute-start | bytes 393224 | tf_op jit(solution)/shard_map/ppermute | solution.py:54
  45.9 11.0 %collective-permute-start.13 = (bf16[32,2048]{1,0:T(8,128)(2,1)S(1)}, bf16[32,2048]{1,0:T(8,128)(2,1)S(1)}, u32[]{:S(2)}, u32[]{:S(2)}) collective-permute-start(bf16[32,2048]{1,0:T(8,128)(2,1)S(1)} %pad_maximum_fusion.9), channel_id=1, source_target_pairs={{0,64},{32,96},{64,128},{96,160},{128,192},{160,224},{192,0},{224,... | collective-permute-start | bytes 393224 | tf_op jit(solution)/shard_map/ppermute | solution.py:54
  48.9 20.4 %collective-permute-start.16 = (bf16[32,2048]{1,0:T(8,128)(2,1)S(1)}, bf16[32,2048]{1,0:T(8,128)(2,1)S(1)}, u32[]{:S(2)}, u32[]{:S(2)}) collective-permute-start(bf16[32,2048]{1,0:T(8,128)(2,1)S(1)} %pad_maximum_fusion.9), channel_id=1, source_target_pairs={{0,32},{32,64},{64,96},{96,128},{128,160},{160,192},{192,224},{224... | collective-permute-start | bytes 393224 | tf_op jit(solution)/shard_map/ppermute | solution.py:54
  50.8 28.1 %all-to-all-start = ((f16[8,64,1792]{2,1,0:T(8,128)(2,1)}), f16[8,64,1792]{2,1,0:T(8,128)(2,1)S(1)}, u32[]{:S(2)}, u32[]{:S(2)}) async-start(f16[8,64,1792]{2,1,0:T(8,128)(2,1)} %bitcast.17), calls=%async_computation | async-start | bytes 3670016 | tf_op jit(solution)/shard_map/all_to_all | solution.py:102
  57.0 10.3 %collective-permute-start.14 = (bf16[32,2048]{1,0:T(8,128)(2,1)S(1)}, bf16[32,2048]{1,0:T(8,128)(2,1)S(1)}, u32[]{:S(2)}, u32[]{:S(2)}) collective-permute-start(bf16[32,2048]{1,0:T(8,128)(2,1)S(1)} %collective-permute-done.13), channel_id=1, source_target_pairs={{0,64},{32,96},{64,128},{96,160},{128,192},{160,224},{192,0},{224,... | collective-permute-start | bytes 393224 | tf_op jit(solution)/shard_map/ppermute | solution.py:54
  58.9 10.3 %collective-permute-start.15 = (bf16[32,2048]{1,0:T(8,128)(2,1)S(1)}, bf16[32,2048]{1,0:T(8,128)(2,1)S(1)}, u32[]{:S(2)}, u32[]{:S(2)}) collective-permute-start(bf16[32,2048]{1,0:T(8,128)(2,1)S(1)} %collective-permute-done.13), channel_id=1, source_target_pairs={{0,32},{32,64},{64,96},{96,128},{128,160},{160,192},{192,224},{224... | collective-permute-start | bytes 393224 | tf_op jit(solution)/shard_map/ppermute | solution.py:54
  113.1 29.4 %all-to-all-start.2 = ((bf16[8,64,1792]{2,1,0:T(8,128)(2,1)}), bf16[8,64,1792]{2,1,0:T(8,128)(2,1)}, u32[]{:S(2)}, u32[]{:S(2)}) async-start(bf16[8,64,1792]{2,1,0:T(8,128)(2,1)} %broadcast_in_dim.5), calls=%async_computation.2 | async-start | bytes 3670016 | tf_op jit(solution)/shard_map/all_to_all | solution.py:102
  120.4 11.8 %collective-permute-start.19 = (bf16[64,2048]{1,0:T(8,128)(2,1)S(1)}, bf16[64,2048]{1,0:T(8,128)(2,1)S(1)}, u32[]{:S(2)}, u32[]{:S(2)}) collective-permute-start(bf16[64,2048]{1,0:T(8,128)(2,1)S(1)} %pad_maximum_fusion.2), channel_id=1, source_target_pairs={{0,32},{32,64},{64,96},{96,128},{128,160},{160,192},{192,224},{224... | collective-permute-start | bytes 786440 | tf_op jit(solution)/shard_map/ppermute | solution.py:54
  120.8 11.5 %collective-permute-start.20 = (bf16[64,2048]{1,0:T(8,128)(2,1)S(1)}, bf16[64,2048]{1,0:T(8,128)(2,1)S(1)}, u32[]{:S(2)}, u32[]{:S(2)}) collective-permute-start(bf16[64,2048]{1,0:T(8,128)(2,1)S(1)} %pad_maximum_fusion.3), channel_id=1, source_target_pairs={{0,224},{32,0},{64,32},{96,64},{128,96},{160,128},{192,160},{224,1... | collective-permute-start | bytes 786440 | tf_op jit(solution)/shard_map/ppermute | solution.py:54
  123.8 8.5 %collective-permute-start.21 = (bf16[16,2048]{1,0:T(8,128)(2,1)S(1)}, bf16[16,2048]{1,0:T(8,128)(2,1)S(1)}, u32[]{:S(2)}, u32[]{:S(2)}) collective-permute-start(bf16[16,2048]{1,0:T(8,128)(2,1)S(1)} %get-tuple-element.41), channel_id=1, source_target_pairs={{0,64},{32,96},{64,128},{96,160},{128,192},{160,224},{192,0},{224,... | collective-permute-start | bytes 196616 | tf_op jit(solution)/shard_map/ppermute | solution.py:54
  123.9 8.4 %collective-permute-start.23 = (bf16[16,2048]{1,0:T(8,128)(2,1)S(1)}, bf16[16,2048]{1,0:T(8,128)(2,1)S(1)}, u32[]{:S(2)}, u32[]{:S(2)}) collective-permute-start(bf16[16,2048]{1,0:T(8,128)(2,1)S(1)} %get-tuple-element.40), channel_id=1, source_target_pairs={{0,192},{32,224},{64,0},{96,32},{128,64},{160,96},{192,128},{224,1... | collective-permute-start | bytes 196616 | tf_op jit(solution)/shard_map/ppermute | solution.py:54
  132.4 9.5 %collective-permute-start.22 = (bf16[32,2048]{1,0:T(8,128)(2,1)S(1)}, bf16[32,2048]{1,0:T(8,128)(2,1)S(1)}, u32[]{:S(2)}, u32[]{:S(2)}) collective-permute-start(bf16[32,2048]{1,0:T(8,128)(2,1)S(1)} %get-tuple-element.31), channel_id=1, source_target_pairs={{0,64},{32,96},{64,128},{96,160},{128,192},{160,224},{192,0},{224,... | collective-permute-start | bytes 393224 | tf_op jit(solution)/shard_map/ppermute | solution.py:54
  134.4 7.6 %collective-permute-start.24 = (bf16[32,2048]{1,0:T(8,128)(2,1)S(1)}, bf16[32,2048]{1,0:T(8,128)(2,1)S(1)}, u32[]{:S(2)}, u32[]{:S(2)}) collective-permute-start(bf16[32,2048]{1,0:T(8,128)(2,1)S(1)} %get-tuple-element.30), channel_id=1, source_target_pairs={{0,192},{32,224},{64,0},{96,32},{128,64},{160,96},{192,128},{224,1... | collective-permute-start | bytes 393224 | tf_op jit(solution)/shard_map/ppermute | solution.py:54
  152.6 10.5 %collective-permute-start.26 = (bf16[64,2048]{1,0:T(8,128)(2,1)S(1)}, bf16[64,2048]{1,0:T(8,128)(2,1)S(1)}, u32[]{:S(2)}, u32[]{:S(2)}) collective-permute-start(bf16[64,2048]{1,0:T(8,128)(2,1)S(1)} %pad_maximum_fusion.4), channel_id=1, source_target_pairs={{0,32},{32,64},{64,96},{96,128},{128,160},{160,192},{192,224},{224... | collective-permute-start | bytes 786440 | tf_op jit(solution)/shard_map/ppermute | solution.py:54
  154.6 9.5 %collective-permute-start.27 = (bf16[64,2048]{1,0:T(8,128)(2,1)S(1)}, bf16[64,2048]{1,0:T(8,128)(2,1)S(1)}, u32[]{:S(2)}, u32[]{:S(2)}) collective-permute-start(bf16[64,2048]{1,0:T(8,128)(2,1)S(1)} %pad_maximum_fusion.5), channel_id=1, source_target_pairs={{0,224},{32,0},{64,32},{96,64},{128,96},{160,128},{192,160},{224,1... | collective-permute-start | bytes 786440 | tf_op jit(solution)/shard_map/ppermute | solution.py:54
  156.2 10.5 %collective-permute-start.28 = (bf16[16,2048]{1,0:T(8,128)(2,1)S(1)}, bf16[16,2048]{1,0:T(8,128)(2,1)S(1)}, u32[]{:S(2)}, u32[]{:S(2)}) collective-permute-start(bf16[16,2048]{1,0:T(8,128)(2,1)S(1)} %get-tuple-element.34), channel_id=1, source_target_pairs={{0,64},{32,96},{64,128},{96,160},{128,192},{160,224},{192,0},{224,... | collective-permute-start | bytes 196616 | tf_op jit(solution)/shard_map/ppermute | solution.py:54
  157.5 9.1 %collective-permute-start.30 = (bf16[16,2048]{1,0:T(8,128)(2,1)S(1)}, bf16[16,2048]{1,0:T(8,128)(2,1)S(1)}, u32[]{:S(2)}, u32[]{:S(2)}) collective-permute-start(bf16[16,2048]{1,0:T(8,128)(2,1)S(1)} %get-tuple-element.35), channel_id=1, source_target_pairs={{0,192},{32,224},{64,0},{96,32},{128,64},{160,96},{192,128},{224,1... | collective-permute-start | bytes 196616 | tf_op jit(solution)/shard_map/ppermute | solution.py:54
  166.7 7.9 %collective-permute-start.29 = (bf16[32,2048]{1,0:T(8,128)(2,1)S(1)}, bf16[32,2048]{1,0:T(8,128)(2,1)S(1)}, u32[]{:S(2)}, u32[]{:S(2)}) collective-permute-start(bf16[32,2048]{1,0:T(8,128)(2,1)S(1)} %get-tuple-element.28), channel_id=1, source_target_pairs={{0,64},{32,96},{64,128},{96,160},{128,192},{160,224},{192,0},{224,... | collective-permute-start | bytes 393224 | tf_op jit(solution)/shard_map/ppermute | solution.py:54
  (16 other events, 87.5 us)
